TPU v7x, 768 devices: a whole 4x8x12 slice. The times are simulated.
768 devices in a mesh: gx: 12 (over z), gy: 64 (over y, x, core).
Axes of the slice: x: 4, y: 8, z: 12, core: 2. Of those that a mesh axis runs over, the one named last changes fastest.
Arguments:
- coarse_state: float32 [384, 5, 384, 128], P('gy', None, 'gx')
- fine_state: float32 [12, 2048, 5, 8, 128], P('gx', 'gy')
- fine_count: int32 [12, 64], P('gx'), may hold values from 10 to 32, as said below
- parent_owner: int32 [12, 2048], P('gx'), may hold values from 0 to 63, as said below
- parent_site: int32 [12, 2048], P('gx'), may hold values from 0 to 47, as said below
- fine_half: int32 [12, 2048], P('gx'), may hold values from 0 to 1
Outputs:
- coarse_out: float32 [384, 5, 384, 128], P('gy', None, 'gx')
- fine_out: float32 [12, 2048, 5, 8, 128], P('gx', 'gy')
Inputs may be any that keep to these rules, and one draw needn't show every extreme that they name: `fine_count`: slots at or above a device's count are empty. In every gx row one device holds 32 live patches and another 32 // 3. `parent_owner`: A parent lies in the same gx row as its fine patch. The live patches of one device name one owner at most 2 times, and some device names one owner exactly 2 times. `parent_site`: site = (t * 2 + e) * 4 + q: tile t of the owner's 6 tiles, patch column 2 e of its block, quadrant q = 2 qy + qz. Fine patches whose parents one device owns name distinct sites, so fine regions never touch one another or one another's outer neighbour cells.
All inputs are finite; a program needn't handle non-finite values.
Results may differ from a plain program's by a relative error of at most 0.0003.
Values sent between devices are 32-bit elements; how exact they have to be, the bound alone decides.
No kernel may reach another device: no remote copies, remote signals or barrier semaphores. Data moves between devices by JAX's collectives and lax.ppermute only.
A program may use at most 128 MiB of HBM per device.

v0:
```python
import jax
import jax.numpy as jnp
from jax import lax
from jax.sharding import PartitionSpec as P

SY = 8
SZ = 16


GAMMA = 1.4
STEP_RATIO = 0.1


def with_halo(x, sides, width):
    for axis, dim in sides:
        size, length = (lax.axis_size(axis), x.shape[dim])
        up = [(i, (i + 1) % size) for i in range(size)]
        down = [(j, i) for i, j in up]
        last = lax.slice_in_dim(x, length - width, length, axis=dim)
        leading = lax.slice_in_dim(x, 0, width, axis=dim)
        before = lax.ppermute(last, axis, up)
        after = lax.ppermute(leading, axis, down)
        x = jnp.concatenate([before, x, after], axis=dim)
    return x


def from_behind(value, axis, steps):
    count = lax.axis_size(axis)
    pairs = [(source, (source + steps) % count) for source in range(count)]
    return lax.ppermute(value, axis, pairs)


def euler_flux(states):
    density = states[..., 0, :, :]
    mom_x = states[..., 1, :, :]
    mom_y = states[..., 2, :, :]
    mom_z = states[..., 3, :, :]
    energy = states[..., 4, :, :]
    velocity = mom_x / density
    kinetic = 0.5 * (mom_x * mom_x + mom_y * mom_y + mom_z * mom_z) / density
    pressure = (GAMMA - 1.0) * (energy - kinetic)
    fluxes = jnp.stack(
        [
            mom_x,
            mom_x * velocity + pressure,
            mom_y * velocity,
            mom_z * velocity,
            (energy + pressure) * velocity,
        ],
        axis=-3,
    )
    signal = jnp.abs(velocity) + jnp.sqrt(GAMMA * pressure / density)
    return (fluxes, signal)


def limit_edges(center, left_edge, right_edge):
    edge_jump = right_edge - left_edge
    curvature = 6.0 * (center - 0.5 * (left_edge + right_edge))
    extremum = (right_edge - center) * (center - left_edge) <= 0.0
    new_left = jnp.where(
        edge_jump * curvature > edge_jump * edge_jump, 3.0 * center - 2.0 * right_edge, left_edge
    )
    new_right = jnp.where(
        -edge_jump * edge_jump > edge_jump * curvature, 3.0 * center - 2.0 * left_edge, right_edge
    )
    return (jnp.where(extremum, center, new_left), jnp.where(extremum, center, new_right))


def face_flux(padded):
    length = padded.shape[-2]
    interior = length - 6
    outer_left = padded[..., 0 : length - 3, :]
    near_left = padded[..., 1 : length - 2, :]
    near_right = padded[..., 2 : length - 1, :]
    outer_right = padded[..., 3:length, :]
    edge_values = 7.0 / 12.0 * (near_left + near_right) - 1.0 / 12.0 * (outer_left + outer_right)
    edge_values = jnp.minimum(
        jnp.maximum(edge_values, jnp.minimum(near_left, near_right)),
        jnp.maximum(near_left, near_right),
    )
    left_lim, right_lim = limit_edges(
        padded[..., 2 : interior + 4, :],
        edge_values[..., 0 : interior + 2, :],
        edge_values[..., 1 : interior + 3, :],
    )
    state_left = right_lim[..., 0 : interior + 1, :]
    state_right = left_lim[..., 1 : interior + 2, :]
    flux_left, signal_left = euler_flux(state_left)
    flux_right, signal_right = euler_flux(state_right)
    signal = jnp.maximum(signal_left, signal_right)[..., None, :, :]
    return 0.5 * (flux_left + flux_right) - 0.5 * signal * (state_right - state_left)


def sweep_cells(padded):
    fluxes = face_flux(padded)
    return (padded[..., 3:-3, :] - STEP_RATIO * (fluxes[..., 1:, :] - fluxes[..., :-1, :]), fluxes)


def expand_cross(values):
    leading = values.shape[:-1]
    grid = values.reshape(leading + (SY // 2, 1, SZ // 2, 1))
    grid = jnp.broadcast_to(grid, leading + (SY // 2, 2, SZ // 2, 2))
    return grid.reshape(leading + (SY * SZ,))


def fold_cross(values):
    leading = values.shape[:-1]
    summed = values.reshape(leading + (SY // 2, 2, SZ // 2, 2)).sum(axis=(-3, -1))
    return summed.reshape(leading + (SY // 2 * (SZ // 2),))


def ghost_cells(ghosts):
    cells = expand_cross(ghosts)
    left_side = jnp.stack([cells[:, :, 0], cells[:, :, 1], cells[:, :, 1]], axis=2)
    right_side = jnp.stack([cells[:, :, 2], cells[:, :, 2], cells[:, :, 3]], axis=2)
    return (left_side, right_side)


def fine_steps(fine, ghost_old, ghost_new):
    cells_x = fine.shape[2]
    left_side, right_side = ghost_cells(ghost_old)
    middle, flux_one = sweep_cells(jnp.concatenate([left_side, fine, right_side], axis=2))
    left_side, right_side = ghost_cells(0.5 * (ghost_old + ghost_new))
    final, flux_two = sweep_cells(jnp.concatenate([left_side, middle, right_side], axis=2))
    bound_one = fold_cross(jnp.stack([flux_one[:, :, 0], flux_one[:, :, cells_x]], axis=2))
    bound_two = fold_cross(jnp.stack([flux_two[:, :, 0], flux_two[:, :, cells_x]], axis=2))
    leading = final.shape[:2]
    restricted = final.reshape(leading + (cells_x // 2, 2, SY * SZ)).sum(axis=3)
    restricted = 0.125 * fold_cross(restricted)
    return (final, bound_one, bound_two, restricted)


def slot_positions(owners, active):
    slot_total = owners.shape[-1]
    slot_order = jnp.arange(slot_total, dtype=jnp.int32)
    earlier = slot_order[None, :] < slot_order[:, None]
    same_owner = owners[..., :, None] == owners[..., None, :]
    return jnp.sum((same_owner & active[..., None, :] & earlier).astype(jnp.int32), axis=-1)


def take_cells(field_data, tile_id, start, quadrant, extent):
    corner = (
        tile_id,
        jnp.zeros((), jnp.int32),
        start,
        quadrant // 2 * (SY // 2),
        quadrant % 2 * (SZ // 2),
    )
    return lax.dynamic_slice(
        field_data, corner, (1, field_data.shape[1], extent, SY // 2, SZ // 2)
    )[0]


def blocks_to_cells(blocks, tile_total, columns, fields, depth):
    grid = blocks.reshape(tile_total, columns, 2, 2, fields, depth, SY // 2, SZ // 2)
    grid = grid.transpose(0, 4, 1, 5, 2, 6, 3, 7)
    return grid.reshape(tile_total, fields, columns * depth, SY * SZ)


def body(coarse_state, fine_state, fine_count, parent_owner, parent_site, fine_half):
    tile_total, fields, cells_x, section = coarse_state.shape
    groups = lax.axis_size("gy")
    own_index = lax.axis_index("gy")
    slot_total = fine_state.shape[1]
    fine_cells = fine_state.shape[3]
    half_cells = fine_cells // 2
    quarter = SY // 2 * (SZ // 2)
    capacity = (slot_total - 2) // groups + 2
    items = groups * capacity
    pairs = cells_x // (2 * fine_cells)
    halfcols = cells_x // half_cells
    owners = parent_owner.reshape(groups, slot_total)
    site_ids = parent_site.reshape(groups, slot_total)
    halves = fine_half.reshape(groups, slot_total)
    active = jnp.arange(slot_total, dtype=jnp.int32)[None, :] < fine_count.reshape(groups, 1)
    positions = slot_positions(owners, active)
    padded = with_halo(coarse_state, (("gx", 2),), 3)
    swept, flux_all = sweep_cells(padded)
    rim_cells = from_behind(swept[:, :, cells_x - 2 :], "gx", 1)
    new_cells = jnp.concatenate([rim_cells, swept], axis=2)
    old_offset = 3
    flux_offset = 0
    picks = (
        (owners == own_index)[:, None, :]
        & active[:, None, :]
        & (positions[:, None, :] == jnp.arange(capacity, dtype=jnp.int32)[None, :, None])
    )
    pick_int = picks.astype(jnp.int32)
    valid = jnp.sum(pick_int, axis=2).reshape(items)
    item_site = jnp.sum(pick_int * site_ids[:, None, :], axis=2).reshape(items)
    item_half = jnp.sum(pick_int * halves[:, None, :], axis=2).reshape(items)
    item_tile = item_site // (pairs * 4)
    item_quad = item_site % 4
    item_start = 2 * (item_site // 4 % pairs) * fine_cells + item_half * half_cells
    old_view = padded.reshape(tile_total, fields, padded.shape[2], SY, SZ)
    new_view = new_cells.reshape(tile_total, fields, new_cells.shape[2], SY, SZ)

    def gather_ghosts(tile_id, start, quadrant):
        pieces = [
            take_cells(old_view, tile_id, start - 2 + old_offset, quadrant, 2),
            take_cells(old_view, tile_id, start + half_cells + old_offset, quadrant, 2),
            take_cells(new_view, tile_id, start, quadrant, 2),
            take_cells(new_view, tile_id, start + half_cells + 2, quadrant, 2),
        ]
        return jnp.concatenate(pieces, axis=1).reshape(fields, 8 * quarter)

    outgoing = jax.vmap(gather_ghosts)(item_tile, item_start, item_quad)
    weight = valid.astype(jnp.float32)[:, None, None]
    outgoing = (outgoing * weight).reshape(groups, capacity, fields, 8 * quarter)
    arrived = lax.all_to_all(outgoing, "gy", split_axis=0, concat_axis=0, tiled=True)
    own_owner = lax.dynamic_index_in_dim(owners, own_index, 0, keepdims=False)
    own_active = lax.dynamic_index_in_dim(active, own_index, 0, keepdims=False)
    own_position = lax.dynamic_index_in_dim(positions, own_index, 0, keepdims=False)
    lookup = own_owner * capacity + jnp.minimum(own_position, capacity - 1)
    ghosts = jnp.take(arrived.reshape(items, fields, 8, quarter), lookup, axis=0)
    fine_now = fine_state.reshape(slot_total, fields, fine_cells, section)
    final, bound_one, bound_two, restricted = fine_steps(
        fine_now, ghosts[:, :, 0:4], ghosts[:, :, 4:8]
    )
    fine_out = jnp.where(own_active[:, None, None, None], final, 0.0).reshape(fine_state.shape)
    restricted_flat = restricted.reshape(slot_total, fields, half_cells * quarter)
    face_part = (0.125 * (bound_one + bound_two)).reshape(slot_total, fields, 2 * quarter)
    returning = jnp.concatenate([restricted_flat, face_part], axis=2)
    returning = jnp.where(own_active[:, None, None], returning, 0.0)
    width_back = returning.shape[2]
    placing = (
        (own_owner * capacity + own_position)[None, :]
        == jnp.arange(items, dtype=jnp.int32)[:, None]
    ) & own_active[None, :]
    outbound = jnp.dot(
        placing.astype(jnp.float32),
        returning.reshape(slot_total, fields * width_back),
        precision=lax.Precision.HIGHEST,
    )
    came_back = lax.all_to_all(
        outbound.reshape(groups, capacity, fields, width_back),
        "gy",
        split_axis=0,
        concat_axis=0,
        tiled=True,
    )
    came_back = came_back.reshape(items, fields, width_back)
    restored = came_back[:, :, : half_cells * quarter]
    face_avg = came_back[:, :, half_cells * quarter :].reshape(items, fields, 2, quarter)
    flux_view = flux_all.reshape(tile_total, fields, flux_all.shape[2], SY, SZ)

    def face_values(tile_id, start, quadrant):
        left_face = take_cells(flux_view, tile_id, start + flux_offset, quadrant, 1)
        right_face = take_cells(flux_view, tile_id, start + half_cells + flux_offset, quadrant, 1)
        return (left_face.reshape(fields, quarter), right_face.reshape(fields, quarter))

    coarse_left, coarse_right = jax.vmap(face_values)(item_tile, item_start, item_quad)
    left_fix = STEP_RATIO * (coarse_left - face_avg[:, :, 0]) * weight
    right_fix = STEP_RATIO * (face_avg[:, :, 1] - coarse_right) * weight
    column = item_start // half_cells
    live_items = valid[None, :] > 0
    block_total = tile_total * halfcols * 4
    target = (item_tile * halfcols + column) * 4 + item_quad
    cover_hit = (
        (target[None, :] == jnp.arange(block_total, dtype=jnp.int32)[:, None]) & live_items
    ).astype(jnp.float32)
    restore_blocks = jnp.dot(
        cover_hit,
        restored.reshape(items, fields * half_cells * quarter),
        precision=lax.Precision.HIGHEST,
    )
    covered = jnp.sum(cover_hit, axis=1)
    left_total = tile_total * (halfcols + 1) * 4
    left_target = (item_tile * (halfcols + 1) + column) * 4 + item_quad
    left_hit = (
        (left_target[None, :] == jnp.arange(left_total, dtype=jnp.int32)[:, None]) & live_items
    ).astype(jnp.float32)
    left_blocks = jnp.dot(
        left_hit, left_fix.reshape(items, fields * quarter), precision=lax.Precision.HIGHEST
    )
    right_target = (item_tile * halfcols + column + 1) * 4 + item_quad
    right_hit = (
        (right_target[None, :] == jnp.arange(block_total, dtype=jnp.int32)[:, None]) & live_items
    ).astype(jnp.float32)
    right_blocks = jnp.dot(
        right_hit, right_fix.reshape(items, fields * quarter), precision=lax.Precision.HIGHEST
    )
    restore_cells = blocks_to_cells(restore_blocks, tile_total, halfcols, fields, half_cells)
    cover_blocks = jnp.broadcast_to(covered[:, None], (block_total, half_cells * quarter))
    cover_cells = blocks_to_cells(cover_blocks, tile_total, halfcols, 1, half_cells)
    left_planes = blocks_to_cells(left_blocks, tile_total, halfcols + 1, fields, 1)
    incoming = from_behind(left_planes[:, :, 0], "gx", -1)
    last_cells = left_planes[:, :, 1:]
    last_cells = last_cells.at[:, :, halfcols - 1].add(incoming)
    first_cells = blocks_to_cells(right_blocks, tile_total, halfcols, fields, 1)
    between = jnp.zeros((tile_total, fields, halfcols, half_cells - 2, section), jnp.float32)
    fixes = jnp.concatenate(
        [first_cells[:, :, :, None], between, last_cells[:, :, :, None]], axis=3
    )
    fixes = fixes.reshape(tile_total, fields, cells_x, section)
    coarse_out = jnp.where(cover_cells > 0.5, restore_cells, swept + fixes)
    return (coarse_out, fine_out)


def solution(mesh):
    placed = (
        P("gy", None, "gx", None),
        P("gx", "gy", None, None, None),
        P("gx", None),
        P("gx", None),
        P("gx", None),
        P("gx", None),
    )
    return jax.shard_map(
        body,
        mesh=mesh,
        in_specs=placed,
        out_specs=(P("gy", None, "gx", None), P("gx", "gy", None, None, None)),
        check_vma=False,
    )
```

profile of v0, /device:TPU:1, one launch (start us, length us, event | category | flops | bytes accessed | tf_op | source)
XLA Modules:
  0.0 314.1 jit_solution(1210600692105570237)
XLA Ops:
  1.6 4.8 %collective-permute-start = (f32[6,5,3,128]{3,2,1,0:T(4,128)S(1)}, f32[6,5,3,128]{3,2,1,0:T(4,128)S(1)}, u32[]{:S(2)}, u32[]{:S(2)}) collective-permute-start(f32[6,5,3,128]{3,2,1,0:T(4,128)S(1)} %get-tuple-element.87), channel_id=1, source_target_pairs={{0,64},{64,128},{128,192},{192,256},{256,320},{320,384},{384,448},... | collective-permute-start | bytes 138248 | tf_op jit(solution)/shard_map/ppermute | solution.py:21
  6.5 12.2 %collective-permute-start.1 = (f32[6,5,3,128]{3,2,1,0:T(4,128)S(1)}, f32[6,5,3,128]{3,2,1,0:T(4,128)S(1)}, u32[]{:S(2)}, u32[]{:S(2)}) collective-permute-start(f32[6,5,3,128]{3,2,1,0:T(4,128)S(1)} %get-tuple-element.88), channel_id=1, source_target_pairs={{64,0},{128,64},{192,128},{256,192},{320,256},{384,320},{448,384},... | collective-permute-start | bytes 138248 | tf_op jit(solution)/shard_map/ppermute | solution.py:22
  29.9 2.4 collective-permute-start.2
  32.5 9.3 %copy.307 = f32[6,5,38,128]{1,0,3,2:T(8,128)} copy(f32[6,5,38,128]{3,2,1,0:T(8,128)S(1)} %pad_maximum_fusion.15) | data formatting | bytes 1167360 | tf_op jit(solution)/shard_map/concatenate | solution.py:23
  41.8 18.8 %gather_fusion = f32[128,5,2,4,8]{1,0,4,3,2:T(8,128)} fusion(f32[6,5,38,8,16]{1,0,4,3,2:T(8,128)} %bitcast.145, s32[128]{0:T(128)S(1)} %get-tuple-element.95), kind=kCustom, calls=%fused_computation | custom fusion | bytes 330240 | tf_op jit(solution)/shard_map/vmap()/gather | solution.py:149
  60.6 22.6 %gather_fusion.1 = f32[128,5,2,4,8]{1,0,4,3,2:T(8,128)} fusion(f32[6,5,38,8,16]{1,0,4,3,2:T(8,128)} %bitcast.146, s32[128]{0:T(128)S(1)} %get-tuple-element.94), kind=kCustom, calls=%fused_computation.1 | custom fusion | bytes 330240 | tf_op jit(solution)/shard_map/vmap()/gather | solution.py:149
  83.3 8.7 %copy.310 = f32[6,5,34,128]{1,0,3,2:T(8,128)} copy(f32[6,5,34,128]{3,2,1,0:T(8,128)S(1)} %pad_maximum_fusion.16) | data formatting | bytes 1044480 | tf_op jit(solution)/shard_map/concatenate | solution.py:180
  92.0 15.5 %gather_fusion.2 = f32[128,5,2,4,8]{1,0,4,3,2:T(8,128)} fusion(f32[6,5,34,8,16]{1,0,4,3,2:T(8,128)} %bitcast.143, s32[128]{0:T(128)S(1)} %get-tuple-element.93), kind=kCustom, calls=%fused_computation.2 | custom fusion | bytes 330240 | tf_op jit(solution)/shard_map/vmap()/gather | solution.py:149
  107.4 19.0 %gather_fusion.3 = f32[128,5,2,4,8]{1,0,4,3,2:T(8,128)} fusion(f32[6,5,34,8,16]{1,0,4,3,2:T(8,128)} %bitcast.144, s32[128]{0:T(128)S(1)} %get-tuple-element.92), kind=kCustom, calls=%fused_computation.3 | custom fusion | bytes 330240 | tf_op jit(solution)/shard_map/vmap()/gather | solution.py:149
  126.4 11.7 %pad_maximum_fusion = f32[128,5,8,4,8]{1,0,4,3,2:T(8,128)} fusion(f32[128,5,2,4,8]{1,0,4,3,2:T(8,128)} %gather_fusion.3, f32[128,5,2,4,8]{1,0,4,3,2:T(8,128)} %gather_fusion.2, f32[128,5,2,4,8]{1,0,4,3,2:T(8,128)} %gather_fusion.1, f32[128,5,2,4,8]{1,0,4,3,2:T(8,128)} %gather_fusion), kind=kLoop, calls=%fused_computation.7 | loop fusion | flops 491520 | bytes 1310720 | tf_op jit(solution)/shard_map/vmap()/concatenate | solution.py:205
  138.0 18.5 %copy.369 = f32[64,2,5,256]{3,1,0,2:T(2,128)S(1)} copy(f32[64,2,5,256]{2,1,0,3:T(2,128)} %bitcast.149) | data formatting | bytes 1310720 | tf_op jit(solution)/shard_map/vmap()/reshape | solution.py:205
  158.0 12.0 %all-to-all-start = ((f32[64,2,5,256]{3,1,2,0:T(2,128)}), f32[64,2,5,256]{3,1,2,0:T(2,128)}, u32[]{:S(2)}, u32[]{:S(2)}) async-start(f32[64,2,5,256]{3,1,2,0:T(2,128)} %copy.313), calls=%async_computation | async-start | bytes 1310720 | tf_op jit(solution)/shard_map/all_to_all | solution.py:210
  171.7 18.2 %all-to-all-done = f32[64,2,5,256]{3,1,2,0:T(2,128)} async-done(((f32[64,2,5,256]{3,1,2,0:T(2,128)}), f32[64,2,5,256]{3,1,2,0:T(2,128)}, u32[]{:S(2)}, u32[]{:S(2)}) %all-to-all-start) | async-done | bytes 655392 | tf_op jit(solution)/shard_map/all_to_all | solution.py:210
  221.7 5.9 %all-to-all-start.1 = ((f32[64,2,5,192]{3,1,2,0:T(2,128)}), f32[64,2,5,192]{3,1,2,0:T(2,128)S(1)}, u32[]{:S(2)}, u32[]{:S(2)}) async-start(f32[64,2,5,192]{3,1,2,0:T(2,128)} %copy.347), calls=%async_computation.1 | async-start | bytes 1310720 | tf_op jit(solution)/shard_map/all_to_all | solution.py:235
  231.4 8.1 %copy.352 = f32[6,5,33,128]{1,2,0,3:T(8,128)} copy(f32[6,5,33,128]{3,2,1,0:T(8,128)S(1)} %fusion.24) | data formatting | bytes 1013760 | tf_op jit(solution)/shard_map/sub | solution.py:91
  239.5 7.5 %gather_fusion.6 = f32[128,5,4,8]{1,0,3,2:T(8,128)S(1)} fusion(f32[6,5,33,8,16]{1,2,0,4,3:T(8,128)} %bitcast.147, s32[128]{0:T(128)S(1)} %get-tuple-element.91), kind=kCustom, calls=%fused_computation.6 | custom fusion | bytes 166400 | tf_op jit(solution)/shard_map/vmap()/gather | solution.py:149
  247.6 10.9 %gather_fusion.5 = f32[128,5,4,8]{1,0,3,2:T(8,128)S(1)} fusion(f32[6,5,33,8,16]{1,2,0,4,3:T(8,128)} %bitcast.148, s32[128]{0:T(128)S(1)} %get-tuple-element.39), kind=kCustom, calls=%fused_computation.5 | custom fusion | bytes 166400 | tf_op jit(solution)/shard_map/vmap()/gather | solution.py:149
  265.4 4.8 %copy.357 = f32[6,5,9,1,2,4,2,8]{7,6,5,4,0,2,1,3:T(2,128)S(1)} copy(f32[6,5,9,1,2,4,2,8]{2,7,5,1,6,4,0,3:T(8,128)} %convolution_bitcast_fusion.1) | data formatting | bytes 276480 | tf_op jit(solution)/shard_map/transpose | solution.py:156
  270.3 3.3 %reshape.1031 = f32[6,5,9,128]{3,0,2,1:T(8,128)S(1)} reshape(f32[6,5,9,1,2,4,2,8]{7,6,5,4,0,2,1,3:T(2,128)S(1)} %copy.357) | data formatting | bytes 276480 | tf_op jit(solution)/shard_map/reshape | solution.py:157
  273.6 3.8 %collective-permute-start.3 = (f32[6,5,128]{2,0,1:T(8,128)S(1)}, f32[6,5,128]{2,0,1:T(8,128)S(1)}, u32[]{:S(2)}, u32[]{:S(2)}) collective-permute-start(f32[6,5,128]{2,0,1:T(8,128)S(1)} %slice_bitcast_fusion.1), channel_id=1, source_target_pairs={{0,704},{64,0},{128,64},{192,128},{256,192},{320,256},{384,320},{4... | collective-permute-start | bytes 46088 | tf_op jit(solution)/shard_map/ppermute | solution.py:30
  277.5 5.4 %convolution_bitcast_fusion = f32[6,5,8,4,2,4,2,8]{7,2,5,3,1,6,4,0:T(8,128)} fusion(f32[5,4,4,8,128,1,1,1]{4,3,2,1,0,7,6,5:T(8,128)S(1)} %bitcast.162, s32[6,8,2,2]{1,3,2,0:T(2,128)S(1)} %multiply_add_fusion.1, s32[128]{0:T(128)S(1)} %get-tuple-element.97, pred[128]{0:T(512)(128)(4,1)S(1)} %gt.49), kind=kOutput, calls=%fused_computation.8 | convolution fusion | flops 188792832 | bytes 820608 | tf_op jit(solution)/shard_map/dot_general | solution.py:262
  285.5 2.8 broadcast_in_dim_reshape.2
  288.3 12.6 %copy.350 = f32[6,5,8,4,2,4,2,8]{7,6,5,4,3,2,1,0:T(2,128)} copy(f32[6,5,8,4,2,4,2,8]{7,2,5,3,1,6,4,0:T(8,128)} %convolution_bitcast_fusion) | data formatting | bytes 983040 | tf_op jit(solution)/shard_map/transpose | solution.py:156
  300.8 11.5 %reshape.1026 = f32[6,5,32,128]{3,2,1,0:T(8,128)S(1)} reshape(f32[6,5,8,4,2,4,2,8]{7,6,5,4,3,2,1,0:T(2,128)} %copy.350) | data formatting | bytes 983040 | tf_op jit(solution)/shard_map/reshape | solution.py:157
  (180 shorter events, 62.1 us)
Async XLA Ops:
  1.6 23.9 %collective-permute-start = (f32[6,5,3,128]{3,2,1,0:T(4,128)S(1)}, f32[6,5,3,128]{3,2,1,0:T(4,128)S(1)}, u32[]{:S(2)}, u32[]{:S(2)}) collective-permute-start(f32[6,5,3,128]{3,2,1,0:T(4,128)S(1)} %get-tuple-element.87), channel_id=1, source_target_pairs={{0,64},{64,128},{128,192},{192,256},{256,320},{320,384},{384,448},... | collective-permute-start | bytes 138248 | tf_op jit(solution)/shard_map/ppermute | solution.py:21
  6.5 19.1 %collective-permute-start.1 = (f32[6,5,3,128]{3,2,1,0:T(4,128)S(1)}, f32[6,5,3,128]{3,2,1,0:T(4,128)S(1)}, u32[]{:S(2)}, u32[]{:S(2)}) collective-permute-start(f32[6,5,3,128]{3,2,1,0:T(4,128)S(1)} %get-tuple-element.88), channel_id=1, source_target_pairs={{64,0},{128,64},{192,128},{256,192},{320,256},{384,320},{448,384},... | collective-permute-start | bytes 138248 | tf_op jit(solution)/shard_map/ppermute | solution.py:22
  28.8 1.0 copy-start
  29.9 53.3 %collective-permute-start.2 = (f32[6,5,2,128]{3,2,1,0:T(2,128)S(1)}, f32[6,5,2,128]{3,2,1,0:T(2,128)S(1)}, u32[]{:S(2)}, u32[]{:S(2)}) collective-permute-start(f32[6,5,2,128]{3,2,1,0:T(2,128)S(1)} %slice.450), channel_id=1, source_target_pairs={{0,64},{64,128},{128,192},{192,256},{256,320},{320,384},{384,448},... | collective-permute-start | bytes 92168 | tf_op jit(solution)/shard_map/ppermute | solution.py:30
  156.6 13.6 %copy-start.1 = (f32[1,32,5,8,128]{4,3,2,1,0:T(8,128)S(1)}, f32[1,32,5,8,128]{4,3,2,1,0:T(8,128)}, u32[]{:S(2)}) copy-start(f32[1,32,5,8,128]{4,3,2,1,0:T(8,128)} %param.9) | copy-start | bytes 1966084
  158.0 31.9 %all-to-all-start = ((f32[64,2,5,256]{3,1,2,0:T(2,128)}), f32[64,2,5,256]{3,1,2,0:T(2,128)}, u32[]{:S(2)}, u32[]{:S(2)}) async-start(f32[64,2,5,256]{3,1,2,0:T(2,128)} %copy.313), calls=%async_computation | async-start | bytes 1310720 | tf_op jit(solution)/shard_map/all_to_all | solution.py:210
  206.7 1.1 copy-start.2
  215.9 2.4 copy-start.4
  221.7 39.9 %all-to-all-start.1 = ((f32[64,2,5,192]{3,1,2,0:T(2,128)}), f32[64,2,5,192]{3,1,2,0:T(2,128)S(1)}, u32[]{:S(2)}, u32[]{:S(2)}) async-start(f32[64,2,5,192]{3,1,2,0:T(2,128)} %copy.347), calls=%async_computation.1 | async-start | bytes 1310720 | tf_op jit(solution)/shard_map/all_to_all | solution.py:235
  258.6 3.9 %copy-start.5 = (f32[128]{0:T(128)S(1)}, f32[128]{0:T(128)}, u32[]{:S(2)}) copy-start(f32[128]{0:T(128)} %mul.895) | copy-start | bytes 1540
  259.2 3.9 %copy-start.6 = (s32[128]{0:T(128)S(1)}, s32[128]{0:T(128)}, u32[]{:S(2)}) copy-start(s32[128]{0:T(128)} %get-tuple-element.96) | copy-start | bytes 1540
  262.2 0.8 copy-start.3
  265.4 11.9 %slice-start = ((f32[128,5,192]{2,0,1:T(8,128)}), f32[128,5,128]{2,0,1:T(8,128)S(1)}, s32[]{:S(2)}) async-start(f32[128,5,192]{2,0,1:T(8,128)} %copy-done.3), calls=%async_computation.2 | async-start | bytes 655360 | tf_op jit(solution)/shard_map/slice | solution.py:243
  273.6 38.7 %collective-permute-start.3 = (f32[6,5,128]{2,0,1:T(8,128)S(1)}, f32[6,5,128]{2,0,1:T(8,128)S(1)}, u32[]{:S(2)}, u32[]{:S(2)}) collective-permute-start(f32[6,5,128]{2,0,1:T(8,128)S(1)} %slice_bitcast_fusion.1), channel_id=1, source_target_pairs={{0,704},{64,0},{128,64},{192,128},{256,192},{320,256},{384,320},{4... | collective-permute-start | bytes 46088 | tf_op jit(solution)/shard_map/ppermute | solution.py:30
  277.5 5.4 %copy-start.7 = (s32[128]{0:T(128)S(1)}, s32[128]{0:T(128)}, u32[]{:S(2)}) copy-start(s32[128]{0:T(128)} %get-tuple-element.35) | copy-start | bytes 1540
  300.8 11.6 %copy-start.8 = (f32[4]{0:T(128)S(1)}, f32[4]{0:T(128)}, u32[]{:S(2)}) copy-start(f32[4]{0:T(128)} %pad.3.clone) | copy-start | bytes 52
where the time goes:
time: 319 us; the launch traced here: 314 us
  local copies, waits for them, and re-layouts  211 us (66%)
  starting transfers between devices  41.1 us (13%)
  other arithmetic  32.3 us (10%)
  waiting for transfers between devices  18.2 us (6%)
  matrix products  9.25 us (3%)
    gather x8, local copies, waits for them, and re-layouts, take_cells(): lax.dynamic_slice(field_data, corner, (1, field_data.shape[1], extent, SY...  95.5 us
    transpose x4, local copies, waits for them, and re-layouts, blocks_to_cells(): grid = grid.transpose(0, 4, 1, 5, 2, 6, 3, 7)  19.4 us
    reshape x1, local copies, waits for them, and re-layouts, gather_ghosts(): return jnp.concatenate(pieces, axis=1).reshape(fields, 8 * quarter)  18.5 us
    all_to_all x1, waiting for transfers between devices, body(): lax.all_to_all(outgoing, 'gy', split_axis=0, concat_axis=0, tiled=True)  18.2 us
    reshape x2, local copies, waits for them, and re-layouts, blocks_to_cells(): return grid.reshape(tile_total, fields, columns * depth, SY * SZ)  14.7 us
    ppermute x1, starting transfers between devices, with_halo(): after = lax.ppermute(leading, axis, down)  12.2 us
    all_to_all x1, starting transfers between devices, body(): lax.all_to_all(outgoing, 'gy', split_axis=0, concat_axis=0, tiled=True)  12 us
    concatenate x1, other arithmetic, gather_ghosts(): return jnp.concatenate(pieces, axis=1).reshape(fields, 8 * quarter)  11.7 us
  transfers between devices with their start and end apart: 6, of which 1 were waited for; matrix products, arithmetic and copies ran while one was open for 41% of the time, Pallas kernels for 0%

commit v1 on v0

v1 whole, which is shorter than its diff:
```python
import functools

import jax
import jax.numpy as jnp
from jax import lax
from jax.experimental import pallas as pl
from jax.experimental.pallas import tpu as pltpu
from jax.sharding import PartitionSpec as P

SY = 8
SZ = 16
LANES = SY * SZ
FIELDS = 5
TILES = 6
CELLS = 32
FINE = 8
GAMMA = 1.4
STEP_RATIO = 0.1
GHOST_ROWS = 2 * FIELDS
BACK_ROWS = 8
STARTS = ((0, 0, 0), (0, 1, 4), (1, 0, 16), (1, 1, 20))
FACES = (0, 4, 8, 16, 20, 24)
VMEM = 48 * 1024 * 1024


def edge_value(outer_left, near_left, near_right, outer_right):
    value = 7.0 / 12.0 * (near_left + near_right) - 1.0 / 12.0 * (outer_left + outer_right)
    low = jnp.minimum(near_left, near_right)
    high = jnp.maximum(near_left, near_right)
    return jnp.minimum(jnp.maximum(value, low), high)


def limit_edges(center, left_edge, right_edge):
    jump = right_edge - left_edge
    product = jump * (6.0 * (center - 0.5 * (left_edge + right_edge)))
    square = jump * jump
    extremum = (right_edge - center) * (center - left_edge) <= 0.0
    new_left = jnp.where(product > square, 3.0 * center - 2.0 * right_edge, left_edge)
    new_right = jnp.where(-square > product, 3.0 * center - 2.0 * left_edge, right_edge)
    return (jnp.where(extremum, center, new_left), jnp.where(extremum, center, new_right))


def euler_flux(state):
    density, mom_x, mom_y, mom_z, energy = state
    inverse = 1.0 / density
    velocity = mom_x * inverse
    kinetic = 0.5 * (mom_x * mom_x + mom_y * mom_y + mom_z * mom_z) * inverse
    pressure = (GAMMA - 1.0) * (energy - kinetic)
    fluxes = (
        mom_x,
        mom_x * velocity + pressure,
        mom_y * velocity,
        mom_z * velocity,
        (energy + pressure) * velocity,
    )
    signal = jnp.abs(velocity) + jnp.sqrt(GAMMA * pressure * inverse)
    return (fluxes, signal)


def riemann(left, right):
    flux_left, signal_left = euler_flux(left)
    flux_right, signal_right = euler_flux(right)
    half_signal = 0.5 * jnp.maximum(signal_left, signal_right)
    return tuple(
        0.5 * (fl + fr) - half_signal * (r - l)
        for fl, fr, l, r in zip(flux_left, flux_right, left, right)
    )


def lane_index(rows):
    return lax.broadcasted_iota(jnp.int32, (rows, LANES), 1)


def pull_lanes(value, index):
    return jnp.take_along_axis(value, index, axis=1)


def coarse_kernel(
    codes, own, before, after, swept, sending, face_out, cells, fresh, fluxes, table
):
    stride = FIELDS * CELLS
    for f in range(FIELDS):
        for j in range(5):
            cells[j, f] = before[pl.ds(f * 8 + 3 + j, TILES, stride=FIELDS * 8), :]
        for j in range(3):
            cells[37 + j, f] = after[pl.ds(f * 8 + j, TILES, stride=FIELDS * 8), :]

    def load_cells(x, carry):
        for f in range(FIELDS):
            cells[x + 5, f] = own[pl.ds(f * CELLS + x, TILES, stride=stride), :]
        return carry

    lax.fori_loop(0, CELLS, load_cells, 0, unroll=4)

    def limited(j, edge_before):
        edges, lefts, rights = ([], [], [])
        for f in range(FIELDS):
            edge = edge_value(cells[j - 1, f], cells[j, f], cells[j + 1, f], cells[j + 2, f])
            left, right = limit_edges(cells[j, f], edge_before[f], edge)
            edges.append(edge)
            lefts.append(left)
            rights.append(right)
        return (tuple(edges), tuple(lefts), tuple(rights))

    def advance(j, carry):
        edges, rights, flux_before = carry
        edges, lefts, next_rights = limited(j, edges)
        flux = riemann(rights, lefts)
        for f in range(FIELDS):
            fluxes[j - 1, f] = flux[f]
        if flux_before is not None:
            for f in range(FIELDS):
                fresh[j - 1, f] = cells[j - 1, f] - STEP_RATIO * (flux[f] - flux_before[f])
        return (edges, next_rights, flux)

    edges = tuple(
        edge_value(cells[0, f], cells[1, f], cells[2, f], cells[3, f]) for f in range(FIELDS)
    )
    edges, _, rights = limited(2, edges)
    carry = advance(3, (edges, rights, None))
    carry = advance(4, carry)
    carry = advance(5, carry)

    def step(x, carry):
        carry = advance(x + 6, carry)
        for f in range(FIELDS):
            swept[pl.ds(f * CELLS + x, TILES, stride=stride), :] = fresh[x + 5, f]
        return carry

    lax.fori_loop(0, CELLS, step, carry, unroll=4)
    for i, face in enumerate(FACES):
        for f in range(FIELDS):
            face_out[i, f] = fluxes[face + 4, f]

    lane = lane_index(TILES)
    upper_z = (lane & 8) != 0
    upper_y = (lane & 64) != 0

    def swap(low, high, upper, shift):
        return (
            jnp.where(upper, pltpu.roll(high, shift, 1), low),
            jnp.where(upper, high, pltpu.roll(low, LANES - shift, 1)),
        )

    for e, h, start in STARTS:
        for age, source in enumerate((cells, fresh)):
            for f in range(FIELDS):
                c0, c1, c2, c3 = [source[start + 5 + o, f] for o in (-2, -1, 4, 5)]
                c0, c1 = swap(c0, c1, upper_z, 8)
                c2, c3 = swap(c2, c3, upper_z, 8)
                c0, c2 = swap(c0, c2, upper_y, 64)
                c1, c3 = swap(c1, c3, upper_y, 64)
                for q, value in enumerate((c0, c1, c2, c3)):
                    row = (e * 8 + q * 2 + h) * GHOST_ROWS + age * FIELDS + f
                    table[pl.ds(row, TILES, stride=16 * GHOST_ROWS), :] = value

    def send(k, carry):
        for c in range(2):
            code = codes[2 * k + c]

            @pl.when(code >= 0)
            def _():
                base = code * GHOST_ROWS
                sending[k, 3 * c] = table[pl.ds(base, 4), :]
                sending[k, 3 * c + 1] = table[pl.ds(base + 4, 4), :]
                sending[k, 2, 2 * c : 2 * c + 2] = table[pl.ds(base + 8, 2), :]

        return carry

    lax.fori_loop(0, sending.shape[0], send, 0, unroll=2)


def fine_kernel(lookups, count, arrived, fine, fine_out, back, ghosts, cells, packed):
    slots = lookups.shape[0]
    stride = FIELDS * FINE
    live = count[0]

    def fetch(s, carry):
        look = lookups[s]
        owner = lax.shift_right_logical(look, 1)
        pos = look & 1
        ghosts[pl.ds(s, 4, stride=slots), :] = arrived[owner, 3 * pos]
        ghosts[pl.ds(s + 4 * slots, 4, stride=slots), :] = arrived[owner, 3 * pos + 1]
        ghosts[pl.ds(s + 8 * slots, 2, stride=slots), :] = arrived[owner, 2, pl.ds(2 * pos, 2)]
        return carry

    lax.fori_loop(0, slots, fetch, 0, unroll=4)

    lane = lane_index(8)
    fine_y = lax.shift_right_logical(lane, 4)
    fine_z = lane & 15
    spread = lax.shift_right_logical(fine_y, 1) * 16 + lax.shift_right_logical(fine_z, 1)
    even_z = (lane & 1) == 0
    even_y = (lane & 16) == 0
    gather_back = (
        (2 * (fine_y & 3) + lax.shift_right_logical(lane, 6)) * 16
        + 2 * (lane & 7)
        + (lax.shift_right_logical(lane, 3) & 1)
    )

    def pair(first, second, even, shift):
        return jnp.where(even, first, pltpu.roll(second, shift, 1)) + jnp.where(
            even, pltpu.roll(first, LANES - shift, 1), second
        )

    def fold_four(a, b, c, d):
        low = pair(a, b, even_z, 1)
        high = pair(c, d, even_z, 1)
        return pull_lanes(0.125 * pair(low, high, even_y, 16), gather_back)

    def put_ghosts(slot, rows):
        for f in range(FIELDS):
            first, second, third, fourth = [
                pull_lanes(rows[f], spread + (t // 2) * 64 + (t % 2) * 8) for t in range(4)
            ]
            cells[slot, 0, f] = first
            cells[slot, 1, f] = second
            cells[slot, 2, f] = second
            cells[slot, 11, f] = third
            cells[slot, 12, f] = third
            cells[slot, 13, f] = fourth

    def sweep(slot, keep):
        edges = None
        rights = None
        before = None
        bounds = []
        for j in range(1, 12):
            new_edges = [
                edge_value(
                    cells[slot, j - 1, f],
                    cells[slot, j, f],
                    cells[slot, j + 1, f],
                    cells[slot, j + 2, f],
                )
                for f in range(FIELDS)
            ]
            if edges is not None:
                pairs = [
                    limit_edges(cells[slot, j, f], edges[f], new_edges[f]) for f in range(FIELDS)
                ]
                if rights is not None:
                    flux = riemann(rights, [p[0] for p in pairs])
                    if before is None:
                        bounds.append(flux)
                    else:
                        for f in range(FIELDS):
                            keep(
                                j - 4,
                                f,
                                cells[slot, j - 1, f] - STEP_RATIO * (flux[f] - before[f]),
                            )
                    before = flux
                rights = [p[1] for p in pairs]
            edges = new_edges
        bounds.append(before)
        return bounds

    def group(g, carry):
        base = g * (8 * stride)
        old = [ghosts[pl.ds(pl.multiple_of(f * slots + g * 8, 8), 8), :] for f in range(FIELDS)]
        new = [
            ghosts[pl.ds(pl.multiple_of((FIELDS + f) * slots + g * 8, 8), 8), :]
            for f in range(FIELDS)
        ]
        put_ghosts(0, old)
        put_ghosts(1, [0.5 * (o + n) for o, n in zip(old, new)])
        for x in range(FINE):
            for f in range(FIELDS):
                cells[0, x + 3, f] = fine[pl.ds(base + f * FINE + x, 8, stride=stride), :]

        def keep_middle(x, f, value):
            cells[1, x + 3, f] = value

        active = (lax.broadcasted_iota(jnp.int32, (8, LANES), 0) + g * 8) < live
        final = {}

        def keep_final(x, f, value):
            final[x, f] = value
            fine_out[pl.ds(base + f * FINE + x, 8, stride=stride), :] = jnp.where(
                active, value, 0.0
            )

        first = sweep(0, keep_middle)
        second = sweep(1, keep_final)
        rows = []
        for f in range(FIELDS):
            rows.append(fold_four(*[final[2 * t, f] + final[2 * t + 1, f] for t in range(4)]))
        faces = [first[side][f] + second[side][f] for side in range(2) for f in range(FIELDS)]
        faces += [faces[-1], faces[-1]]
        for t in range(3):
            rows.append(fold_four(*faces[4 * t : 4 * t + 4]))
        for r, value in enumerate(rows):
            packed[pl.ds(g * 64 + r, 8, stride=BACK_ROWS), :] = value
        return carry

    lax.fori_loop(0, slots // 8, group, 0)

    def put(s, carry):
        @pl.when(s < live)
        def _():
            target = pl.multiple_of(lookups[s] * BACK_ROWS, BACK_ROWS)
            source = pl.multiple_of(s * BACK_ROWS, BACK_ROWS)
            back[pl.ds(target, BACK_ROWS), :] = packed[pl.ds(source, BACK_ROWS), :]

        return carry

    lax.fori_loop(0, slots, put, 0, unroll=4)


def merge_kernel(codes, came, swept, face_in, out, left_out, field, cover):
    stride = FIELDS * CELLS
    for i in range(TILES * 2):
        cover[8 * i : 8 * i + 8, :] = jnp.zeros((8, LANES), jnp.float32)
    lane = lane_index(8)
    quads = lane & 72

    def scatter(i, carry):
        code = codes[i]

        @pl.when(code >= 0)
        def _():
            quad = lax.shift_right_logical(code, 1) & 3
            offset = lax.shift_right_logical(quad, 1) * 64 + (quad & 1) * 8
            line = lax.shift_right_logical(code, 3) * 8 + (code & 1) * 4
            value = came[pl.ds(pl.multiple_of(i * BACK_ROWS, BACK_ROWS), BACK_ROWS), :]
            inside = quads == offset
            for t in range(4):
                shift = (offset + LANES - ((t // 2) * 64 + (t % 2) * 8)) & (LANES - 1)
                moved = pltpu.roll(value, shift, 1)
                rows = pl.ds(pl.multiple_of((line + t) * 8, 8), 8)
                field[rows, :] = jnp.where(inside, moved, field[rows, :])
            rows = pl.ds(line, 4)
            cover[rows, :] = jnp.where(inside[:4], 1.0, cover[rows, :])

        return carry

    lax.fori_loop(0, codes.shape[0], scatter, 0, unroll=2)

    for t in range(TILES):
        for e in range(2):
            hit = cover[pl.ds(t * 16 + e * 8, 8), :] > 0.5
            for f in range(FIELDS):
                row = t * stride + f * CELLS + e * 16
                value = field[pl.ds((t * 16 + e * 8) * 8 + f, 8, stride=8), :]
                out[row : row + 8, :] = jnp.where(hit, value, swept[row : row + 8, :])
                out[row + 8 : row + 16, :] = swept[row + 8 : row + 16, :]

    for e, h, start in STARTS:
        line = e * 8 + h * 4
        hit = cover[pl.ds(line, TILES, stride=16), :] > 0.5
        for side in range(2):
            for f in range(FIELDS):
                item = side * FIELDS + f
                face = field[
                    pl.ds((line + item % 4) * 8 + FIELDS + item // 4, TILES, stride=128), :
                ]
                coarse = face_in[FACES.index(start + 4 * side), f]
                fix = STEP_RATIO * ((face - coarse) if side else (coarse - face))
                fix = jnp.where(hit, fix, 0.0)
                cell = start + 4 if side else start - 1
                if cell < 0:
                    left_out[f] = fix
                else:
                    rows = pl.ds(f * CELLS + cell, TILES, stride=stride)
                    out[rows, :] = out[rows, :] + fix


def last_kernel(incoming, block, out):
    out[...] = block[...]
    for f in range(FIELDS):
        for t in range(TILES):
            out[t, f, 7:8, :] = block[t, f, 7:8, :] + incoming[f, t : t + 1, :]


def in_vmem():
    return pl.BlockSpec(memory_space=pltpu.VMEM)


def in_smem():
    return pl.BlockSpec(memory_space=pltpu.SMEM)


def shaped(*dims):
    return jax.ShapeDtypeStruct(dims, jnp.float32)


def body(coarse_state, fine_state, fine_count, parent_owner, parent_site, fine_half):
    groups = lax.axis_size("gy")
    rows_x = lax.axis_size("gx")
    me = lax.axis_index("gy")
    slots = fine_state.shape[1]
    params = pltpu.CompilerParams(vmem_limit_bytes=VMEM)

    up = [(i, (i + 1) % rows_x) for i in range(rows_x)]
    down = [(j, i) for i, j in up]
    before = lax.ppermute(coarse_state[:, :, CELLS - 8 :], "gx", up)
    after = lax.ppermute(coarse_state[:, :, :8], "gx", down)

    order = jnp.arange(slots, dtype=jnp.int32)
    joined = parent_owner * LANES + parent_site * 2 + fine_half
    joined = joined.reshape(groups, slots)
    active = order[None, :] < fine_count.reshape(groups, 1)
    hit = (lax.shift_right_logical(joined, 7) == me) & active
    key = order[None, :] * LANES + (joined & (LANES - 1))
    big = slots * LANES
    low = jnp.min(jnp.where(hit, key, big), axis=1)
    high = jnp.max(jnp.where(hit, key, -1), axis=1)
    codes = jnp.stack(
        [
            jnp.where(low < big, low & (LANES - 1), -1),
            jnp.where(high > low, high & (LANES - 1), -1),
        ],
        axis=1,
    ).reshape(2 * groups)
    mine = lax.dynamic_index_in_dim(parent_owner.reshape(groups, slots), me, 0, keepdims=False)
    live = lax.dynamic_slice_in_dim(fine_count.reshape(groups), me, 1, 0)
    twin = (mine[:, None] == mine[None, :]) & (order[None, :] < order[:, None])
    lookups = 2 * mine + jnp.any(twin, axis=1).astype(jnp.int32)

    swept, sending, faces = pl.pallas_call(
        coarse_kernel,
        out_shape=(
            shaped(TILES * FIELDS * CELLS, LANES),
            shaped(groups, 5, 4, LANES),
            shaped(len(FACES), FIELDS, TILES, LANES),
        ),
        in_specs=[in_smem(), in_vmem(), in_vmem(), in_vmem()],
        out_specs=(in_vmem(), in_vmem(), in_vmem()),
        scratch_shapes=[
            pltpu.VMEM((40, FIELDS, TILES, LANES), jnp.float32),
            pltpu.VMEM((40, FIELDS, TILES, LANES), jnp.float32),
            pltpu.VMEM((40, FIELDS, TILES, LANES), jnp.float32),
            pltpu.VMEM((TILES * 16 * GHOST_ROWS, LANES), jnp.float32),
        ],
        compiler_params=params,
        name="coarse",
    )(
        codes,
        coarse_state.reshape(-1, LANES),
        before.reshape(-1, LANES),
        after.reshape(-1, LANES),
    )
    arrived = lax.all_to_all(sending, "gy", split_axis=0, concat_axis=0, tiled=True)

    fine_out, back = pl.pallas_call(
        fine_kernel,
        out_shape=(
            shaped(slots * FIELDS * FINE, LANES),
            shaped(groups * 2 * BACK_ROWS, LANES),
        ),
        in_specs=[in_smem(), in_smem(), in_vmem(), in_vmem()],
        out_specs=(in_vmem(), in_vmem()),
        scratch_shapes=[
            pltpu.VMEM((GHOST_ROWS * slots, LANES), jnp.float32),
            pltpu.VMEM((2, FINE + 6, FIELDS, 8, LANES), jnp.float32),
            pltpu.VMEM((slots * BACK_ROWS, LANES), jnp.float32),
        ],
        compiler_params=params,
        name="fine",
    )(lookups, live, arrived, fine_state.reshape(-1, LANES))
    came = lax.all_to_all(
        back.reshape(groups, 2 * BACK_ROWS, LANES), "gy", split_axis=0, concat_axis=0, tiled=True
    )

    merged, left_fix = pl.pallas_call(
        merge_kernel,
        out_shape=(
            shaped(TILES * FIELDS * CELLS, LANES),
            shaped(FIELDS, TILES, LANES),
        ),
        in_specs=[in_smem(), in_vmem(), in_vmem(), in_vmem()],
        out_specs=(in_vmem(), in_vmem()),
        scratch_shapes=[
            pltpu.VMEM((TILES * 16 * 8, LANES), jnp.float32),
            pltpu.VMEM((TILES * 16, LANES), jnp.float32),
        ],
        compiler_params=params,
        name="merge",
    )(codes, came.reshape(-1, LANES), swept, faces)
    incoming = lax.ppermute(left_fix, "gx", down)
    spec = pl.BlockSpec((TILES, FIELDS, 8, LANES), lambda i: (0, 0, 3, 0))
    coarse_out = pl.pallas_call(
        last_kernel,
        grid=(1,),
        out_shape=shaped(TILES, FIELDS, CELLS, LANES),
        in_specs=[pl.BlockSpec((FIELDS, TILES, LANES), lambda i: (0, 0, 0)), spec],
        out_specs=spec,
        input_output_aliases={1: 0},
        compiler_params=params,
        name="last",
    )(incoming, merged.reshape(TILES, FIELDS, CELLS, LANES))
    return (coarse_out, fine_out.reshape(fine_state.shape))


def solution(mesh):
    placed = (
        P("gy", None, "gx", None),
        P("gx", "gy", None, None, None),
        P("gx", None),
        P("gx", None),
        P("gx", None),
        P("gx", None),
    )
    return jax.shard_map(
        body,
        mesh=mesh,
        in_specs=placed,
        out_specs=(P("gy", None, "gx", None), P("gx", "gy", None, None, None)),
        check_vma=False,
    )
```

time: 319 us -> 104 us (0.33); the launches traced: 314 us -> 103 us
  local copies, waits for them, and re-layouts: 211 us -> 3.35 us
  other arithmetic: 32.3 us -> 1.85 us
  blocking collectives: 0 us -> 23.4 us
  Pallas kernels: 0 us -> 19.1 us
  starting transfers between devices: 41.1 us -> 31.3 us
  matrix products: 9.25 us -> 0 us
  waiting for transfers between devices: 18.2 us -> 23.6 us
    gather x9 -> x0, local copies, waits for them, and re-layouts: 97.9 us -> none  [the longest x8 95.5 us: take_cells(): lax.dynamic_slice(field_data, corner, (1, field_data.shape[1], extent, SY...]
    reshape x10 -> x2, local copies, waits for them, and re-layouts: 37.5 us -> 0.21 us  [the longest x1 0.14 us: body(): codes = jnp.stack([jnp.where(low < big, low & LANES - 1, -1), jnp.where(h...]
    all_to_all x0 -> x1, blocking collectives: none -> 23.4 us  [body(): lax.all_to_all(back.reshape(groups, 2 * BACK_ROWS, LANES), 'gy', split_ax...]
    transpose x4 -> x0, local copies, waits for them, and re-layouts: 19.4 us -> none  [blocks_to_cells(): grid = grid.transpose(0, 4, 1, 5, 2, 6, 3, 7)]
    pallas_call x0 -> x4, Pallas kernels: none -> 19.1 us  [the longest x1 6.95 us: body(): pl.pallas_call(coarse_kernel, out_shape=(shaped(TILES * FIELDS * CELLS, L...]
    concatenate x4 -> x0, local copies, waits for them, and re-layouts: 18.7 us -> none  [the longest x1 9.29 us: with_halo(): x = jnp.concatenate([before, x, after], axis=dim)]
    concatenate x7 -> x0, other arithmetic: 13.2 us -> none  [the longest x1 11.7 us: gather_ghosts(): return jnp.concatenate(pieces, axis=1).reshape(fields, 8 * quarter)]
    slice x23 -> x1, local copies, waits for them, and re-layouts: 14.1 us -> 1.04 us  [body(): after = lax.ppermute(coarse_state[:, :, :8], 'gx', down)]
  transfers between devices with their start and end apart: 6 -> 4, of which waited for: 1 -> 3; matrix products, arithmetic and copies ran while one was open for 41% -> 3% of each run, Pallas kernels for 0% -> 0%
where the time goes in v1:
time: 104 us; the launch traced here: 103 us
  starting transfers between devices  31.3 us (30%)
  waiting for transfers between devices  23.6 us (23%)
  blocking collectives  23.4 us (22%)
  Pallas kernels  19.1 us (18%)
  local copies, waits for them, and re-layouts  3.35 us (3%)
  other arithmetic  1.85 us (2%)
    all_to_all x1, blocking collectives, body(): lax.all_to_all(back.reshape(groups, 2 * BACK_ROWS, LANES), 'gy', split_ax...  23.4 us
    all_to_all x1, waiting for transfers between devices, body(): lax.all_to_all(sending, 'gy', split_axis=0, concat_axis=0, tiled=True)  18.2 us
    ppermute x1, starting transfers between devices, body(): after = lax.ppermute(coarse_state[:, :, :8], 'gx', down)  15.1 us
    all_to_all x1, starting transfers between devices, body(): lax.all_to_all(sending, 'gy', split_axis=0, concat_axis=0, tiled=True)  12.4 us
    pallas_call x1, Pallas kernels, body(): pl.pallas_call(coarse_kernel, out_shape=(shaped(TILES * FIELDS * CELLS, L...  6.95 us
    pallas_call x1, Pallas kernels, body(): pl.pallas_call(fine_kernel, out_shape=(shaped(slots * FIELDS * FINE, LANE...  6.06 us
    pallas_call x1, Pallas kernels, body(): pl.pallas_call(merge_kernel, out_shape=(shaped(TILES * FIELDS * CELLS, LA...  4.47 us
    ppermute x1, waiting for transfers between devices, body(): before = lax.ppermute(coarse_state[:, :, CELLS - 8:], 'gx', up)  2.81 us
  transfers between devices with their start and end apart: 4, of which 3 were waited for; matrix products, arithmetic and copies ran while one was open for 3% of the time, Pallas kernels for 0%

profile of v1, /device:TPU:1, one launch (start us, length us, event | category | flops | bytes accessed | tf_op | source)
XLA Modules:
  0.0 103.3 jit_solution(11135794761731449792)
XLA Ops:
  0.6 1.0 %fusion.5 = (f32[6,5,8,128]{3,2,1,0:T(8,128)S(1)}, f32[6,5,8,128]{3,2,1,0:T(8,128)S(1)}) fusion(f32[6,5,32,128]{3,2,1,0:T(8,128)} %param.6), kind=kLoop, calls=%fused_computation.19 | loop fusion | bytes 491520 | tf_op jit(solution)/shard_map/slice | solution.py:398
  1.7 15.1 %collective-permute-start.1 = (f32[6,5,8,128]{3,2,1,0:T(8,128)S(1)}, f32[6,5,8,128]{3,2,1,0:T(8,128)S(1)}, u32[]{:S(2)}, u32[]{:S(2)}) collective-permute-start(f32[6,5,8,128]{3,2,1,0:T(8,128)S(1)} %get-tuple-element.20), channel_id=1, source_target_pairs={{64,0},{128,64},{192,128},{256,192},{320,256},{384,320},{448,384},... | collective-permute-start | bytes 368648 | tf_op jit(solution)/shard_map/ppermute | solution.py:398
  16.8 1.9 %collective-permute-start = (f32[6,5,8,128]{3,2,1,0:T(8,128)S(1)}, f32[6,5,8,128]{3,2,1,0:T(8,128)S(1)}, u32[]{:S(2)}, u32[]{:S(2)}) collective-permute-start(f32[6,5,8,128]{3,2,1,0:T(8,128)S(1)} %get-tuple-element.21), channel_id=1, source_target_pairs={{0,64},{64,128},{128,192},{192,256},{256,320},{320,384},{384,448},... | collective-permute-start | bytes 368648 | tf_op jit(solution)/shard_map/ppermute | solution.py:397
  18.8 0.8 compare_reduce_fusion
  19.6 0.1 eq.32
  19.7 0.1 and.57
  19.7 0.7 copy-done.3
  20.4 0.2 select_reduce_fusion.1
  20.6 0.1 copy.11
  20.7 0.1 reshape.117.codes
  20.9 2.8 %collective-permute-done = f32[6,5,8,128]{3,2,1,0:T(8,128)S(1)} collective-permute-done((f32[6,5,8,128]{3,2,1,0:T(8,128)S(1)}, f32[6,5,8,128]{3,2,1,0:T(8,128)S(1)}, u32[]{:S(2)}, u32[]{:S(2)}) %collective-permute-start) | collective-permute-done | bytes 122912 | tf_op jit(solution)/shard_map/ppermute | solution.py:397
  23.7 7.0 %coarse.1 = (f32[960,128]{1,0:T(8,128)S(1)}, f32[64,5,4,128]{3,2,1,0:T(4,128)}, f32[6,5,6,128]{3,2,1,0:T(8,128)S(1)}) custom-call(s32[128]{0:T(128)S(1)} %reshape.117.codes, f32[960,128]{1,0:T(8,128)S(1)} %bitcast.19, f32[240,128]{1,0:T(8,128)S(1)} %bitcast.23, f32[240,128]{1,0:T(8,128)S(1)} %bitcast.22), custom_call_target="tpu_custom_call" | custom-call | tf_op jit(solution)/shard_map/coarse/pallas_call | solution.py:421
  30.6 12.4 %all-to-all-start = ((f32[64,5,4,128]{3,2,1,0:T(4,128)}), f32[64,5,4,128]{3,2,1,0:T(4,128)S(1)}, u32[]{:S(2)}, u32[]{:S(2)}) async-start(f32[64,5,4,128]{3,2,1,0:T(4,128)} %get-tuple-element.9), calls=%async_computation | async-start | bytes 1310720 | tf_op jit(solution)/shard_map/all_to_all | solution.py:444
  43.0 0.7 constant_dynamic-slice_fusion
  43.7 0.5 broadcast.153
  44.2 0.7 reduce.9
  44.9 0.2 fusion.2
  45.1 18.2 %all-to-all-done.arrived = f32[64,5,4,128]{3,2,1,0:T(4,128)S(1)} async-done(((f32[64,5,4,128]{3,2,1,0:T(4,128)}), f32[64,5,4,128]{3,2,1,0:T(4,128)S(1)}, u32[]{:S(2)}, u32[]{:S(2)}) %all-to-all-start) | async-done | bytes 655392 | tf_op jit(solution)/shard_map/all_to_all | solution.py:444
  63.3 6.1 %fine.1 = (f32[1280,128]{1,0:T(8,128)}, f32[1024,128]{1,0:T(8,128)S(1)}) custom-call(s32[32]{0:T(128)S(1)} %convert_add_fusion.lookups, s32[1]{0:T(128)} %bitcast.4.count, f32[64,5,4,128]{3,2,1,0:T(4,128)S(1)} %all-to-all-done.arrived, f32[1280,128]{1,0:T(8,128)S(1)} %bitcast.20), custom_call_target="tpu_custom_call" | custom-call | tf_op jit(solution)/shard_map/fine/pallas_call | solution.py:446
  69.4 23.4 %all_to_all.10 = f32[64,16,128]{2,1,0:T(8,128)S(1)} all-to-all(f32[64,16,128]{2,1,0:T(8,128)S(1)} %bitcast.21), channel_id=1, replica_groups=mesh['gx'=12,'gy'=64] {'gy'}, dimensions={0} | all-to-all | bytes 1048576 | tf_op jit(solution)/shard_map/all_to_all | solution.py:462
  92.8 4.5 %merge.1 = (f32[960,128]{1,0:T(8,128)}, f32[5,6,128]{2,1,0:T(8,128)S(1)}) custom-call(s32[128]{0:T(128)S(1)} %reshape.117.codes, f32[1024,128]{1,0:T(8,128)S(1)} %bitcast.18, f32[960,128]{1,0:T(8,128)S(1)} %get-tuple-element.11.swept, f32[6,5,6,128]{3,2,1,0:T(8,128)S(1)} %get-tuple-element.12.face_in), custom_call_target="tpu_custom_call" | custom-call | tf_op jit(solution)/shard_map/merge/pallas_call | solution.py:466
  97.2 1.9 %collective-permute-start.2 = (f32[5,6,128]{2,1,0:T(8,128)S(1)}, f32[5,6,128]{2,1,0:T(8,128)S(1)}, u32[]{:S(2)}, u32[]{:S(2)}) collective-permute-start(f32[5,6,128]{2,1,0:T(8,128)S(1)} %get-tuple-element.13), channel_id=1, source_target_pairs={{64,0},{128,64},{192,128},{256,192},{320,256},{384,320},{448,384},... | collective-permute-start | bytes 46088 | tf_op jit(solution)/shard_map/ppermute | solution.py:481
  99.2 2.6 %collective-permute-done.2.incoming = f32[5,6,128]{2,1,0:T(8,128)S(1)} collective-permute-done((f32[5,6,128]{2,1,0:T(8,128)S(1)}, f32[5,6,128]{2,1,0:T(8,128)S(1)}, u32[]{:S(2)}, u32[]{:S(2)}) %collective-permute-start.2) | collective-permute-done | bytes 15392 | tf_op jit(solution)/shard_map/ppermute | solution.py:481
  101.8 1.6 %last.1 = f32[6,5,32,128]{3,2,1,0:T(8,128)} custom-call(f32[5,6,128]{2,1,0:T(8,128)S(1)} %collective-permute-done.2.incoming, f32[6,5,32,128]{3,2,1,0:T(8,128)} %bitcast.24), custom_call_target="tpu_custom_call", output_to_operand_aliasing={{}: (1, {})} | custom-call | tf_op jit(solution)/shard_map/last/pallas_call | solution.py:483
  (15 shorter events, 0.2 us)
Async XLA Ops:
  0.6 23.0 %copy-start = (f32[6,5,32,128]{3,2,1,0:T(8,128)S(1)}, f32[6,5,32,128]{3,2,1,0:T(8,128)}, u32[]{:S(2)}) copy-start(f32[6,5,32,128]{3,2,1,0:T(8,128)} %param.6) | copy-start | bytes 1474564
  1.7 17.1 %copy-start.2 = (s32[1,2048]{1,0:T(1,128)S(1)}, s32[1,2048]{1,0:T(1,128)}, u32[]{:S(2)}) copy-start(s32[1,2048]{1,0:T(1,128)} %param.9) | copy-start | bytes 24580
  1.7 19.2 %collective-permute-start.1 = (f32[6,5,8,128]{3,2,1,0:T(8,128)S(1)}, f32[6,5,8,128]{3,2,1,0:T(8,128)S(1)}, u32[]{:S(2)}, u32[]{:S(2)}) collective-permute-start(f32[6,5,8,128]{3,2,1,0:T(8,128)S(1)} %get-tuple-element.20), channel_id=1, source_target_pairs={{64,0},{128,64},{192,128},{256,192},{320,256},{384,320},{448,384},... | collective-permute-start | bytes 368648 | tf_op jit(solution)/shard_map/ppermute | solution.py:398
  16.8 6.8 %collective-permute-start = (f32[6,5,8,128]{3,2,1,0:T(8,128)S(1)}, f32[6,5,8,128]{3,2,1,0:T(8,128)S(1)}, u32[]{:S(2)}, u32[]{:S(2)}) collective-permute-start(f32[6,5,8,128]{3,2,1,0:T(8,128)S(1)} %get-tuple-element.21), channel_id=1, source_target_pairs={{0,64},{64,128},{128,192},{192,256},{256,320},{320,384},{384,448},... | collective-permute-start | bytes 368648 | tf_op jit(solution)/shard_map/ppermute | solution.py:397
  19.7 0.7 copy-start.3
  30.6 32.7 %copy-start.1 = (f32[1,32,5,8,128]{4,3,2,1,0:T(8,128)S(1)}, f32[1,32,5,8,128]{4,3,2,1,0:T(8,128)}, u32[]{:S(2)}) copy-start(f32[1,32,5,8,128]{4,3,2,1,0:T(8,128)} %param.7) | copy-start | bytes 1966084
  30.6 32.7 %all-to-all-start = ((f32[64,5,4,128]{3,2,1,0:T(4,128)}), f32[64,5,4,128]{3,2,1,0:T(4,128)S(1)}, u32[]{:S(2)}, u32[]{:S(2)}) async-start(f32[64,5,4,128]{3,2,1,0:T(4,128)} %get-tuple-element.9), calls=%async_computation | async-start | bytes 1310720 | tf_op jit(solution)/shard_map/all_to_all | solution.py:444
  97.2 4.5 %collective-permute-start.2 = (f32[5,6,128]{2,1,0:T(8,128)S(1)}, f32[5,6,128]{2,1,0:T(8,128)S(1)}, u32[]{:S(2)}, u32[]{:S(2)}) collective-permute-start(f32[5,6,128]{2,1,0:T(8,128)S(1)} %get-tuple-element.13), channel_id=1, source_target_pairs={{64,0},{128,64},{192,128},{256,192},{320,256},{384,320},{448,384},... | collective-permute-start | bytes 46088 | tf_op jit(solution)/shard_map/ppermute | solution.py:481

commit v2 on v1

--- a/solution.py
+++ b/solution.py
@@ -1,5 +1,3 @@
-import functools
-
 import jax
 import jax.numpy as jnp
 from jax import lax
@@ -20,6 +18,8 @@
 BACK_ROWS = 8
 STARTS = ((0, 0, 0), (0, 1, 4), (1, 0, 16), (1, 1, 20))
 FACES = (0, 4, 8, 16, 20, 24)
+ALL_ITEMS = 8
+LEFT_ITEMS = 256
 VMEM = 48 * 1024 * 1024
 
 
@@ -31,13 +31,17 @@
 
 
 def limit_edges(center, left_edge, right_edge):
-    jump = right_edge - left_edge
-    product = jump * (6.0 * (center - 0.5 * (left_edge + right_edge)))
-    square = jump * jump
-    extremum = (right_edge - center) * (center - left_edge) <= 0.0
-    new_left = jnp.where(product > square, 3.0 * center - 2.0 * right_edge, left_edge)
-    new_right = jnp.where(-square > product, 3.0 * center - 2.0 * left_edge, right_edge)
-    return (jnp.where(extremum, center, new_left), jnp.where(extremum, center, new_right))
+    down = center - left_edge
+    up = right_edge - center
+    twice_down = down + down
+    twice_up = up + up
+    new_down = jnp.maximum(jnp.minimum(down, twice_up), 0.0) + jnp.minimum(
+        jnp.maximum(down, twice_up), 0.0
+    )
+    new_up = jnp.maximum(jnp.minimum(up, twice_down), 0.0) + jnp.minimum(
+        jnp.maximum(up, twice_down), 0.0
+    )
+    return (center - new_down, center + new_up)
 
 
 def euler_flux(state):
@@ -57,13 +61,12 @@
     return (fluxes, signal)
 
 
-def riemann(left, right):
+def double_flux(left, right):
     flux_left, signal_left = euler_flux(left)
     flux_right, signal_right = euler_flux(right)
-    half_signal = 0.5 * jnp.maximum(signal_left, signal_right)
+    signal = jnp.maximum(signal_left, signal_right)
     return tuple(
-        0.5 * (fl + fr) - half_signal * (r - l)
-        for fl, fr, l, r in zip(flux_left, flux_right, left, right)
+        (fl + fr) - signal * (r - l) for fl, fr, l, r in zip(flux_left, flux_right, left, right)
     )
 
 
@@ -75,19 +78,110 @@
     return jnp.take_along_axis(value, index, axis=1)
 
 
-def coarse_kernel(
-    codes, own, before, after, swept, sending, face_out, cells, fresh, fluxes, table
-):
+def swept_cells(cell, first, last):
+    values = {x: cell(x) for x in range(first - 3, last + 4)}
+    edges = {}
+    for x in range(first - 2, last + 2):
+        edges[x] = [
+            edge_value(*(values[x + o][f] for o in (-1, 0, 1, 2))) for f in range(FIELDS)
+        ]
+    limits = {}
+    for x in range(first - 1, last + 2):
+        limits[x] = [
+            limit_edges(values[x][f], edges[x - 1][f], edges[x][f]) for f in range(FIELDS)
+        ]
+    flux = {}
+    for x in range(first, last + 2):
+        flux[x] = double_flux([p[1] for p in limits[x - 1]], [p[0] for p in limits[x]])
+    return {
+        x: [
+            values[x][f] - 0.5 * STEP_RATIO * (flux[x + 1][f] - flux[x][f]) for f in range(FIELDS)
+        ]
+        for x in range(first, last + 1)
+    }
+
+
+def own_cell(own):
+    def cell(x):
+        return [
+            own[pl.ds(f * CELLS + x, TILES, stride=FIELDS * CELLS), :] for f in range(FIELDS)
+        ]
+
+    return cell
+
+
+def write_boxes(table, e, h, old, new):
+    lane = lane_index(TILES)
+    upper_z = (lane & 8) != 0
+    upper_y = (lane & 64) != 0
+
+    def swap(low, high, upper, shift):
+        return (
+            jnp.where(upper, pltpu.roll(high, shift, 1), low),
+            jnp.where(upper, high, pltpu.roll(low, LANES - shift, 1)),
+        )
+
+    for age, source in enumerate((old, new)):
+        for f in range(FIELDS):
+            c0, c1, c2, c3 = [source[o][f] for o in range(4)]
+            c0, c1 = swap(c0, c1, upper_z, 8)
+            c2, c3 = swap(c2, c3, upper_z, 8)
+            c0, c2 = swap(c0, c2, upper_y, 64)
+            c1, c3 = swap(c1, c3, upper_y, 64)
+            for q, value in enumerate((c0, c1, c2, c3)):
+                row = (e * 8 + q * 2 + h) * GHOST_ROWS + age * FIELDS + f
+                table[pl.ds(row, TILES, stride=16 * GHOST_ROWS), :] = value
+
+
+def inner_kernel(own, table, kept):
+    cell = own_cell(own)
+    new = {}
+    for first, last in ((8, 9), (14, 15), (18, 21), (24, 25)):
+        new.update(swept_cells(cell, first, last))
+    for x in (8, 9):
+        for f in range(FIELDS):
+            kept[x - 8, f] = new[x][f]
+    for e, h, start in STARTS[2:]:
+        where = [start + o for o in (-2, -1, 4, 5)]
+        write_boxes(table, e, h, [cell(x) for x in where], [new[x] for x in where])
+
+
+def edge_kernel(codes, own, before, kept, table_in, table, sending):
+    inner = own_cell(own)
+
+    def cell(x):
+        if x >= 0:
+            return inner(x)
+        return [before[pl.ds(f * 8 + 8 + x, TILES, stride=FIELDS * 8), :] for f in range(FIELDS)]
+
+    new = swept_cells(cell, -2, 5)
+    for x in (8, 9):
+        new[x] = [kept[x - 8, f] for f in range(FIELDS)]
+    for e, h, start in STARTS[:2]:
+        where = [start + o for o in (-2, -1, 4, 5)]
+        write_boxes(table, e, h, [cell(x) for x in where], [new[x] for x in where])
+
+    def send(k, carry):
+        for c in range(2):
+            base = jnp.maximum(codes[2 * k + c], 0) * GHOST_ROWS
+            sending[k, 3 * c] = table[pl.ds(base, 4), :]
+            sending[k, 3 * c + 1] = table[pl.ds(base + 4, 4), :]
+            sending[k, 2, 2 * c : 2 * c + 2] = table[pl.ds(base + 8, 2), :]
+        return carry
+
+    lax.fori_loop(0, sending.shape[0], send, 0, unroll=8)
+
+
+def coarse_kernel(codes, own, before, after, table, swept, face_out, lists, cells, fluxes):
     stride = FIELDS * CELLS
     for f in range(FIELDS):
-        for j in range(5):
-            cells[j, f] = before[pl.ds(f * 8 + 3 + j, TILES, stride=FIELDS * 8), :]
         for j in range(3):
-            cells[37 + j, f] = after[pl.ds(f * 8 + j, TILES, stride=FIELDS * 8), :]
+            cells[j, f] = before[pl.ds(f * 8 + 5 + j, TILES, stride=FIELDS * 8), :]
+            cells[35 + j, f] = after[pl.ds(f * 8 + j, TILES, stride=FIELDS * 8), :]
 
     def load_cells(x, carry):
         for f in range(FIELDS):
-            cells[x + 5, f] = own[pl.ds(f * CELLS + x, TILES, stride=stride), :]
+            cells[x + 3, f] = own[pl.ds(f * CELLS + x, TILES, stride=stride), :]
         return carry
 
     lax.fori_loop(0, CELLS, load_cells, 0, unroll=4)
@@ -102,72 +196,46 @@
             rights.append(right)
         return (tuple(edges), tuple(lefts), tuple(rights))
 
-    def advance(j, carry):
-        edges, rights, flux_before = carry
+    def advance(j, edges, rights):
         edges, lefts, next_rights = limited(j, edges)
-        flux = riemann(rights, lefts)
-        for f in range(FIELDS):
-            fluxes[j - 1, f] = flux[f]
-        if flux_before is not None:
-            for f in range(FIELDS):
-                fresh[j - 1, f] = cells[j - 1, f] - STEP_RATIO * (flux[f] - flux_before[f])
+        flux = double_flux(rights, lefts)
+        for f in range(FIELDS):
+            fluxes[j - 3, f] = flux[f]
         return (edges, next_rights, flux)
 
     edges = tuple(
         edge_value(cells[0, f], cells[1, f], cells[2, f], cells[3, f]) for f in range(FIELDS)
     )
     edges, _, rights = limited(2, edges)
-    carry = advance(3, (edges, rights, None))
-    carry = advance(4, carry)
-    carry = advance(5, carry)
+    carry = advance(3, edges, rights)
 
     def step(x, carry):
-        carry = advance(x + 6, carry)
-        for f in range(FIELDS):
-            swept[pl.ds(f * CELLS + x, TILES, stride=stride), :] = fresh[x + 5, f]
-        return carry
+        edges, rights, flux_before = carry
+        edges, rights, flux = advance(x + 4, edges, rights)
+        for f in range(FIELDS):
+            swept[pl.ds(f * CELLS + x, TILES, stride=stride), :] = cells[
+                x + 3, f
+            ] - 0.5 * STEP_RATIO * (flux[f] - flux_before[f])
+        return (edges, rights, flux)
 
     lax.fori_loop(0, CELLS, step, carry, unroll=4)
     for i, face in enumerate(FACES):
         for f in range(FIELDS):
-            face_out[i, f] = fluxes[face + 4, f]
-
-    lane = lane_index(TILES)
-    upper_z = (lane & 8) != 0
-    upper_y = (lane & 64) != 0
-
-    def swap(low, high, upper, shift):
-        return (
-            jnp.where(upper, pltpu.roll(high, shift, 1), low),
-            jnp.where(upper, high, pltpu.roll(low, LANES - shift, 1)),
-        )
-
-    for e, h, start in STARTS:
-        for age, source in enumerate((cells, fresh)):
-            for f in range(FIELDS):
-                c0, c1, c2, c3 = [source[start + 5 + o, f] for o in (-2, -1, 4, 5)]
-                c0, c1 = swap(c0, c1, upper_z, 8)
-                c2, c3 = swap(c2, c3, upper_z, 8)
-                c0, c2 = swap(c0, c2, upper_y, 64)
-                c1, c3 = swap(c1, c3, upper_y, 64)
-                for q, value in enumerate((c0, c1, c2, c3)):
-                    row = (e * 8 + q * 2 + h) * GHOST_ROWS + age * FIELDS + f
-                    table[pl.ds(row, TILES, stride=16 * GHOST_ROWS), :] = value
-
-    def send(k, carry):
-        for c in range(2):
-            code = codes[2 * k + c]
-
-            @pl.when(code >= 0)
-            def _():
-                base = code * GHOST_ROWS
-                sending[k, 3 * c] = table[pl.ds(base, 4), :]
-                sending[k, 3 * c + 1] = table[pl.ds(base + 4, 4), :]
-                sending[k, 2, 2 * c : 2 * c + 2] = table[pl.ds(base + 8, 2), :]
-
-        return carry
-
-    lax.fori_loop(0, sending.shape[0], send, 0, unroll=2)
+            face_out[i, f] = 0.5 * fluxes[face, f]
+
+    def collect(i, carry):
+        total, first = carry
+        code = codes[i]
+        entry = i * LANES + code
+        lists[ALL_ITEMS + total] = entry
+        lists[LEFT_ITEMS + first] = entry
+        valid = code >= 0
+        leftmost = valid & ((code & 9) == 0)
+        return (total + valid.astype(jnp.int32), first + leftmost.astype(jnp.int32))
+
+    total, first = lax.fori_loop(0, codes.shape[0], collect, (0, 0), unroll=4)
+    lists[0] = total
+    lists[1] = first
 
 
 def fine_kernel(lookups, count, arrived, fine, fine_out, back, ghosts, cells, packed):
@@ -203,10 +271,10 @@
             even, pltpu.roll(first, LANES - shift, 1), second
         )
 
-    def fold_four(a, b, c, d):
+    def fold_four(scale, a, b, c, d):
         low = pair(a, b, even_z, 1)
         high = pair(c, d, even_z, 1)
-        return pull_lanes(0.125 * pair(low, high, even_y, 16), gather_back)
+        return pull_lanes(scale * pair(low, high, even_y, 16), gather_back)
 
     def put_ghosts(slot, rows):
         for f in range(FIELDS):
@@ -240,7 +308,7 @@
                     limit_edges(cells[slot, j, f], edges[f], new_edges[f]) for f in range(FIELDS)
                 ]
                 if rights is not None:
-                    flux = riemann(rights, [p[0] for p in pairs])
+                    flux = double_flux(rights, [p[0] for p in pairs])
                     if before is None:
                         bounds.append(flux)
                     else:
@@ -248,7 +316,8 @@
                             keep(
                                 j - 4,
                                 f,
-                                cells[slot, j - 1, f] - STEP_RATIO * (flux[f] - before[f]),
+                                cells[slot, j - 1, f]
+                                - 0.5 * STEP_RATIO * (flux[f] - before[f]),
                             )
                     before = flux
                 rights = [p[1] for p in pairs]
@@ -285,11 +354,13 @@
         second = sweep(1, keep_final)
         rows = []
         for f in range(FIELDS):
-            rows.append(fold_four(*[final[2 * t, f] + final[2 * t + 1, f] for t in range(4)]))
+            rows.append(
+                fold_four(0.125, *[final[2 * t, f] + final[2 * t + 1, f] for t in range(4)])
+            )
         faces = [first[side][f] + second[side][f] for side in range(2) for f in range(FIELDS)]
         faces += [faces[-1], faces[-1]]
         for t in range(3):
-            rows.append(fold_four(*faces[4 * t : 4 * t + 4]))
+            rows.append(fold_four(0.0625, *faces[4 * t : 4 * t + 4]))
         for r, value in enumerate(rows):
             packed[pl.ds(g * 64 + r, 8, stride=BACK_ROWS), :] = value
         return carry
@@ -308,34 +379,63 @@
     lax.fori_loop(0, slots, put, 0, unroll=4)
 
 
-def merge_kernel(codes, came, swept, face_in, out, left_out, field, cover):
+def quad_offset(code):
+    quad = lax.shift_right_logical(code, 1) & 3
+    return lax.shift_right_logical(quad, 1) * 64 + (quad & 1) * 8
+
+
+def to_quad(value, offset, t):
+    return pltpu.roll(value, (offset + LANES - ((t // 2) * 64 + (t % 2) * 8)) & (LANES - 1), 1)
+
+
+def came_item(came, entry):
+    row = lax.shift_right_logical(entry, 7) * BACK_ROWS
+    return came[pl.ds(pl.multiple_of(row, BACK_ROWS), BACK_ROWS), :]
+
+
+def left_kernel(lists, came, face_in, left_out):
+    for f in range(FIELDS):
+        left_out[f] = jnp.zeros((TILES, LANES), jnp.float32)
+    quads = lane_index(1) & 72
+
+    def scatter(n, carry):
+        entry = lists[LEFT_ITEMS + n]
+        code = entry & (LANES - 1)
+        offset = quad_offset(code)
+        tile = pl.ds(lax.shift_right_logical(code, 4), 1)
+        value = came_item(came, entry)
+        moved = [to_quad(value, offset, t) for t in range(4)]
+        inside = quads == offset
+        for f in range(FIELDS):
+            row = FIELDS + f // 4
+            fix = STEP_RATIO * (face_in[0, f, tile] - moved[f % 4][row : row + 1])
+            left_out[f, tile] = jnp.where(inside, fix, left_out[f, tile])
+        return carry
+
+    lax.fori_loop(0, lists[1], scatter, 0)
+
+
+def merge_kernel(lists, came, swept, face_in, left_in, out, field, cover):
     stride = FIELDS * CELLS
     for i in range(TILES * 2):
         cover[8 * i : 8 * i + 8, :] = jnp.zeros((8, LANES), jnp.float32)
-    lane = lane_index(8)
-    quads = lane & 72
-
-    def scatter(i, carry):
-        code = codes[i]
-
-        @pl.when(code >= 0)
-        def _():
-            quad = lax.shift_right_logical(code, 1) & 3
-            offset = lax.shift_right_logical(quad, 1) * 64 + (quad & 1) * 8
-            line = lax.shift_right_logical(code, 3) * 8 + (code & 1) * 4
-            value = came[pl.ds(pl.multiple_of(i * BACK_ROWS, BACK_ROWS), BACK_ROWS), :]
-            inside = quads == offset
-            for t in range(4):
-                shift = (offset + LANES - ((t // 2) * 64 + (t % 2) * 8)) & (LANES - 1)
-                moved = pltpu.roll(value, shift, 1)
-                rows = pl.ds(pl.multiple_of((line + t) * 8, 8), 8)
-                field[rows, :] = jnp.where(inside, moved, field[rows, :])
-            rows = pl.ds(line, 4)
-            cover[rows, :] = jnp.where(inside[:4], 1.0, cover[rows, :])
-
+    quads = lane_index(8) & 72
+
+    def scatter(n, carry):
+        entry = lists[ALL_ITEMS + n]
+        code = entry & (LANES - 1)
+        offset = quad_offset(code)
+        line = lax.shift_right_logical(code, 3) * 8 + (code & 1) * 4
+        value = came_item(came, entry)
+        inside = quads == offset
+        for t in range(4):
+            rows = pl.ds(pl.multiple_of((line + t) * 8, 8), 8)
+            field[rows, :] = jnp.where(inside, to_quad(value, offset, t), field[rows, :])
+        rows = pl.ds(line, 4)
+        cover[rows, :] = jnp.where(inside[:4], 1.0, cover[rows, :])
         return carry
 
-    lax.fori_loop(0, codes.shape[0], scatter, 0, unroll=2)
+    lax.fori_loop(0, lists[0], scatter, 0)
 
     for t in range(TILES):
         for e in range(2):
@@ -350,6 +450,9 @@
         line = e * 8 + h * 4
         hit = cover[pl.ds(line, TILES, stride=16), :] > 0.5
         for side in range(2):
+            cell = start + 4 if side else start - 1
+            if cell < 0:
+                continue
             for f in range(FIELDS):
                 item = side * FIELDS + f
                 face = field[
@@ -358,12 +461,8 @@
                 coarse = face_in[FACES.index(start + 4 * side), f]
                 fix = STEP_RATIO * ((face - coarse) if side else (coarse - face))
                 fix = jnp.where(hit, fix, 0.0)
-                cell = start + 4 if side else start - 1
-                if cell < 0:
-                    left_out[f] = fix
-                else:
-                    rows = pl.ds(f * CELLS + cell, TILES, stride=stride)
-                    out[rows, :] = out[rows, :] + fix
+                rows = pl.ds(f * CELLS + cell, TILES, stride=stride)
+                out[rows, :] = out[rows, :] + fix
 
 
 def last_kernel(incoming, block, out):
@@ -418,29 +517,52 @@
     twin = (mine[:, None] == mine[None, :]) & (order[None, :] < order[:, None])
     lookups = 2 * mine + jnp.any(twin, axis=1).astype(jnp.int32)
 
-    swept, sending, faces = pl.pallas_call(
+    whole = coarse_state.reshape(-1, LANES)
+    before = before.reshape(-1, LANES)
+    table_shape = shaped(TILES * 16 * GHOST_ROWS, LANES)
+    table, kept = pl.pallas_call(
+        inner_kernel,
+        out_shape=(table_shape, shaped(2, FIELDS, TILES, LANES)),
+        in_specs=[in_vmem()],
+        out_specs=(in_vmem(), in_vmem()),
+        cost_estimate=pl.CostEstimate(flops=4_000_000, bytes_accessed=3_000_000, transcendentals=0),
+        compiler_params=params,
+        name="inner",
+    )(whole)
+    table, sending = pl.pallas_call(
+        edge_kernel,
+        out_shape=(table_shape, shaped(groups, 5, 4, LANES)),
+        in_specs=[in_smem(), in_vmem(), in_vmem(), in_vmem(), in_vmem()],
+        out_specs=(in_vmem(), in_vmem()),
+        input_output_aliases={4: 0},
+        compiler_params=params,
+        name="edge",
+    )(codes, whole, before, kept, table)
+    swept, faces, lists = pl.pallas_call(
         coarse_kernel,
         out_shape=(
             shaped(TILES * FIELDS * CELLS, LANES),
-            shaped(groups, 5, 4, LANES),
             shaped(len(FACES), FIELDS, TILES, LANES),
+            jax.ShapeDtypeStruct((512,), jnp.int32),
         ),
-        in_specs=[in_smem(), in_vmem(), in_vmem(), in_vmem()],
-        out_specs=(in_vmem(), in_vmem(), in_vmem()),
+        in_specs=[
+            in_smem(),
+            in_vmem(),
+            in_vmem(),
+            in_vmem(),
+            pl.BlockSpec(memory_space=pl.ANY),
+        ],
+        out_specs=(in_vmem(), in_vmem(), in_smem()),
         scratch_shapes=[
-            pltpu.VMEM((40, FIELDS, TILES, LANES), jnp.float32),
-            pltpu.VMEM((40, FIELDS, TILES, LANES), jnp.float32),
-            pltpu.VMEM((40, FIELDS, TILES, LANES), jnp.float32),
-            pltpu.VMEM((TILES * 16 * GHOST_ROWS, LANES), jnp.float32),
+            pltpu.VMEM((CELLS + 6, FIELDS, TILES, LANES), jnp.float32),
+            pltpu.VMEM((CELLS + 1, FIELDS, TILES, LANES), jnp.float32),
         ],
+        cost_estimate=pl.CostEstimate(
+            flops=10_000_000, bytes_accessed=12_000_000, transcendentals=0
+        ),
         compiler_params=params,
         name="coarse",
-    )(
-        codes,
-        coarse_state.reshape(-1, LANES),
-        before.reshape(-1, LANES),
-        after.reshape(-1, LANES),
-    )
+    )(codes, whole, before, after.reshape(-1, LANES), table)
     arrived = lax.all_to_all(sending, "gy", split_axis=0, concat_axis=0, tiled=True)
 
     fine_out, back = pl.pallas_call(
@@ -463,22 +585,35 @@
         back.reshape(groups, 2 * BACK_ROWS, LANES), "gy", split_axis=0, concat_axis=0, tiled=True
     )
 
-    merged, left_fix = pl.pallas_call(
+    came = came.reshape(-1, LANES)
+    left_fix = pl.pallas_call(
+        left_kernel,
+        out_shape=shaped(FIELDS, TILES, LANES),
+        in_specs=[in_smem(), in_vmem(), in_vmem()],
+        out_specs=in_vmem(),
+        compiler_params=params,
+        name="left",
+    )(lists, came, faces)
+    incoming = lax.ppermute(left_fix, "gx", down)
+    merged = pl.pallas_call(
         merge_kernel,
-        out_shape=(
-            shaped(TILES * FIELDS * CELLS, LANES),
-            shaped(FIELDS, TILES, LANES),
-        ),
-        in_specs=[in_smem(), in_vmem(), in_vmem(), in_vmem()],
-        out_specs=(in_vmem(), in_vmem()),
+        out_shape=shaped(TILES * FIELDS * CELLS, LANES),
+        in_specs=[
+            in_smem(),
+            in_vmem(),
+            in_vmem(),
+            in_vmem(),
+            pl.BlockSpec(memory_space=pl.ANY),
+        ],
+        out_specs=in_vmem(),
         scratch_shapes=[
             pltpu.VMEM((TILES * 16 * 8, LANES), jnp.float32),
             pltpu.VMEM((TILES * 16, LANES), jnp.float32),
         ],
+        cost_estimate=pl.CostEstimate(flops=2_000_000, bytes_accessed=8_000_000, transcendentals=0),
         compiler_params=params,
         name="merge",
-    )(codes, came.reshape(-1, LANES), swept, faces)
-    incoming = lax.ppermute(left_fix, "gx", down)
+    )(lists, came, swept, faces, left_fix)
     spec = pl.BlockSpec((TILES, FIELDS, 8, LANES), lambda i: (0, 0, 3, 0))
     coarse_out = pl.pallas_call(
         last_kernel,

time: 104 us -> 93.5 us (0.90)
  blocking collectives: 23.4 us -> 0 us
  waiting for transfers between devices: 23.6 us -> 39.2 us
  starting transfers between devices: 31.3 us -> 28.5 us
    all_to_all x1 -> x0, blocking collectives: 23.4 us -> none  [body(): lax.all_to_all(back.reshape(groups, 2 * BACK_ROWS, LANES), 'gy', split_ax...]
    ppermute x1, starting transfers between devices: 15.1 us -> 3.36 us  [body(): after = lax.ppermute(coarse_state[:, :, :8], 'gx', down)]
    all_to_all x0 -> x1, waiting for transfers between devices: none -> 7.62 us  [body(): lax.all_to_all(back.reshape(groups, 2 * BACK_ROWS, LANES), 'gy', split_ax...]
    ppermute x1, waiting for transfers between devices: 2.81 us -> 10.4 us  [body(): before = lax.ppermute(coarse_state[:, :, CELLS - 8:], 'gx', up)]
    all_to_all x0 -> x1, starting transfers between devices: none -> 5.86 us  [body(): lax.all_to_all(back.reshape(groups, 2 * BACK_ROWS, LANES), 'gy', split_ax...]
    pallas_call x1 -> x4, Pallas kernels: 4.47 us -> 8.13 us  [the longest x1 3.8 us: body(): pl.pallas_call(merge_kernel, out_shape=shaped(TILES * FIELDS * CELLS, LAN...]
    pallas_call x1, Pallas kernels: 6.95 us -> 3.75 us  [body(): pl.pallas_call(coarse_kernel, out_shape=(shaped(TILES * FIELDS * CELLS, L...]
    ppermute x1, waiting for transfers between devices: 0.01 us -> 2.96 us  [body(): after = lax.ppermute(coarse_state[:, :, :8], 'gx', down)]
  transfers between devices with their start and end apart: 4 -> 5, of which waited for: 3 -> 4; matrix products, arithmetic and copies ran while one was open for 3% -> 4% of each run, Pallas kernels for 0% -> 9%
where the time goes in v2:
time: 93.5 us; the launch traced here: 93 us
  waiting for transfers between devices  39.2 us (42%)
  starting transfers between devices  28.5 us (30%)
  Pallas kernels  19.3 us (21%)
  local copies, waits for them, and re-layouts  3.34 us (4%)
  other arithmetic  1.85 us (2%)
    all_to_all x1, waiting for transfers between devices, body(): lax.all_to_all(sending, 'gy', split_axis=0, concat_axis=0, tiled=True)  18.2 us
    all_to_all x1, starting transfers between devices, body(): lax.all_to_all(sending, 'gy', split_axis=0, concat_axis=0, tiled=True)  11.5 us
    ppermute x1, waiting for transfers between devices, body(): before = lax.ppermute(coarse_state[:, :, CELLS - 8:], 'gx', up)  10.4 us
    all_to_all x1, waiting for transfers between devices, body(): lax.all_to_all(back.reshape(groups, 2 * BACK_ROWS, LANES), 'gy', split_ax...  7.62 us
    all_to_all x1, starting transfers between devices, body(): lax.all_to_all(back.reshape(groups, 2 * BACK_ROWS, LANES), 'gy', split_ax...  5.86 us
    pallas_call x1, Pallas kernels, body(): pl.pallas_call(fine_kernel, out_shape=(shaped(slots * FIELDS * FINE, LANE...  5.83 us
    ppermute x1, starting transfers between devices, body(): before = lax.ppermute(coarse_state[:, :, CELLS - 8:], 'gx', up)  4.83 us
    pallas_call x1, Pallas kernels, body(): pl.pallas_call(merge_kernel, out_shape=shaped(TILES * FIELDS * CELLS, LAN...  3.8 us
  transfers between devices with their start and end apart: 5, of which 4 were waited for; matrix products, arithmetic and copies ran while one was open for 4% of the time, Pallas kernels for 9%

profile of v2, /device:TPU:1, one launch (start us, length us, event | category | flops | bytes accessed | tf_op | source)
XLA Modules:
  0.0 93.0 jit_solution(7958111542516459518)
XLA Ops:
  0.6 1.0 %fusion.5 = (f32[6,5,8,128]{3,2,1,0:T(8,128)S(1)}, f32[6,5,8,128]{3,2,1,0:T(8,128)S(1)}) fusion(f32[6,5,32,128]{3,2,1,0:T(8,128)} %param.6), kind=kLoop, calls=%fused_computation.19 | loop fusion | bytes 491520 | tf_op jit(solution)/shard_map/slice | solution.py:497
  1.7 4.8 %collective-permute-start = (f32[6,5,8,128]{3,2,1,0:T(8,128)S(1)}, f32[6,5,8,128]{3,2,1,0:T(8,128)S(1)}, u32[]{:S(2)}, u32[]{:S(2)}) collective-permute-start(f32[6,5,8,128]{3,2,1,0:T(8,128)S(1)} %get-tuple-element.25), channel_id=1, source_target_pairs={{0,64},{64,128},{128,192},{192,256},{256,320},{320,384},{384,448},... | collective-permute-start | bytes 368648 | tf_op jit(solution)/shard_map/ppermute | solution.py:496
  6.6 0.8 compare_reduce_fusion
  7.5 0.7 copy-done.3
  8.2 0.2 select_reduce_fusion.1
  8.6 0.9 inner.1
  9.5 10.4 %collective-permute-done = f32[6,5,8,128]{3,2,1,0:T(8,128)S(1)} collective-permute-done((f32[6,5,8,128]{3,2,1,0:T(8,128)S(1)}, f32[6,5,8,128]{3,2,1,0:T(8,128)S(1)}, u32[]{:S(2)}, u32[]{:S(2)}) %collective-permute-start) | collective-permute-done | bytes 122912 | tf_op jit(solution)/shard_map/ppermute | solution.py:496
  19.9 2.2 %edge.1 = (f32[960,128]{1,0:T(8,128)S(1)}, f32[64,5,4,128]{3,2,1,0:T(4,128)}) custom-call(s32[128]{0:T(128)S(1)} %reshape.117.codes, f32[960,128]{1,0:T(8,128)S(1)} %bitcast.19, f32[240,128]{1,0:T(8,128)S(1)} %bitcast.24, f32[2,5,6,128]{3,2,1,0:T(8,128)S(1)} %get-tuple-element.11.kept, ...), custom_call_target="tpu_custom_call", output_to_operand_aliasing={{0}: (4, {})} | custom-call | tf_op jit(solution)/shard_map/edge/pallas_call | solution.py:532
  22.1 11.5 %all-to-all-start = ((f32[64,5,4,128]{3,2,1,0:T(4,128)}), f32[64,5,4,128]{3,2,1,0:T(4,128)S(1)}, u32[]{:S(2)}, u32[]{:S(2)}) async-start(f32[64,5,4,128]{3,2,1,0:T(4,128)} %get-tuple-element.15), calls=%async_computation | async-start | bytes 1310720 | tf_op jit(solution)/shard_map/all_to_all | solution.py:566
  33.6 0.7 constant_dynamic-slice_fusion
  34.2 0.5 broadcast.153
  34.7 0.7 reduce.9
  35.5 0.2 fusion.2
  35.7 18.2 %all-to-all-done.arrived = f32[64,5,4,128]{3,2,1,0:T(4,128)S(1)} async-done(((f32[64,5,4,128]{3,2,1,0:T(4,128)}), f32[64,5,4,128]{3,2,1,0:T(4,128)S(1)}, u32[]{:S(2)}, u32[]{:S(2)}) %all-to-all-start) | async-done | bytes 655392 | tf_op jit(solution)/shard_map/all_to_all | solution.py:566
  53.9 5.8 %fine.1 = (f32[1280,128]{1,0:T(8,128)}, f32[1024,128]{1,0:T(8,128)}) custom-call(s32[32]{0:T(128)S(1)} %convert_add_fusion.lookups, s32[1]{0:T(128)} %bitcast.7.count, f32[64,5,4,128]{3,2,1,0:T(4,128)S(1)} %all-to-all-done.arrived, f32[1280,128]{1,0:T(8,128)S(1)} %bitcast.23), custom_call_target="tpu_custom_call" | custom-call | tf_op jit(solution)/shard_map/fine/pallas_call | solution.py:568
  59.8 5.9 %all-to-all-start.1 = ((f32[64,16,128]{2,1,0:T(8,128)}), f32[64,16,128]{2,1,0:T(8,128)S(1)}, u32[]{:S(2)}, u32[]{:S(2)}) async-start(f32[64,16,128]{2,1,0:T(8,128)} %bitcast.9), calls=%async_computation.1 | async-start | bytes 1048576 | tf_op jit(solution)/shard_map/all_to_all | solution.py:584
  65.6 3.4 %collective-permute-start.1 = (f32[6,5,8,128]{3,2,1,0:T(8,128)S(1)}, f32[6,5,8,128]{3,2,1,0:T(8,128)S(1)}, u32[]{:S(2)}, u32[]{:S(2)}) collective-permute-start(f32[6,5,8,128]{3,2,1,0:T(8,128)S(1)} %get-tuple-element.24), channel_id=1, source_target_pairs={{64,0},{128,64},{192,128},{256,192},{320,256},{384,320},{448,384},... | collective-permute-start | bytes 368648 | tf_op jit(solution)/shard_map/ppermute | solution.py:497
  69.0 3.0 %collective-permute-done.1 = f32[6,5,8,128]{3,2,1,0:T(8,128)S(1)} collective-permute-done((f32[6,5,8,128]{3,2,1,0:T(8,128)S(1)}, f32[6,5,8,128]{3,2,1,0:T(8,128)S(1)}, u32[]{:S(2)}, u32[]{:S(2)}) %collective-permute-start.1) | collective-permute-done | bytes 122912 | tf_op jit(solution)/shard_map/ppermute | solution.py:497
  72.0 3.8 %coarse.1 = (f32[960,128]{1,0:T(8,128)S(1)}, f32[6,5,6,128]{3,2,1,0:T(8,128)S(1)}, s32[512]{0:T(512)S(1)}) custom-call(s32[128]{0:T(128)S(1)} %reshape.117.codes, f32[960,128]{1,0:T(8,128)S(1)} %bitcast.20, f32[240,128]{1,0:T(8,128)S(1)} %bitcast.25, f32[240,128]{1,0:T(8,128)S(1)} %bitcast.26, f32[960,128]{1,0:T(8,128)S(1)} %get-tuple-element.13.table), custom_call_target="tpu_custom_call" | custom-call | flops 10000000 | bytes 12000000 | tf_op jit(solution)/shard_map/coarse/pallas_call | solution.py:541
  75.7 7.6 %all-to-all-done.1 = f32[64,16,128]{2,1,0:T(8,128)S(1)} async-done(((f32[64,16,128]{2,1,0:T(8,128)}), f32[64,16,128]{2,1,0:T(8,128)S(1)}, u32[]{:S(2)}, u32[]{:S(2)}) %all-to-all-start.1) | async-done | bytes 524320 | tf_op jit(solution)/shard_map/all_to_all | solution.py:584
  83.3 1.3 %left.1.left_in = f32[5,6,128]{2,1,0:T(8,128)S(1)} custom-call(s32[512]{0:T(512)S(1)} %get-tuple-element.14.lists, f32[1024,128]{1,0:T(8,128)S(1)} %bitcast.21, f32[6,5,6,128]{3,2,1,0:T(8,128)S(1)} %get-tuple-element.17.face_in), custom_call_target="tpu_custom_call" | custom-call | tf_op jit(solution)/shard_map/left/pallas_call | solution.py:589
  84.6 3.0 %collective-permute-start.2 = (f32[5,6,128]{2,1,0:T(8,128)S(1)}, f32[5,6,128]{2,1,0:T(8,128)S(1)}, u32[]{:S(2)}, u32[]{:S(2)}) collective-permute-start(f32[5,6,128]{2,1,0:T(8,128)S(1)} %left.1.left_in), channel_id=1, source_target_pairs={{64,0},{128,64},{192,128},{256,192},{320,256},{384,320},{448,384},... | collective-permute-start | bytes 46088 | tf_op jit(solution)/shard_map/ppermute | solution.py:597
  87.6 3.8 %merge.1 = f32[960,128]{1,0:T(8,128)} custom-call(s32[512]{0:T(512)S(1)} %get-tuple-element.14.lists, f32[1024,128]{1,0:T(8,128)S(1)} %bitcast.22, f32[960,128]{1,0:T(8,128)S(1)} %get-tuple-element.18.swept, f32[6,5,6,128]{3,2,1,0:T(8,128)S(1)} %get-tuple-element.17.face_in, f32[5,6,128]{2,1,0:T(8,128)S(1)} %left.1.left_in), custom_call_target="tpu_custom_call" | custom-call | flops 2000000 | bytes 8000000 | tf_op jit(solution)/shard_map/merge/pallas_call | solution.py:598
  91.4 1.6 %last.1 = f32[6,5,32,128]{3,2,1,0:T(8,128)} custom-call(f32[5,6,128]{2,1,0:T(8,128)S(1)} %collective-permute-done.2.incoming, f32[6,5,32,128]{3,2,1,0:T(8,128)} %bitcast.27), custom_call_target="tpu_custom_call", output_to_operand_aliasing={{}: (1, {})} | custom-call | tf_op jit(solution)/shard_map/last/pallas_call | solution.py:618
  (19 shorter events, 0.5 us)
Async XLA Ops:
  0.6 8.0 %copy-start = (f32[6,5,32,128]{3,2,1,0:T(8,128)S(1)}, f32[6,5,32,128]{3,2,1,0:T(8,128)}, u32[]{:S(2)}) copy-start(f32[6,5,32,128]{3,2,1,0:T(8,128)} %param.6) | copy-start | bytes 1474564
  1.7 4.9 %copy-start.2 = (s32[1,2048]{1,0:T(1,128)S(1)}, s32[1,2048]{1,0:T(1,128)}, u32[]{:S(2)}) copy-start(s32[1,2048]{1,0:T(1,128)} %param.9) | copy-start | bytes 24580
  1.7 18.2 %collective-permute-start = (f32[6,5,8,128]{3,2,1,0:T(8,128)S(1)}, f32[6,5,8,128]{3,2,1,0:T(8,128)S(1)}, u32[]{:S(2)}, u32[]{:S(2)}) collective-permute-start(f32[6,5,8,128]{3,2,1,0:T(8,128)S(1)} %get-tuple-element.25), channel_id=1, source_target_pairs={{0,64},{64,128},{128,192},{192,256},{256,320},{320,384},{384,448},... | collective-permute-start | bytes 368648 | tf_op jit(solution)/shard_map/ppermute | solution.py:496
  7.5 0.7 copy-start.3
  22.1 31.9 %copy-start.1 = (f32[1,32,5,8,128]{4,3,2,1,0:T(8,128)S(1)}, f32[1,32,5,8,128]{4,3,2,1,0:T(8,128)}, u32[]{:S(2)}) copy-start(f32[1,32,5,8,128]{4,3,2,1,0:T(8,128)} %param.7) | copy-start | bytes 1966084
  22.1 31.8 %all-to-all-start = ((f32[64,5,4,128]{3,2,1,0:T(4,128)}), f32[64,5,4,128]{3,2,1,0:T(4,128)S(1)}, u32[]{:S(2)}, u32[]{:S(2)}) async-start(f32[64,5,4,128]{3,2,1,0:T(4,128)} %get-tuple-element.15), calls=%async_computation | async-start | bytes 1310720 | tf_op jit(solution)/shard_map/all_to_all | solution.py:566
  59.8 23.6 %all-to-all-start.1 = ((f32[64,16,128]{2,1,0:T(8,128)}), f32[64,16,128]{2,1,0:T(8,128)S(1)}, u32[]{:S(2)}, u32[]{:S(2)}) async-start(f32[64,16,128]{2,1,0:T(8,128)} %bitcast.9), calls=%async_computation.1 | async-start | bytes 1048576 | tf_op jit(solution)/shard_map/all_to_all | solution.py:584
  65.6 6.3 %collective-permute-start.1 = (f32[6,5,8,128]{3,2,1,0:T(8,128)S(1)}, f32[6,5,8,128]{3,2,1,0:T(8,128)S(1)}, u32[]{:S(2)}, u32[]{:S(2)}) collective-permute-start(f32[6,5,8,128]{3,2,1,0:T(8,128)S(1)} %get-tuple-element.24), channel_id=1, source_target_pairs={{64,0},{128,64},{192,128},{256,192},{320,256},{384,320},{448,384},... | collective-permute-start | bytes 368648 | tf_op jit(solution)/shard_map/ppermute | solution.py:497
  84.6 6.8 %collective-permute-start.2 = (f32[5,6,128]{2,1,0:T(8,128)S(1)}, f32[5,6,128]{2,1,0:T(8,128)S(1)}, u32[]{:S(2)}, u32[]{:S(2)}) collective-permute-start(f32[5,6,128]{2,1,0:T(8,128)S(1)} %left.1.left_in), channel_id=1, source_target_pairs={{64,0},{128,64},{192,128},{256,192},{320,256},{384,320},{448,384},... | collective-permute-start | bytes 46088 | tf_op jit(solution)/shard_map/ppermute | solution.py:597

commit v3 on v2

--- a/solution.py
+++ b/solution.py
@@ -16,8 +16,11 @@
 STEP_RATIO = 0.1
 GHOST_ROWS = 2 * FIELDS
 BACK_ROWS = 8
+BATCH = 16
 STARTS = ((0, 0, 0), (0, 1, 4), (1, 0, 16), (1, 1, 20))
+KEPT = (3, 4, 5, 8, 9)
 FACES = (0, 4, 8, 16, 20, 24)
+MERGE_STEP = 4
 ALL_ITEMS = 8
 LEFT_ITEMS = 256
 VMEM = 48 * 1024 * 1024
@@ -136,11 +139,11 @@
 def inner_kernel(own, table, kept):
     cell = own_cell(own)
     new = {}
-    for first, last in ((8, 9), (14, 15), (18, 21), (24, 25)):
+    for first, last in ((3, 5), (8, 9), (14, 15), (18, 21), (24, 25)):
         new.update(swept_cells(cell, first, last))
-    for x in (8, 9):
-        for f in range(FIELDS):
-            kept[x - 8, f] = new[x][f]
+    for i, x in enumerate(KEPT):
+        for f in range(FIELDS):
+            kept[i, f] = new[x][f]
     for e, h, start in STARTS[2:]:
         where = [start + o for o in (-2, -1, 4, 5)]
         write_boxes(table, e, h, [cell(x) for x in where], [new[x] for x in where])
@@ -154,9 +157,14 @@
             return inner(x)
         return [before[pl.ds(f * 8 + 8 + x, TILES, stride=FIELDS * 8), :] for f in range(FIELDS)]
 
-    new = swept_cells(cell, -2, 5)
-    for x in (8, 9):
-        new[x] = [kept[x - 8, f] for f in range(FIELDS)]
+    half = 8 * GHOST_ROWS
+    for t in range(TILES):
+        rows = slice((2 * t + 1) * half, (2 * t + 2) * half)
+        table[rows, :] = table_in[rows, :]
+    new = swept_cells(cell, -2, -1)
+    new.update(swept_cells(cell, 2, 2))
+    for i, x in enumerate(KEPT):
+        new[x] = [kept[i, f] for f in range(FIELDS)]
     for e, h, start in STARTS[:2]:
         where = [start + o for o in (-2, -1, 4, 5)]
         write_boxes(table, e, h, [cell(x) for x in where], [new[x] for x in where])
@@ -234,14 +242,16 @@
         return (total + valid.astype(jnp.int32), first + leftmost.astype(jnp.int32))
 
     total, first = lax.fori_loop(0, codes.shape[0], collect, (0, 0), unroll=4)
-    lists[0] = total
+    for i in range(MERGE_STEP):
+        lists[ALL_ITEMS + total + i] = TILES * 16
+    lists[0] = lax.shift_right_logical(total + (MERGE_STEP - 1), 2)
     lists[1] = first
 
 
-def fine_kernel(lookups, count, arrived, fine, fine_out, back, ghosts, cells, packed):
-    slots = lookups.shape[0]
+def fine_kernel(lookups, arrived, fine, final_out, back, ghosts, cells, packed):
+    slots = fine.shape[0] // (FIELDS * FINE)
     stride = FIELDS * FINE
-    live = count[0]
+    live = lookups[slots]
 
     def fetch(s, carry):
         look = lookups[s]
@@ -252,9 +262,9 @@
         ghosts[pl.ds(s + 8 * slots, 2, stride=slots), :] = arrived[owner, 2, pl.ds(2 * pos, 2)]
         return carry
 
-    lax.fori_loop(0, slots, fetch, 0, unroll=4)
-
-    lane = lane_index(8)
+    lax.fori_loop(0, slots, fetch, 0, unroll=8)
+
+    lane = lane_index(BATCH)
     fine_y = lax.shift_right_logical(lane, 4)
     fine_z = lane & 15
     spread = lax.shift_right_logical(fine_y, 1) * 16 + lax.shift_right_logical(fine_z, 1)
@@ -326,29 +336,25 @@
         return bounds
 
     def group(g, carry):
-        base = g * (8 * stride)
-        old = [ghosts[pl.ds(pl.multiple_of(f * slots + g * 8, 8), 8), :] for f in range(FIELDS)]
-        new = [
-            ghosts[pl.ds(pl.multiple_of((FIELDS + f) * slots + g * 8, 8), 8), :]
-            for f in range(FIELDS)
+        base = g * (BATCH * stride)
+        rows = [
+            ghosts[pl.ds(pl.multiple_of(r * slots + g * BATCH, 8), BATCH), :]
+            for r in range(GHOST_ROWS)
         ]
-        put_ghosts(0, old)
-        put_ghosts(1, [0.5 * (o + n) for o, n in zip(old, new)])
+        put_ghosts(0, rows[:FIELDS])
+        put_ghosts(1, [0.5 * (o + n) for o, n in zip(rows[:FIELDS], rows[FIELDS:])])
         for x in range(FINE):
             for f in range(FIELDS):
-                cells[0, x + 3, f] = fine[pl.ds(base + f * FINE + x, 8, stride=stride), :]
+                cells[0, x + 3, f] = fine[pl.ds(base + f * FINE + x, BATCH, stride=stride), :]
 
         def keep_middle(x, f, value):
             cells[1, x + 3, f] = value
 
-        active = (lax.broadcasted_iota(jnp.int32, (8, LANES), 0) + g * 8) < live
         final = {}
 
         def keep_final(x, f, value):
             final[x, f] = value
-            fine_out[pl.ds(base + f * FINE + x, 8, stride=stride), :] = jnp.where(
-                active, value, 0.0
-            )
+            final_out[pl.ds(base + f * FINE + x, BATCH, stride=stride), :] = value
 
         first = sweep(0, keep_middle)
         second = sweep(1, keep_final)
@@ -362,10 +368,10 @@
         for t in range(3):
             rows.append(fold_four(0.0625, *faces[4 * t : 4 * t + 4]))
         for r, value in enumerate(rows):
-            packed[pl.ds(g * 64 + r, 8, stride=BACK_ROWS), :] = value
+            packed[pl.ds(g * (BATCH * BACK_ROWS) + r, BATCH, stride=BACK_ROWS), :] = value
         return carry
 
-    lax.fori_loop(0, slots // 8, group, 0)
+    lax.fori_loop(0, slots // BATCH, group, 0)
 
     def put(s, carry):
         @pl.when(s < live)
@@ -376,7 +382,7 @@
 
         return carry
 
-    lax.fori_loop(0, slots, put, 0, unroll=4)
+    lax.fori_loop(0, slots, put, 0, unroll=8)
 
 
 def quad_offset(code):
@@ -409,30 +415,33 @@
         for f in range(FIELDS):
             row = FIELDS + f // 4
             fix = STEP_RATIO * (face_in[0, f, tile] - moved[f % 4][row : row + 1])
-            left_out[f, tile] = jnp.where(inside, fix, left_out[f, tile])
+            pltpu.store(left_out.at[f, tile], fix, mask=inside)
         return carry
 
     lax.fori_loop(0, lists[1], scatter, 0)
 
 
 def merge_kernel(lists, came, swept, face_in, left_in, out, field, cover):
+    out[...] = swept[...]
     stride = FIELDS * CELLS
     for i in range(TILES * 2):
         cover[8 * i : 8 * i + 8, :] = jnp.zeros((8, LANES), jnp.float32)
     quads = lane_index(8) & 72
 
+    ones = jnp.ones((4, LANES), jnp.float32)
+
     def scatter(n, carry):
-        entry = lists[ALL_ITEMS + n]
-        code = entry & (LANES - 1)
-        offset = quad_offset(code)
-        line = lax.shift_right_logical(code, 3) * 8 + (code & 1) * 4
-        value = came_item(came, entry)
-        inside = quads == offset
-        for t in range(4):
-            rows = pl.ds(pl.multiple_of((line + t) * 8, 8), 8)
-            field[rows, :] = jnp.where(inside, to_quad(value, offset, t), field[rows, :])
-        rows = pl.ds(line, 4)
-        cover[rows, :] = jnp.where(inside[:4], 1.0, cover[rows, :])
+        for i in range(MERGE_STEP):
+            entry = lists[ALL_ITEMS + n * MERGE_STEP + i]
+            code = entry & (LANES - 1)
+            offset = quad_offset(code)
+            line = lax.shift_right_logical(code, 3) * 8 + (code & 1) * 4
+            value = came_item(came, entry)
+            inside = quads == offset
+            for t in range(4):
+                rows = pl.ds(pl.multiple_of((line + t) * 8, 8), 8)
+                pltpu.store(field.at[rows, :], to_quad(value, offset, t), mask=inside)
+            pltpu.store(cover.at[pl.ds(line, 4), :], ones, mask=inside[:4])
         return carry
 
     lax.fori_loop(0, lists[0], scatter, 0)
@@ -443,8 +452,7 @@
             for f in range(FIELDS):
                 row = t * stride + f * CELLS + e * 16
                 value = field[pl.ds((t * 16 + e * 8) * 8 + f, 8, stride=8), :]
-                out[row : row + 8, :] = jnp.where(hit, value, swept[row : row + 8, :])
-                out[row + 8 : row + 16, :] = swept[row + 8 : row + 16, :]
+                pltpu.store(out.at[row : row + 8, :], value, mask=hit)
 
     for e, h, start in STARTS:
         line = e * 8 + h * 4
@@ -465,11 +473,12 @@
                 out[rows, :] = out[rows, :] + fix
 
 
-def last_kernel(incoming, block, out):
-    out[...] = block[...]
+def last_kernel(incoming, merged, out):
+    out[...] = merged[...]
     for f in range(FIELDS):
         for t in range(TILES):
-            out[t, f, 7:8, :] = block[t, f, 7:8, :] + incoming[f, t : t + 1, :]
+            cell = slice(CELLS - 1, CELLS)
+            out[t, f, cell, :] = merged[t, f, cell, :] + incoming[f, t : t + 1, :]
 
 
 def in_vmem():
@@ -494,7 +503,6 @@
     up = [(i, (i + 1) % rows_x) for i in range(rows_x)]
     down = [(j, i) for i, j in up]
     before = lax.ppermute(coarse_state[:, :, CELLS - 8 :], "gx", up)
-    after = lax.ppermute(coarse_state[:, :, :8], "gx", down)
 
     order = jnp.arange(slots, dtype=jnp.int32)
     joined = parent_owner * LANES + parent_site * 2 + fine_half
@@ -515,14 +523,14 @@
     mine = lax.dynamic_index_in_dim(parent_owner.reshape(groups, slots), me, 0, keepdims=False)
     live = lax.dynamic_slice_in_dim(fine_count.reshape(groups), me, 1, 0)
     twin = (mine[:, None] == mine[None, :]) & (order[None, :] < order[:, None])
-    lookups = 2 * mine + jnp.any(twin, axis=1).astype(jnp.int32)
+    lookups = jnp.concatenate([2 * mine + jnp.any(twin, axis=1).astype(jnp.int32), live])
 
     whole = coarse_state.reshape(-1, LANES)
     before = before.reshape(-1, LANES)
     table_shape = shaped(TILES * 16 * GHOST_ROWS, LANES)
     table, kept = pl.pallas_call(
         inner_kernel,
-        out_shape=(table_shape, shaped(2, FIELDS, TILES, LANES)),
+        out_shape=(table_shape, shaped(len(KEPT), FIELDS, TILES, LANES)),
         in_specs=[in_vmem()],
         out_specs=(in_vmem(), in_vmem()),
         cost_estimate=pl.CostEstimate(flops=4_000_000, bytes_accessed=3_000_000, transcendentals=0),
@@ -534,10 +542,11 @@
         out_shape=(table_shape, shaped(groups, 5, 4, LANES)),
         in_specs=[in_smem(), in_vmem(), in_vmem(), in_vmem(), in_vmem()],
         out_specs=(in_vmem(), in_vmem()),
-        input_output_aliases={4: 0},
         compiler_params=params,
         name="edge",
     )(codes, whole, before, kept, table)
+    held, table = lax.optimization_barrier((coarse_state, table))
+    after = lax.ppermute(held[:, :, :8], "gx", down)
     swept, faces, lists = pl.pallas_call(
         coarse_kernel,
         out_shape=(
@@ -565,22 +574,25 @@
     )(codes, whole, before, after.reshape(-1, LANES), table)
     arrived = lax.all_to_all(sending, "gy", split_axis=0, concat_axis=0, tiled=True)
 
-    fine_out, back = pl.pallas_call(
+    final, back = pl.pallas_call(
         fine_kernel,
         out_shape=(
             shaped(slots * FIELDS * FINE, LANES),
             shaped(groups * 2 * BACK_ROWS, LANES),
         ),
-        in_specs=[in_smem(), in_smem(), in_vmem(), in_vmem()],
+        in_specs=[in_smem(), in_vmem(), in_vmem()],
         out_specs=(in_vmem(), in_vmem()),
         scratch_shapes=[
             pltpu.VMEM((GHOST_ROWS * slots, LANES), jnp.float32),
-            pltpu.VMEM((2, FINE + 6, FIELDS, 8, LANES), jnp.float32),
+            pltpu.VMEM((2, FINE + 6, FIELDS, BATCH, LANES), jnp.float32),
             pltpu.VMEM((slots * BACK_ROWS, LANES), jnp.float32),
         ],
         compiler_params=params,
         name="fine",
-    )(lookups, live, arrived, fine_state.reshape(-1, LANES))
+    )(lookups, arrived, fine_state.reshape(-1, LANES))
+    fine_out = jnp.where(
+        (order < live)[:, None, None, None], final.reshape(slots, FIELDS, FINE, LANES), 0.0
+    )
     came = lax.all_to_all(
         back.reshape(groups, 2 * BACK_ROWS, LANES), "gy", split_axis=0, concat_axis=0, tiled=True
     )
@@ -607,21 +619,18 @@
         ],
         out_specs=in_vmem(),
         scratch_shapes=[
-            pltpu.VMEM((TILES * 16 * 8, LANES), jnp.float32),
-            pltpu.VMEM((TILES * 16, LANES), jnp.float32),
+            pltpu.VMEM(((TILES * 16 + 8) * 8, LANES), jnp.float32),
+            pltpu.VMEM((TILES * 16 + 8, LANES), jnp.float32),
         ],
         cost_estimate=pl.CostEstimate(flops=2_000_000, bytes_accessed=8_000_000, transcendentals=0),
         compiler_params=params,
         name="merge",
     )(lists, came, swept, faces, left_fix)
-    spec = pl.BlockSpec((TILES, FIELDS, 8, LANES), lambda i: (0, 0, 3, 0))
     coarse_out = pl.pallas_call(
         last_kernel,
-        grid=(1,),
         out_shape=shaped(TILES, FIELDS, CELLS, LANES),
-        in_specs=[pl.BlockSpec((FIELDS, TILES, LANES), lambda i: (0, 0, 0)), spec],
-        out_specs=spec,
-        input_output_aliases={1: 0},
+        in_specs=[in_vmem(), in_vmem()],
+        out_specs=in_vmem(),
         compiler_params=params,
         name="last",
     )(incoming, merged.reshape(TILES, FIELDS, CELLS, LANES))

time: 93.5 us -> 90.2 us (0.965)
  Pallas kernels: 19.3 us -> 14.9 us
  waiting for transfers between devices: 39.2 us -> 37.4 us
  other arithmetic: 1.85 us -> 3.42 us
    pallas_call x1, Pallas kernels: 3.8 us -> 1.56 us  [body(): pl.pallas_call(merge_kernel, out_shape=shaped(TILES * FIELDS * CELLS, LAN...]
    pallas_call x1, Pallas kernels: 5.83 us -> 4.51 us  [body(): pl.pallas_call(fine_kernel, out_shape=(shaped(slots * FIELDS * FINE, LANE...]
    unnamed x9 -> x15, local copies, waits for them, and re-layouts: 1.18 us -> 2.25 us
    select_n x0 -> x1, other arithmetic: none -> 0.95 us  [body(): jnp.where((order < live)[:, None, None, None], final.reshape(slots, FIELD...]
  transfers between devices with their start and end apart: 5 -> 5, of which waited for: 4 -> 4; matrix products, arithmetic and copies ran while one was open for 4% -> 6% of each run, Pallas kernels for 9% -> 7%
where the time goes in v3:
time: 90.2 us; the launch traced here: 89.8 us
  waiting for transfers between devices  37.4 us (41%)
  starting transfers between devices  29 us (32%)
  Pallas kernels  14.9 us (17%)
  local copies, waits for them, and re-layouts  4.25 us (5%)
  other arithmetic  3.42 us (4%)
    all_to_all x1, waiting for transfers between devices, body(): lax.all_to_all(sending, 'gy', split_axis=0, concat_axis=0, tiled=True)  17.6 us
    all_to_all x1, starting transfers between devices, body(): lax.all_to_all(sending, 'gy', split_axis=0, concat_axis=0, tiled=True)  11.5 us
    ppermute x1, waiting for transfers between devices, body(): before = lax.ppermute(coarse_state[:, :, CELLS - 8:], 'gx', up)  9.88 us
    all_to_all x1, waiting for transfers between devices, body(): lax.all_to_all(back.reshape(groups, 2 * BACK_ROWS, LANES), 'gy', split_ax...  7.58 us
    all_to_all x1, starting transfers between devices, body(): lax.all_to_all(back.reshape(groups, 2 * BACK_ROWS, LANES), 'gy', split_ax...  5.99 us
    ppermute x1, starting transfers between devices, body(): before = lax.ppermute(coarse_state[:, :, CELLS - 8:], 'gx', up)  4.83 us
    pallas_call x1, Pallas kernels, body(): pl.pallas_call(fine_kernel, out_shape=(shaped(slots * FIELDS * FINE, LANE...  4.51 us
    pallas_call x1, Pallas kernels, body(): pl.pallas_call(coarse_kernel, out_shape=(shaped(TILES * FIELDS * CELLS, L...  3.76 us
  transfers between devices with their start and end apart: 5, of which 4 were waited for; matrix products, arithmetic and copies ran while one was open for 6% of the time, Pallas kernels for 7%

profile of v3, /device:TPU:1, one launch (start us, length us, event | category | flops | bytes accessed | tf_op | source)
XLA Modules:
  0.0 89.8 jit_solution(16906273478368186239)
XLA Ops:
  0.7 0.9 %slice.6 = f32[6,5,8,128]{3,2,1,0:T(8,128)S(1)} slice(f32[6,5,32,128]{3,2,1,0:T(8,128)} %param.6), slice={[0:6], [0:5], [24:32], [0:128]} | slice | bytes 245760 | tf_op jit(solution)/shard_map/slice | solution.py:505
  1.6 4.8 %collective-permute-start = (f32[6,5,8,128]{3,2,1,0:T(8,128)S(1)}, f32[6,5,8,128]{3,2,1,0:T(8,128)S(1)}, u32[]{:S(2)}, u32[]{:S(2)}) collective-permute-start(f32[6,5,8,128]{3,2,1,0:T(8,128)S(1)} %slice.6), channel_id=1, source_target_pairs={{0,64},{64,128},{128,192},{192,256},{256,320},{320,384},{384,448},... | collective-permute-start | bytes 368648 | tf_op jit(solution)/shard_map/ppermute | solution.py:505
  6.7 0.7 copy-done.6
  7.8 1.0 %copy-done = f32[6,5,32,128]{3,2,1,0:T(8,128)S(1)} copy-done((f32[6,5,32,128]{3,2,1,0:T(8,128)S(1)}, f32[6,5,32,128]{3,2,1,0:T(8,128)}, u32[]{:S(2)}) %copy-start) | copy-done | bytes 491544
  8.9 1.0 %inner.1 = (f32[960,128]{1,0:T(8,128)S(1)}, f32[5,5,6,128]{3,2,1,0:T(8,128)S(1)}) custom-call(f32[960,128]{1,0:T(8,128)S(1)} %bitcast.19), custom_call_target="tpu_custom_call" | custom-call | flops 4000000 | bytes 3000000 | tf_op jit(solution)/shard_map/inner/pallas_call | solution.py:531
  9.9 9.9 %collective-permute-done = f32[6,5,8,128]{3,2,1,0:T(8,128)S(1)} collective-permute-done((f32[6,5,8,128]{3,2,1,0:T(8,128)S(1)}, f32[6,5,8,128]{3,2,1,0:T(8,128)S(1)}, u32[]{:S(2)}, u32[]{:S(2)}) %collective-permute-start) | collective-permute-done | bytes 122912 | tf_op jit(solution)/shard_map/ppermute | solution.py:505
  19.8 2.2 %edge.1 = (f32[960,128]{1,0:T(8,128)S(1)}, f32[64,5,4,128]{3,2,1,0:T(4,128)}) custom-call(s32[128]{0:T(128)S(1)} %reshape.133.codes, f32[960,128]{1,0:T(8,128)S(1)} %bitcast.20, f32[240,128]{1,0:T(8,128)S(1)} %bitcast.27, f32[5,5,6,128]{3,2,1,0:T(8,128)S(1)} %get-tuple-element.13.kept, f32[960,128]{1,0:T(8,128)S(1)} %get-tuple-element.14.table_in), custom_call_target="tpu_custom_call" | custom-call | tf_op jit(solution)/shard_map/edge/pallas_call | solution.py:540
  22.0 11.5 %all-to-all-start = ((f32[64,5,4,128]{3,2,1,0:T(4,128)}), f32[64,5,4,128]{3,2,1,0:T(4,128)S(1)}, u32[]{:S(2)}, u32[]{:S(2)}) async-start(f32[64,5,4,128]{3,2,1,0:T(4,128)} %get-tuple-element.19), calls=%async_computation | async-start | bytes 1310720 | tf_op jit(solution)/shard_map/all_to_all | solution.py:575
  33.5 0.6 constant_dynamic-slice_fusion
  34.6 0.6 reduce.9
  35.5 0.7 pad_add_fusion.1.lookups
  36.3 17.6 %all-to-all-done.arrived = f32[64,5,4,128]{3,2,1,0:T(4,128)S(1)} async-done(((f32[64,5,4,128]{3,2,1,0:T(4,128)}), f32[64,5,4,128]{3,2,1,0:T(4,128)S(1)}, u32[]{:S(2)}, u32[]{:S(2)}) %all-to-all-start) | async-done | bytes 655392 | tf_op jit(solution)/shard_map/all_to_all | solution.py:575
  53.9 4.5 %fine.1 = (f32[1280,128]{1,0:T(8,128)S(1)}, f32[1024,128]{1,0:T(8,128)}) custom-call(s32[33]{0:T(128)S(1)} %pad_add_fusion.1.lookups, f32[64,5,4,128]{3,2,1,0:T(4,128)S(1)} %all-to-all-done.arrived, f32[1280,128]{1,0:T(8,128)S(1)} %bitcast.25), custom_call_target="tpu_custom_call" | custom-call | tf_op jit(solution)/shard_map/fine/pallas_call | solution.py:577
  58.4 6.0 %all-to-all-start.1 = ((f32[64,16,128]{2,1,0:T(8,128)}), f32[64,16,128]{2,1,0:T(8,128)S(1)}, u32[]{:S(2)}, u32[]{:S(2)}) async-start(f32[64,16,128]{2,1,0:T(8,128)} %bitcast.9), calls=%async_computation.1 | async-start | bytes 1048576 | tf_op jit(solution)/shard_map/all_to_all | solution.py:596
  64.4 3.4 %collective-permute-start.1 = (f32[6,5,8,128]{3,2,1,0:T(8,128)S(1)}, f32[6,5,8,128]{3,2,1,0:T(8,128)S(1)}, u32[]{:S(2)}, u32[]{:S(2)}) collective-permute-start(f32[6,5,8,128]{3,2,1,0:T(8,128)S(1)} %slice.7), channel_id=1, source_target_pairs={{64,0},{128,64},{192,128},{256,192},{320,256},{384,320},{448,384},... | collective-permute-start | bytes 368648 | tf_op jit(solution)/shard_map/ppermute | solution.py:549
  67.8 0.7 iota_compare_fusion.2
  68.4 2.3 %collective-permute-done.1 = f32[6,5,8,128]{3,2,1,0:T(8,128)S(1)} collective-permute-done((f32[6,5,8,128]{3,2,1,0:T(8,128)S(1)}, f32[6,5,8,128]{3,2,1,0:T(8,128)S(1)}, u32[]{:S(2)}, u32[]{:S(2)}) %collective-permute-start.1) | collective-permute-done | bytes 122912 | tf_op jit(solution)/shard_map/ppermute | solution.py:549
  70.7 3.8 %coarse.1 = (f32[960,128]{1,0:T(8,128)S(1)}, f32[6,5,6,128]{3,2,1,0:T(8,128)S(1)}, s32[512]{0:T(512)S(1)}) custom-call(s32[128]{0:T(128)S(1)} %reshape.133.codes, f32[960,128]{1,0:T(8,128)S(1)} %bitcast.21, f32[240,128]{1,0:T(8,128)S(1)} %bitcast.28, f32[240,128]{1,0:T(8,128)S(1)} %bitcast.29, f32[960,128]{1,0:T(8,128)S(1)} %get-tuple-element.17.table), custom_call_target="tpu_custom_call" | custom-call | flops 10000000 | bytes 12000000 | tf_op jit(solution)/shard_map/coarse/pallas_call | solution.py:550
  74.5 7.6 %all-to-all-done.1 = f32[64,16,128]{2,1,0:T(8,128)S(1)} async-done(((f32[64,16,128]{2,1,0:T(8,128)}), f32[64,16,128]{2,1,0:T(8,128)S(1)}, u32[]{:S(2)}, u32[]{:S(2)}) %all-to-all-start.1) | async-done | bytes 524320 | tf_op jit(solution)/shard_map/all_to_all | solution.py:596
  82.1 0.9 %left.1.left_in = f32[5,6,128]{2,1,0:T(8,128)S(1)} custom-call(s32[512]{0:T(512)S(1)} %get-tuple-element.18.lists, f32[1024,128]{1,0:T(8,128)S(1)} %bitcast.22, f32[6,5,6,128]{3,2,1,0:T(8,128)S(1)} %get-tuple-element.21.face_in), custom_call_target="tpu_custom_call" | custom-call | tf_op jit(solution)/shard_map/left/pallas_call | solution.py:601
  83.0 3.4 %collective-permute-start.2 = (f32[5,6,128]{2,1,0:T(8,128)S(1)}, f32[5,6,128]{2,1,0:T(8,128)S(1)}, u32[]{:S(2)}, u32[]{:S(2)}) collective-permute-start(f32[5,6,128]{2,1,0:T(8,128)S(1)} %left.1.left_in), channel_id=1, source_target_pairs={{64,0},{128,64},{192,128},{256,192},{320,256},{384,320},{448,384},... | collective-permute-start | bytes 46088 | tf_op jit(solution)/shard_map/ppermute | solution.py:609
  86.4 0.9 %broadcast_select_fusion = f32[1,32,5,8,128]{4,3,2,1,0:T(8,128)} fusion(f32[1,32,5,8,128]{4,3,2,1,0:T(8,128)S(1)} %bitcast.26, pred[32]{0:T(512)(128)(4,1)S(1)} %iota_compare_fusion.2), kind=kLoop, calls=%fused_computation | loop fusion | flops 163840 | bytes 1310752 | tf_op jit(solution)/shard_map/jit(_where)/select_n | solution.py:593
  87.3 1.6 %merge.1 = f32[960,128]{1,0:T(8,128)S(1)} custom-call(s32[512]{0:T(512)S(1)} %get-tuple-element.18.lists, f32[1024,128]{1,0:T(8,128)S(1)} %bitcast.23, f32[960,128]{1,0:T(8,128)S(1)} %get-tuple-element.22.swept, f32[6,5,6,128]{3,2,1,0:T(8,128)S(1)} %get-tuple-element.21.face_in, f32[5,6,128]{2,1,0:T(8,128)S(1)} %left.1.left_in), custom_call_target="tpu_custom_call" | custom-call | flops 2000000 | bytes 8000000 | tf_op jit(solution)/shard_map/merge/pallas_call | solution.py:610
  88.9 0.8 last.1
  (29 shorter events, 1.5 us)
Async XLA Ops:
  0.6 5.8 %copy-start.3 = (s32[1,2048]{1,0:T(1,128)S(1)}, s32[1,2048]{1,0:T(1,128)}, u32[]{:S(2)}) copy-start(s32[1,2048]{1,0:T(1,128)} %param.9) | copy-start | bytes 24580
  0.6 5.8 %copy-start.4 = (s32[1,2048]{1,0:T(1,128)S(1)}, s32[1,2048]{1,0:T(1,128)}, u32[]{:S(2)}) copy-start(s32[1,2048]{1,0:T(1,128)} %param.11) | copy-start | bytes 24580
  0.7 5.8 %copy-start.5 = (s32[1,2048]{1,0:T(1,128)S(1)}, s32[1,2048]{1,0:T(1,128)}, u32[]{:S(2)}) copy-start(s32[1,2048]{1,0:T(1,128)} %param.10) | copy-start | bytes 24580
  1.6 18.2 %collective-permute-start = (f32[6,5,8,128]{3,2,1,0:T(8,128)S(1)}, f32[6,5,8,128]{3,2,1,0:T(8,128)S(1)}, u32[]{:S(2)}, u32[]{:S(2)}) collective-permute-start(f32[6,5,8,128]{3,2,1,0:T(8,128)S(1)} %slice.6), channel_id=1, source_target_pairs={{0,64},{64,128},{128,192},{192,256},{256,320},{320,384},{384,448},... | collective-permute-start | bytes 368648 | tf_op jit(solution)/shard_map/ppermute | solution.py:505
  6.7 0.7 copy-start.6
  7.8 1.0 %copy-start = (f32[6,5,32,128]{3,2,1,0:T(8,128)S(1)}, f32[6,5,32,128]{3,2,1,0:T(8,128)}, u32[]{:S(2)}) copy-start(f32[6,5,32,128]{3,2,1,0:T(8,128)} %param.6) | copy-start | bytes 1474564
  22.0 31.9 %copy-start.2 = (f32[1,32,5,8,128]{4,3,2,1,0:T(8,128)S(1)}, f32[1,32,5,8,128]{4,3,2,1,0:T(8,128)}, u32[]{:S(2)}) copy-start(f32[1,32,5,8,128]{4,3,2,1,0:T(8,128)} %param.7) | copy-start | bytes 1966084
  22.0 31.8 %all-to-all-start = ((f32[64,5,4,128]{3,2,1,0:T(4,128)}), f32[64,5,4,128]{3,2,1,0:T(4,128)S(1)}, u32[]{:S(2)}, u32[]{:S(2)}) async-start(f32[64,5,4,128]{3,2,1,0:T(4,128)} %get-tuple-element.19), calls=%async_computation | async-start | bytes 1310720 | tf_op jit(solution)/shard_map/all_to_all | solution.py:575
  58.4 6.0 %copy-start.1 = (f32[6,5,32,128]{3,2,1,0:T(8,128)S(1)}, f32[6,5,32,128]{3,2,1,0:T(8,128)}, u32[]{:S(2)}) copy-start(f32[6,5,32,128]{3,2,1,0:T(8,128)} %param.6) | copy-start | bytes 1474564
  58.4 23.7 %all-to-all-start.1 = ((f32[64,16,128]{2,1,0:T(8,128)}), f32[64,16,128]{2,1,0:T(8,128)S(1)}, u32[]{:S(2)}, u32[]{:S(2)}) async-start(f32[64,16,128]{2,1,0:T(8,128)} %bitcast.9), calls=%async_computation.1 | async-start | bytes 1048576 | tf_op jit(solution)/shard_map/all_to_all | solution.py:596
  64.4 6.3 %collective-permute-start.1 = (f32[6,5,8,128]{3,2,1,0:T(8,128)S(1)}, f32[6,5,8,128]{3,2,1,0:T(8,128)S(1)}, u32[]{:S(2)}, u32[]{:S(2)}) collective-permute-start(f32[6,5,8,128]{3,2,1,0:T(8,128)S(1)} %slice.7), channel_id=1, source_target_pairs={{64,0},{128,64},{192,128},{256,192},{320,256},{384,320},{448,384},... | collective-permute-start | bytes 368648 | tf_op jit(solution)/shard_map/ppermute | solution.py:549
  83.0 5.9 %collective-permute-start.2 = (f32[5,6,128]{2,1,0:T(8,128)S(1)}, f32[5,6,128]{2,1,0:T(8,128)S(1)}, u32[]{:S(2)}, u32[]{:S(2)}) collective-permute-start(f32[5,6,128]{2,1,0:T(8,128)S(1)} %left.1.left_in), channel_id=1, source_target_pairs={{64,0},{128,64},{192,128},{256,192},{320,256},{384,320},{448,384},... | collective-permute-start | bytes 46088 | tf_op jit(solution)/shard_map/ppermute | solution.py:609

commit v4 on v3

--- a/solution.py
+++ b/solution.py
@@ -113,7 +113,7 @@
     return cell
 
 
-def write_boxes(table, e, h, old, new):
+def write_boxes(table, e, h, cells_of_age):
     lane = lane_index(TILES)
     upper_z = (lane & 8) != 0
     upper_y = (lane & 64) != 0
@@ -124,7 +124,7 @@
             jnp.where(upper, high, pltpu.roll(low, LANES - shift, 1)),
         )
 
-    for age, source in enumerate((old, new)):
+    for age, source in cells_of_age.items():
         for f in range(FIELDS):
             c0, c1, c2, c3 = [source[o][f] for o in range(4)]
             c0, c1 = swap(c0, c1, upper_z, 8)
@@ -136,6 +136,33 @@
                 table[pl.ds(row, TILES, stride=16 * GHOST_ROWS), :] = value
 
 
+def load_kernel(
+    coarse, owner, site, half, count, own, tail, joined, count_out, tables, sems
+):
+    rows = FIELDS * CELLS
+    loads = [
+        pltpu.make_async_copy(ref, tables.at[i], sems.at[TILES + i])
+        for i, ref in enumerate((owner, site, half))
+    ]
+    loads.append(pltpu.make_async_copy(count, count_out, sems.at[TILES + 3]))
+    cells = [
+        pltpu.make_async_copy(
+            coarse.at[t * rows : (t + 1) * rows], own.at[t * rows : (t + 1) * rows], sems.at[t]
+        )
+        for t in range(TILES)
+    ]
+    for copy in cells + loads:
+        copy.start()
+    for t in range(TILES):
+        cells[t].wait()
+        for f in range(FIELDS):
+            i = t * FIELDS + f
+            tail[8 * i : 8 * i + 8, :] = own[(i + 1) * CELLS - 8 : (i + 1) * CELLS, :]
+    for copy in loads:
+        copy.wait()
+    joined[...] = tables[0] * LANES + tables[1] * 2 + tables[2]
+
+
 def inner_kernel(own, table, kept):
     cell = own_cell(own)
     new = {}
@@ -144,12 +171,15 @@
     for i, x in enumerate(KEPT):
         for f in range(FIELDS):
             kept[i, f] = new[x][f]
-    for e, h, start in STARTS[2:]:
+    for e, h, start in STARTS[1:]:
         where = [start + o for o in (-2, -1, 4, 5)]
-        write_boxes(table, e, h, [cell(x) for x in where], [new[x] for x in where])
-
-
-def edge_kernel(codes, own, before, kept, table_in, table, sending):
+        ages = {0: [cell(x) for x in where]}
+        if e:
+            ages[1] = [new[x] for x in where]
+        write_boxes(table, e, h, ages)
+
+
+def edge_kernel(codes, own, before, kept, table_in, table, sending, staged, sems):
     inner = own_cell(own)
 
     def cell(x):
@@ -157,27 +187,36 @@
             return inner(x)
         return [before[pl.ds(f * 8 + 8 + x, TILES, stride=FIELDS * 8), :] for f in range(FIELDS)]
 
-    half = 8 * GHOST_ROWS
-    for t in range(TILES):
-        rows = slice((2 * t + 1) * half, (2 * t + 2) * half)
-        table[rows, :] = table_in[rows, :]
+    table[...] = table_in[...]
     new = swept_cells(cell, -2, -1)
     new.update(swept_cells(cell, 2, 2))
     for i, x in enumerate(KEPT):
         new[x] = [kept[i, f] for f in range(FIELDS)]
     for e, h, start in STARTS[:2]:
         where = [start + o for o in (-2, -1, 4, 5)]
-        write_boxes(table, e, h, [cell(x) for x in where], [new[x] for x in where])
+        ages = {1: [new[x] for x in where]}
+        if h == 0:
+            ages[0] = [cell(x) for x in where]
+        write_boxes(table, e, h, ages)
 
     def send(k, carry):
         for c in range(2):
             base = jnp.maximum(codes[2 * k + c], 0) * GHOST_ROWS
-            sending[k, 3 * c] = table[pl.ds(base, 4), :]
-            sending[k, 3 * c + 1] = table[pl.ds(base + 4, 4), :]
-            sending[k, 2, 2 * c : 2 * c + 2] = table[pl.ds(base + 8, 2), :]
+            staged[k, 3 * c] = table[pl.ds(base, 4), :]
+            staged[k, 3 * c + 1] = table[pl.ds(base + 4, 4), :]
+            staged[k, 2, 2 * c : 2 * c + 2] = table[pl.ds(base + 8, 2), :]
         return carry
 
-    lax.fori_loop(0, sending.shape[0], send, 0, unroll=8)
+    chunks = sems.shape[0]
+    size = staged.shape[0] // chunks
+    copies = []
+    for i in range(chunks):
+        lax.fori_loop(i * size, (i + 1) * size, send, 0, unroll=8)
+        part = slice(i * size, (i + 1) * size)
+        copies.append(pltpu.make_async_copy(staged.at[part], sending.at[part], sems.at[i]))
+        copies[-1].start()
+    for copy in copies:
+        copy.wait()
 
 
 def coarse_kernel(codes, own, before, after, table, swept, face_out, lists, cells, fluxes):
@@ -244,11 +283,12 @@
     total, first = lax.fori_loop(0, codes.shape[0], collect, (0, 0), unroll=4)
     for i in range(MERGE_STEP):
         lists[ALL_ITEMS + total + i] = TILES * 16
+        lists[LEFT_ITEMS + first + i] = TILES * 16
     lists[0] = lax.shift_right_logical(total + (MERGE_STEP - 1), 2)
-    lists[1] = first
-
-
-def fine_kernel(lookups, arrived, fine, final_out, back, ghosts, cells, packed):
+    lists[1] = lax.shift_right_logical(first + (MERGE_STEP - 1), 2)
+
+
+def fine_kernel(lookups, arrived, fine, final_out, back, ghosts, cells, packed, sems):
     slots = fine.shape[0] // (FIELDS * FINE)
     stride = FIELDS * FINE
     live = lookups[slots]
@@ -335,6 +375,13 @@
         bounds.append(before)
         return bounds
 
+    def put(s):
+        source = pl.multiple_of(s * BACK_ROWS, BACK_ROWS)
+        target = pl.multiple_of(lookups[s] * BACK_ROWS, BACK_ROWS)
+        return pltpu.make_async_copy(
+            packed.at[pl.ds(source, BACK_ROWS)], back.at[pl.ds(target, BACK_ROWS)], sems.at[s]
+        )
+
     def group(g, carry):
         base = g * (BATCH * stride)
         rows = [
@@ -369,20 +416,25 @@
             rows.append(fold_four(0.0625, *faces[4 * t : 4 * t + 4]))
         for r, value in enumerate(rows):
             packed[pl.ds(g * (BATCH * BACK_ROWS) + r, BATCH, stride=BACK_ROWS), :] = value
+        for i in range(BATCH):
+            s = g * BATCH + i
+
+            @pl.when(s < live)
+            def _():
+                put(s).start()
+
         return carry
 
     lax.fori_loop(0, slots // BATCH, group, 0)
 
-    def put(s, carry):
+    def finish(s, carry):
         @pl.when(s < live)
         def _():
-            target = pl.multiple_of(lookups[s] * BACK_ROWS, BACK_ROWS)
-            source = pl.multiple_of(s * BACK_ROWS, BACK_ROWS)
-            back[pl.ds(target, BACK_ROWS), :] = packed[pl.ds(source, BACK_ROWS), :]
+            put(s).wait()
 
         return carry
 
-    lax.fori_loop(0, slots, put, 0, unroll=8)
+    lax.fori_loop(0, slots, finish, 0, unroll=8)
 
 
 def quad_offset(code):
@@ -405,17 +457,18 @@
     quads = lane_index(1) & 72
 
     def scatter(n, carry):
-        entry = lists[LEFT_ITEMS + n]
-        code = entry & (LANES - 1)
-        offset = quad_offset(code)
-        tile = pl.ds(lax.shift_right_logical(code, 4), 1)
-        value = came_item(came, entry)
-        moved = [to_quad(value, offset, t) for t in range(4)]
-        inside = quads == offset
-        for f in range(FIELDS):
-            row = FIELDS + f // 4
-            fix = STEP_RATIO * (face_in[0, f, tile] - moved[f % 4][row : row + 1])
-            pltpu.store(left_out.at[f, tile], fix, mask=inside)
+        for i in range(MERGE_STEP):
+            entry = lists[LEFT_ITEMS + n * MERGE_STEP + i]
+            code = entry & (LANES - 1)
+            offset = quad_offset(code)
+            tile = pl.ds(jnp.minimum(lax.shift_right_logical(code, 4), TILES - 1), 1)
+            value = came_item(came, entry)
+            moved = [to_quad(value, offset, t) for t in range(4)]
+            inside = quads == jnp.where(code < TILES * 16, offset, LANES)
+            for f in range(FIELDS):
+                row = FIELDS + f // 4
+                fix = STEP_RATIO * (face_in[0, f, tile] - moved[f % 4][row : row + 1])
+                pltpu.store(left_out.at[f, tile], fix, mask=inside)
         return carry
 
     lax.fori_loop(0, lists[1], scatter, 0)
@@ -489,6 +542,10 @@
     return pl.BlockSpec(memory_space=pltpu.SMEM)
 
 
+def anywhere():
+    return pl.BlockSpec(memory_space=pl.ANY)
+
+
 def shaped(*dims):
     return jax.ShapeDtypeStruct(dims, jnp.float32)
 
@@ -502,12 +559,30 @@
 
     up = [(i, (i + 1) % rows_x) for i in range(rows_x)]
     down = [(j, i) for i, j in up]
-    before = lax.ppermute(coarse_state[:, :, CELLS - 8 :], "gx", up)
+    entries = parent_owner.shape[1]
+    whole, tail, joined, counts = pl.pallas_call(
+        load_kernel,
+        out_shape=(
+            shaped(TILES * FIELDS * CELLS, LANES),
+            shaped(TILES * FIELDS * 8, LANES),
+            jax.ShapeDtypeStruct((1, entries), jnp.int32),
+            jax.ShapeDtypeStruct((1, groups), jnp.int32),
+        ),
+        in_specs=[anywhere()] * 5,
+        out_specs=(in_vmem(), in_vmem(), in_vmem(), in_vmem()),
+        scratch_shapes=[
+            pltpu.VMEM((3, 1, entries), jnp.int32),
+            pltpu.SemaphoreType.DMA((TILES + 4,)),
+        ],
+        compiler_params=params,
+        name="load",
+    )(coarse_state.reshape(-1, LANES), parent_owner, parent_site, fine_half, fine_count)
+    before = lax.ppermute(tail, "gx", up)
 
     order = jnp.arange(slots, dtype=jnp.int32)
-    joined = parent_owner * LANES + parent_site * 2 + fine_half
     joined = joined.reshape(groups, slots)
-    active = order[None, :] < fine_count.reshape(groups, 1)
+    counts = counts.reshape(groups)
+    active = order[None, :] < counts[:, None]
     hit = (lax.shift_right_logical(joined, 7) == me) & active
     key = order[None, :] * LANES + (joined & (LANES - 1))
     big = slots * LANES
@@ -520,13 +595,12 @@
         ],
         axis=1,
     ).reshape(2 * groups)
-    mine = lax.dynamic_index_in_dim(parent_owner.reshape(groups, slots), me, 0, keepdims=False)
-    live = lax.dynamic_slice_in_dim(fine_count.reshape(groups), me, 1, 0)
+    mine = lax.dynamic_index_in_dim(joined, me, 0, keepdims=False)
+    mine = lax.shift_right_logical(mine, 7)
+    live = lax.dynamic_slice_in_dim(counts, me, 1, 0)
     twin = (mine[:, None] == mine[None, :]) & (order[None, :] < order[:, None])
     lookups = jnp.concatenate([2 * mine + jnp.any(twin, axis=1).astype(jnp.int32), live])
 
-    whole = coarse_state.reshape(-1, LANES)
-    before = before.reshape(-1, LANES)
     table_shape = shaped(TILES * 16 * GHOST_ROWS, LANES)
     table, kept = pl.pallas_call(
         inner_kernel,
@@ -541,11 +615,16 @@
         edge_kernel,
         out_shape=(table_shape, shaped(groups, 5, 4, LANES)),
         in_specs=[in_smem(), in_vmem(), in_vmem(), in_vmem(), in_vmem()],
-        out_specs=(in_vmem(), in_vmem()),
+        out_specs=(in_vmem(), anywhere()),
+        scratch_shapes=[
+            pltpu.VMEM((groups, 5, 4, LANES), jnp.float32),
+            pltpu.SemaphoreType.DMA((4,)),
+        ],
         compiler_params=params,
         name="edge",
     )(codes, whole, before, kept, table)
-    held, table = lax.optimization_barrier((coarse_state, table))
+    held, table = lax.optimization_barrier((whole, table))
+    held = held.reshape(TILES, FIELDS, CELLS, LANES)
     after = lax.ppermute(held[:, :, :8], "gx", down)
     swept, faces, lists = pl.pallas_call(
         coarse_kernel,
@@ -559,7 +638,7 @@
             in_vmem(),
             in_vmem(),
             in_vmem(),
-            pl.BlockSpec(memory_space=pl.ANY),
+            anywhere(),
         ],
         out_specs=(in_vmem(), in_vmem(), in_smem()),
         scratch_shapes=[
@@ -581,11 +660,12 @@
             shaped(groups * 2 * BACK_ROWS, LANES),
         ),
         in_specs=[in_smem(), in_vmem(), in_vmem()],
-        out_specs=(in_vmem(), in_vmem()),
+        out_specs=(in_vmem(), anywhere()),
         scratch_shapes=[
             pltpu.VMEM((GHOST_ROWS * slots, LANES), jnp.float32),
             pltpu.VMEM((2, FINE + 6, FIELDS, BATCH, LANES), jnp.float32),
             pltpu.VMEM((slots * BACK_ROWS, LANES), jnp.float32),
+            pltpu.SemaphoreType.DMA((slots,)),
         ],
         compiler_params=params,
         name="fine",
@@ -615,7 +695,7 @@
             in_vmem(),
             in_vmem(),
             in_vmem(),
-            pl.BlockSpec(memory_space=pl.ANY),
+            anywhere(),
         ],
         out_specs=in_vmem(),
         scratch_shapes=[

time: 90.2 us -> 93.3 us (1.034)
  waiting for transfers between devices: 37.4 us -> 39 us
  local copies, waits for them, and re-layouts: 4.25 us -> 5.2 us
    unnamed x15 -> x12, local copies, waits for them, and re-layouts: 2.25 us -> 3.77 us
    all_to_all x1, waiting for transfers between devices: 17.6 us -> 18.8 us  [body(): lax.all_to_all(sending, 'gy', split_axis=0, concat_axis=0, tiled=True)]
  transfers between devices with their start and end apart: 5 -> 5, of which waited for: 4 -> 4; matrix products, arithmetic and copies ran while one was open for 6% -> 5% of each run, Pallas kernels for 7% -> 7%
where the time goes in v4:
time: 93.3 us; the launch traced here: 92.7 us
  waiting for transfers between devices  39 us (42%)
  starting transfers between devices  28.9 us (31%)
  Pallas kernels  15.4 us (17%)
  local copies, waits for them, and re-layouts  5.2 us (6%)
  other arithmetic  3.4 us (4%)
    all_to_all x1, waiting for transfers between devices, body(): lax.all_to_all(sending, 'gy', split_axis=0, concat_axis=0, tiled=True)  18.8 us
    all_to_all x1, starting transfers between devices, body(): lax.all_to_all(sending, 'gy', split_axis=0, concat_axis=0, tiled=True)  11.5 us
    ppermute x1, waiting for transfers between devices, body(): before = lax.ppermute(tail, 'gx', up)  10.3 us
    all_to_all x1, waiting for transfers between devices, body(): lax.all_to_all(back.reshape(groups, 2 * BACK_ROWS, LANES), 'gy', split_ax...  7.57 us
    all_to_all x1, starting transfers between devices, body(): lax.all_to_all(back.reshape(groups, 2 * BACK_ROWS, LANES), 'gy', split_ax...  5.87 us
    ppermute x1, starting transfers between devices, body(): before = lax.ppermute(tail, 'gx', up)  4.83 us
    pallas_call x1, Pallas kernels, body(): pl.pallas_call(fine_kernel, out_shape=(shaped(slots * FIELDS * FINE, LANE...  4.49 us
    pallas_call x1, Pallas kernels, body(): pl.pallas_call(coarse_kernel, out_shape=(shaped(TILES * FIELDS * CELLS, L...  3.78 us
  transfers between devices with their start and end apart: 5, of which 4 were waited for; matrix products, arithmetic and copies ran while one was open for 5% of the time, Pallas kernels for 7%

profile of v4, /device:TPU:1, one launch (start us, length us, event | category | flops | bytes accessed | tf_op | source)
XLA Modules:
  0.0 92.7 jit_solution(4864061236853567047)
XLA Ops:
  1.3 1.0 %copy-done.1 = f32[6,5,32,128]{3,2,1,0:T(8,128)S(1)} copy-done((f32[6,5,32,128]{3,2,1,0:T(8,128)S(1)}, f32[6,5,32,128]{3,2,1,0:T(8,128)}, u32[]{:S(2)}) %copy-start.1) | copy-done | bytes 491544
  2.3 0.7 copy-done.2
  3.0 0.7 copy-done.3
  3.7 0.7 copy-done.4
  4.4 0.8 load.1
  5.2 4.8 %collective-permute-start = (f32[240,128]{1,0:T(8,128)S(1)}, f32[240,128]{1,0:T(8,128)S(1)}, u32[]{:S(2)}, u32[]{:S(2)}) collective-permute-start(f32[240,128]{1,0:T(8,128)S(1)} %get-tuple-element.20), channel_id=1, source_target_pairs={{0,64},{64,128},{128,192},{192,256},{256,320},{320,384},{384,448},... | collective-permute-start | bytes 368648 | tf_op jit(solution)/shard_map/ppermute | solution.py:580
  10.5 0.7 reduce.3
  11.7 1.3 %inner.1 = (f32[960,128]{1,0:T(8,128)S(1)}, f32[5,5,6,128]{3,2,1,0:T(8,128)S(1)}) custom-call(f32[960,128]{1,0:T(8,128)S(1)} %get-tuple-element.24.own), custom_call_target="tpu_custom_call" | custom-call | flops 4000000 | bytes 3000000 | tf_op jit(solution)/shard_map/inner/pallas_call | solution.py:605
  13.0 10.3 %collective-permute-done.before = f32[240,128]{1,0:T(8,128)S(1)} collective-permute-done((f32[240,128]{1,0:T(8,128)S(1)}, f32[240,128]{1,0:T(8,128)S(1)}, u32[]{:S(2)}, u32[]{:S(2)}) %collective-permute-start) | collective-permute-done | bytes 122912 | tf_op jit(solution)/shard_map/ppermute | solution.py:580
  23.4 1.9 %edge.1 = (f32[960,128]{1,0:T(8,128)S(1)}, f32[64,5,4,128]{3,2,1,0:T(4,128)}) custom-call(s32[128]{0:T(128)S(1)} %reshape.132.codes, f32[960,128]{1,0:T(8,128)S(1)} %get-tuple-element.24.own, f32[240,128]{1,0:T(8,128)S(1)} %collective-permute-done.before, f32[5,5,6,128]{3,2,1,0:T(8,128)S(1)} %get-tuple-element.21.kept, f32[960,128]{1,0:T(8,128)S(1)} %get-tuple-element.22.table_in), custom_call_target="tpu_custom_call" | custom-call | tf_op jit(solution)/shard_map/edge/pallas_call | solution.py:614
  25.2 11.5 %all-to-all-start = ((f32[64,5,4,128]{3,2,1,0:T(4,128)}), f32[64,5,4,128]{3,2,1,0:T(4,128)S(1)}, u32[]{:S(2)}, u32[]{:S(2)}) async-start(f32[64,5,4,128]{3,2,1,0:T(4,128)} %get-tuple-element.27), calls=%async_computation | async-start | bytes 1310720 | tf_op jit(solution)/shard_map/all_to_all | solution.py:654
  37.5 0.7 pad_add_fusion.1.lookups
  38.3 18.8 %all-to-all-done.arrived = f32[64,5,4,128]{3,2,1,0:T(4,128)S(1)} async-done(((f32[64,5,4,128]{3,2,1,0:T(4,128)}), f32[64,5,4,128]{3,2,1,0:T(4,128)S(1)}, u32[]{:S(2)}, u32[]{:S(2)}) %all-to-all-start) | async-done | bytes 655392 | tf_op jit(solution)/shard_map/all_to_all | solution.py:654
  57.1 4.5 %fine.1 = (f32[1280,128]{1,0:T(8,128)S(1)}, f32[1024,128]{1,0:T(8,128)}) custom-call(s32[33]{0:T(128)S(1)} %pad_add_fusion.1.lookups, f32[64,5,4,128]{3,2,1,0:T(4,128)S(1)} %all-to-all-done.arrived, f32[1280,128]{1,0:T(8,128)S(1)} %bitcast.23), custom_call_target="tpu_custom_call" | custom-call | tf_op jit(solution)/shard_map/fine/pallas_call | solution.py:656
  61.6 5.9 %all-to-all-start.1 = ((f32[64,16,128]{2,1,0:T(8,128)}), f32[64,16,128]{2,1,0:T(8,128)S(1)}, u32[]{:S(2)}, u32[]{:S(2)}) async-start(f32[64,16,128]{2,1,0:T(8,128)} %bitcast.9), calls=%async_computation.1 | async-start | bytes 1048576 | tf_op jit(solution)/shard_map/all_to_all | solution.py:676
  67.5 3.4 %collective-permute-start.1 = (f32[6,5,8,128]{3,2,1,0:T(8,128)S(1)}, f32[6,5,8,128]{3,2,1,0:T(8,128)S(1)}, u32[]{:S(2)}, u32[]{:S(2)}) collective-permute-start(f32[6,5,8,128]{3,2,1,0:T(8,128)S(1)} %slice.4), channel_id=1, source_target_pairs={{64,0},{128,64},{192,128},{256,192},{320,256},{384,320},{448,384},... | collective-permute-start | bytes 368648 | tf_op jit(solution)/shard_map/ppermute | solution.py:628
  71.5 2.3 %collective-permute-done.1 = f32[6,5,8,128]{3,2,1,0:T(8,128)S(1)} collective-permute-done((f32[6,5,8,128]{3,2,1,0:T(8,128)S(1)}, f32[6,5,8,128]{3,2,1,0:T(8,128)S(1)}, u32[]{:S(2)}, u32[]{:S(2)}) %collective-permute-start.1) | collective-permute-done | bytes 122912 | tf_op jit(solution)/shard_map/ppermute | solution.py:628
  73.8 3.8 %coarse.1 = (f32[960,128]{1,0:T(8,128)S(1)}, f32[6,5,6,128]{3,2,1,0:T(8,128)S(1)}, s32[512]{0:T(512)S(1)}) custom-call(s32[128]{0:T(128)S(1)} %reshape.132.codes, f32[960,128]{1,0:T(8,128)S(1)} %get-tuple-element.24.own, f32[240,128]{1,0:T(8,128)S(1)} %collective-permute-done.before, f32[240,128]{1,0:T(8,128)S(1)} %bitcast.26, ...), custom_call_target="tpu_custom_call" | custom-call | flops 10000000 | bytes 12000000 | tf_op jit(solution)/shard_map/coarse/pallas_call | solution.py:629
  77.6 7.6 %all-to-all-done.1 = f32[64,16,128]{2,1,0:T(8,128)S(1)} async-done(((f32[64,16,128]{2,1,0:T(8,128)}), f32[64,16,128]{2,1,0:T(8,128)S(1)}, u32[]{:S(2)}, u32[]{:S(2)}) %all-to-all-start.1) | async-done | bytes 524320 | tf_op jit(solution)/shard_map/all_to_all | solution.py:676
  85.2 0.8 left.1.left_in
  86.0 3.4 %collective-permute-start.2 = (f32[5,6,128]{2,1,0:T(8,128)S(1)}, f32[5,6,128]{2,1,0:T(8,128)S(1)}, u32[]{:S(2)}, u32[]{:S(2)}) collective-permute-start(f32[5,6,128]{2,1,0:T(8,128)S(1)} %left.1.left_in), channel_id=1, source_target_pairs={{64,0},{128,64},{192,128},{256,192},{320,256},{384,320},{448,384},... | collective-permute-start | bytes 46088 | tf_op jit(solution)/shard_map/ppermute | solution.py:689
  89.3 0.9 %broadcast_select_fusion = f32[1,32,5,8,128]{4,3,2,1,0:T(8,128)} fusion(f32[1,32,5,8,128]{4,3,2,1,0:T(8,128)S(1)} %bitcast.24, pred[32]{0:T(512)(128)(4,1)S(1)} %iota_compare_fusion.2), kind=kLoop, calls=%fused_computation | loop fusion | flops 163840 | bytes 1310752 | tf_op jit(solution)/shard_map/jit(_where)/select_n | solution.py:673
  90.3 1.6 %merge.1 = f32[960,128]{1,0:T(8,128)S(1)} custom-call(s32[512]{0:T(512)S(1)} %get-tuple-element.26.lists, f32[1024,128]{1,0:T(8,128)S(1)} %bitcast.21, f32[960,128]{1,0:T(8,128)S(1)} %get-tuple-element.30.swept, f32[6,5,6,128]{3,2,1,0:T(8,128)S(1)} %get-tuple-element.29.face_in, f32[5,6,128]{2,1,0:T(8,128)S(1)} %left.1.left_in), custom_call_target="tpu_custom_call" | custom-call | flops 2000000 | bytes 8000000 | tf_op jit(solution)/shard_map/merge/pallas_call | solution.py:690
  91.9 0.8 last.1
  (23 shorter events, 3.1 us)
Async XLA Ops:
  0.6 0.7 copy-start.5
  1.3 1.0 %copy-start.1 = (f32[6,5,32,128]{3,2,1,0:T(8,128)S(1)}, f32[6,5,32,128]{3,2,1,0:T(8,128)}, u32[]{:S(2)}) copy-start(f32[6,5,32,128]{3,2,1,0:T(8,128)} %param.6) | copy-start | bytes 1474564
  2.3 0.7 copy-start.2
  3.0 0.7 copy-start.3
  3.7 0.7 copy-start.4
  5.2 18.2 %collective-permute-start = (f32[240,128]{1,0:T(8,128)S(1)}, f32[240,128]{1,0:T(8,128)S(1)}, u32[]{:S(2)}, u32[]{:S(2)}) collective-permute-start(f32[240,128]{1,0:T(8,128)S(1)} %get-tuple-element.20), channel_id=1, source_target_pairs={{0,64},{64,128},{128,192},{192,256},{256,320},{320,384},{384,448},... | collective-permute-start | bytes 368648 | tf_op jit(solution)/shard_map/ppermute | solution.py:580
  25.2 31.9 %copy-start = (f32[1,32,5,8,128]{4,3,2,1,0:T(8,128)S(1)}, f32[1,32,5,8,128]{4,3,2,1,0:T(8,128)}, u32[]{:S(2)}) copy-start(f32[1,32,5,8,128]{4,3,2,1,0:T(8,128)} %param.7) | copy-start | bytes 1966084
  25.2 31.9 %all-to-all-start = ((f32[64,5,4,128]{3,2,1,0:T(4,128)}), f32[64,5,4,128]{3,2,1,0:T(4,128)S(1)}, u32[]{:S(2)}, u32[]{:S(2)}) async-start(f32[64,5,4,128]{3,2,1,0:T(4,128)} %get-tuple-element.27), calls=%async_computation | async-start | bytes 1310720 | tf_op jit(solution)/shard_map/all_to_all | solution.py:654
  61.6 23.6 %all-to-all-start.1 = ((f32[64,16,128]{2,1,0:T(8,128)}), f32[64,16,128]{2,1,0:T(8,128)S(1)}, u32[]{:S(2)}, u32[]{:S(2)}) async-start(f32[64,16,128]{2,1,0:T(8,128)} %bitcast.9), calls=%async_computation.1 | async-start | bytes 1048576 | tf_op jit(solution)/shard_map/all_to_all | solution.py:676
  67.5 6.3 %collective-permute-start.1 = (f32[6,5,8,128]{3,2,1,0:T(8,128)S(1)}, f32[6,5,8,128]{3,2,1,0:T(8,128)S(1)}, u32[]{:S(2)}, u32[]{:S(2)}) collective-permute-start(f32[6,5,8,128]{3,2,1,0:T(8,128)S(1)} %slice.4), channel_id=1, source_target_pairs={{64,0},{128,64},{192,128},{256,192},{320,256},{384,320},{448,384},... | collective-permute-start | bytes 368648 | tf_op jit(solution)/shard_map/ppermute | solution.py:628
  86.0 5.9 %collective-permute-start.2 = (f32[5,6,128]{2,1,0:T(8,128)S(1)}, f32[5,6,128]{2,1,0:T(8,128)S(1)}, u32[]{:S(2)}, u32[]{:S(2)}) collective-permute-start(f32[5,6,128]{2,1,0:T(8,128)S(1)} %left.1.left_in), channel_id=1, source_target_pairs={{64,0},{128,64},{192,128},{256,192},{320,256},{384,320},{448,384},... | collective-permute-start | bytes 46088 | tf_op jit(solution)/shard_map/ppermute | solution.py:689

commit v5 on v4

--- a/solution.py
+++ b/solution.py
@@ -136,33 +136,6 @@
                 table[pl.ds(row, TILES, stride=16 * GHOST_ROWS), :] = value
 
 
-def load_kernel(
-    coarse, owner, site, half, count, own, tail, joined, count_out, tables, sems
-):
-    rows = FIELDS * CELLS
-    loads = [
-        pltpu.make_async_copy(ref, tables.at[i], sems.at[TILES + i])
-        for i, ref in enumerate((owner, site, half))
-    ]
-    loads.append(pltpu.make_async_copy(count, count_out, sems.at[TILES + 3]))
-    cells = [
-        pltpu.make_async_copy(
-            coarse.at[t * rows : (t + 1) * rows], own.at[t * rows : (t + 1) * rows], sems.at[t]
-        )
-        for t in range(TILES)
-    ]
-    for copy in cells + loads:
-        copy.start()
-    for t in range(TILES):
-        cells[t].wait()
-        for f in range(FIELDS):
-            i = t * FIELDS + f
-            tail[8 * i : 8 * i + 8, :] = own[(i + 1) * CELLS - 8 : (i + 1) * CELLS, :]
-    for copy in loads:
-        copy.wait()
-    joined[...] = tables[0] * LANES + tables[1] * 2 + tables[2]
-
-
 def inner_kernel(own, table, kept):
     cell = own_cell(own)
     new = {}
@@ -201,7 +174,7 @@
 
     def send(k, carry):
         for c in range(2):
-            base = jnp.maximum(codes[2 * k + c], 0) * GHOST_ROWS
+            base = (codes[2 * k + c] & (LANES - 1)) * GHOST_ROWS
             staged[k, 3 * c] = table[pl.ds(base, 4), :]
             staged[k, 3 * c + 1] = table[pl.ds(base + 4, 4), :]
             staged[k, 2, 2 * c : 2 * c + 2] = table[pl.ds(base + 8, 2), :]
@@ -219,7 +192,18 @@
         copy.wait()
 
 
-def coarse_kernel(codes, own, before, after, table, swept, face_out, lists, cells, fluxes):
+def coarse_kernel(
+    codes, counts, live, own, before, after, final, fine_out, swept, face_out, lists, cells, fluxes
+):
+    size = FIELDS * FINE
+    bound = live[0]
+
+    def keep_live(s, carry):
+        rows = pl.ds(pl.multiple_of(s * size, size), size)
+        fine_out[rows, :] = jnp.where(s < bound, final[rows, :], 0.0)
+        return carry
+
+    lax.fori_loop(0, fine_out.shape[0] // size, keep_live, 0, unroll=2)
     stride = FIELDS * CELLS
     for f in range(FIELDS):
         for j in range(3):
@@ -272,11 +256,11 @@
 
     def collect(i, carry):
         total, first = carry
-        code = codes[i]
+        code = codes[i] & (LANES - 1)
         entry = i * LANES + code
         lists[ALL_ITEMS + total] = entry
         lists[LEFT_ITEMS + first] = entry
-        valid = code >= 0
+        valid = lax.shift_right_logical(codes[i], 7) < counts[lax.shift_right_logical(i, 1)]
         leftmost = valid & ((code & 9) == 0)
         return (total + valid.astype(jnp.int32), first + leftmost.astype(jnp.int32))
 
@@ -288,7 +272,7 @@
     lists[1] = lax.shift_right_logical(first + (MERGE_STEP - 1), 2)
 
 
-def fine_kernel(lookups, arrived, fine, final_out, back, ghosts, cells, packed, sems):
+def fine_kernel(lookups, arrived, fine, after, final_out, back, ghosts, cells, packed, sems):
     slots = fine.shape[0] // (FIELDS * FINE)
     stride = FIELDS * FINE
     live = lookups[slots]
@@ -559,42 +543,20 @@
 
     up = [(i, (i + 1) % rows_x) for i in range(rows_x)]
     down = [(j, i) for i, j in up]
-    entries = parent_owner.shape[1]
-    whole, tail, joined, counts = pl.pallas_call(
-        load_kernel,
-        out_shape=(
-            shaped(TILES * FIELDS * CELLS, LANES),
-            shaped(TILES * FIELDS * 8, LANES),
-            jax.ShapeDtypeStruct((1, entries), jnp.int32),
-            jax.ShapeDtypeStruct((1, groups), jnp.int32),
-        ),
-        in_specs=[anywhere()] * 5,
-        out_specs=(in_vmem(), in_vmem(), in_vmem(), in_vmem()),
-        scratch_shapes=[
-            pltpu.VMEM((3, 1, entries), jnp.int32),
-            pltpu.SemaphoreType.DMA((TILES + 4,)),
-        ],
-        compiler_params=params,
-        name="load",
-    )(coarse_state.reshape(-1, LANES), parent_owner, parent_site, fine_half, fine_count)
-    before = lax.ppermute(tail, "gx", up)
+    before = lax.ppermute(coarse_state[:, :, CELLS - 8 :], "gx", up)
+    after = lax.ppermute(coarse_state[:, :, :8], "gx", down)
+    whole, before, after = (v.reshape(-1, LANES) for v in (coarse_state, before, after))
 
     order = jnp.arange(slots, dtype=jnp.int32)
+    joined = parent_owner * LANES + parent_site * 2 + fine_half
     joined = joined.reshape(groups, slots)
-    counts = counts.reshape(groups)
-    active = order[None, :] < counts[:, None]
-    hit = (lax.shift_right_logical(joined, 7) == me) & active
+    hit = lax.shift_right_logical(joined, 7) == me
     key = order[None, :] * LANES + (joined & (LANES - 1))
-    big = slots * LANES
-    low = jnp.min(jnp.where(hit, key, big), axis=1)
-    high = jnp.max(jnp.where(hit, key, -1), axis=1)
-    codes = jnp.stack(
-        [
-            jnp.where(low < big, low & (LANES - 1), -1),
-            jnp.where(high > low, high & (LANES - 1), -1),
-        ],
-        axis=1,
-    ).reshape(2 * groups)
+    key = jnp.where(hit, key, slots * LANES)
+    low = jnp.min(key, axis=1)
+    next_low = jnp.min(jnp.where(key > low[:, None], key, slots * LANES), axis=1)
+    codes = jnp.stack([low, next_low], axis=1).reshape(2 * groups)
+    counts = fine_count.reshape(groups)
     mine = lax.dynamic_index_in_dim(joined, me, 0, keepdims=False)
     mine = lax.shift_right_logical(mine, 7)
     live = lax.dynamic_slice_in_dim(counts, me, 1, 0)
@@ -623,24 +585,35 @@
         compiler_params=params,
         name="edge",
     )(codes, whole, before, kept, table)
-    held, table = lax.optimization_barrier((whole, table))
-    held = held.reshape(TILES, FIELDS, CELLS, LANES)
-    after = lax.ppermute(held[:, :, :8], "gx", down)
-    swept, faces, lists = pl.pallas_call(
+    arrived = lax.all_to_all(sending, "gy", split_axis=0, concat_axis=0, tiled=True)
+
+    final, back = pl.pallas_call(
+        fine_kernel,
+        out_shape=(
+            shaped(slots * FIELDS * FINE, LANES),
+            shaped(groups * 2 * BACK_ROWS, LANES),
+        ),
+        in_specs=[in_smem(), in_vmem(), in_vmem(), in_vmem()],
+        out_specs=(in_vmem(), anywhere()),
+        scratch_shapes=[
+            pltpu.VMEM((GHOST_ROWS * slots, LANES), jnp.float32),
+            pltpu.VMEM((2, FINE + 6, FIELDS, BATCH, LANES), jnp.float32),
+            pltpu.VMEM((slots * BACK_ROWS, LANES), jnp.float32),
+            pltpu.SemaphoreType.DMA((slots,)),
+        ],
+        compiler_params=params,
+        name="fine",
+    )(lookups, arrived, fine_state.reshape(-1, LANES), after)
+    fine_out, swept, faces, lists = pl.pallas_call(
         coarse_kernel,
         out_shape=(
+            shaped(slots * FIELDS * FINE, LANES),
             shaped(TILES * FIELDS * CELLS, LANES),
             shaped(len(FACES), FIELDS, TILES, LANES),
             jax.ShapeDtypeStruct((512,), jnp.int32),
         ),
-        in_specs=[
-            in_smem(),
-            in_vmem(),
-            in_vmem(),
-            in_vmem(),
-            anywhere(),
-        ],
-        out_specs=(in_vmem(), in_vmem(), in_smem()),
+        in_specs=[in_smem(), in_smem(), in_smem()] + [in_vmem()] * 4,
+        out_specs=(in_vmem(), in_vmem(), in_vmem(), in_smem()),
         scratch_shapes=[
             pltpu.VMEM((CELLS + 6, FIELDS, TILES, LANES), jnp.float32),
             pltpu.VMEM((CELLS + 1, FIELDS, TILES, LANES), jnp.float32),
@@ -650,29 +623,7 @@
         ),
         compiler_params=params,
         name="coarse",
-    )(codes, whole, before, after.reshape(-1, LANES), table)
-    arrived = lax.all_to_all(sending, "gy", split_axis=0, concat_axis=0, tiled=True)
-
-    final, back = pl.pallas_call(
-        fine_kernel,
-        out_shape=(
-            shaped(slots * FIELDS * FINE, LANES),
-            shaped(groups * 2 * BACK_ROWS, LANES),
-        ),
-        in_specs=[in_smem(), in_vmem(), in_vmem()],
-        out_specs=(in_vmem(), anywhere()),
-        scratch_shapes=[
-            pltpu.VMEM((GHOST_ROWS * slots, LANES), jnp.float32),
-            pltpu.VMEM((2, FINE + 6, FIELDS, BATCH, LANES), jnp.float32),
-            pltpu.VMEM((slots * BACK_ROWS, LANES), jnp.float32),
-            pltpu.SemaphoreType.DMA((slots,)),
-        ],
-        compiler_params=params,
-        name="fine",
-    )(lookups, arrived, fine_state.reshape(-1, LANES))
-    fine_out = jnp.where(
-        (order < live)[:, None, None, None], final.reshape(slots, FIELDS, FINE, LANES), 0.0
-    )
+    )(codes, counts, live, whole, before, after, final)
     came = lax.all_to_all(
         back.reshape(groups, 2 * BACK_ROWS, LANES), "gy", split_axis=0, concat_axis=0, tiled=True
     )

time: 93.3 us -> 89.5 us (0.959)
  local copies, waits for them, and re-layouts: 5.2 us -> 2.57 us
  other arithmetic: 3.4 us -> 1.99 us
  Pallas kernels: 15.4 us -> 16.5 us
    all_to_all x1, waiting for transfers between devices: 7.57 us -> 12.7 us  [body(): lax.all_to_all(back.reshape(groups, 2 * BACK_ROWS, LANES), 'gy', split_ax...]
    all_to_all x1, waiting for transfers between devices: 18.8 us -> 14 us  [body(): lax.all_to_all(sending, 'gy', split_axis=0, concat_axis=0, tiled=True)]
    unnamed x12 -> x8, local copies, waits for them, and re-layouts: 3.77 us -> 0.65 us
    ppermute x2, waiting for transfers between devices: 12.6 us -> 11.4 us  [the longest x1 10.6 us: body(): before = lax.ppermute(coarse_state[:, :, CELLS - 8:], 'gx', up)]
    slice x1, local copies, waits for them, and re-layouts: 0.02 us -> 1.04 us  [body(): after = lax.ppermute(coarse_state[:, :, :8], 'gx', down)]
    select_n x2 -> x0, other arithmetic: 0.96 us -> none  [the longest x1 0.95 us: body(): jnp.where((order < live)[:, None, None, None], final.reshape(slots, FIELD...]
    pallas_call x2 -> x1, Pallas kernels: 4.53 us -> 4.99 us  [body(): pl.pallas_call(coarse_kernel, out_shape=(shaped(slots * FIELDS * FINE, LA...]
  transfers between devices with their start and end apart: 5 -> 5, of which waited for: 4 -> 4; matrix products, arithmetic and copies ran while one was open for 5% -> 3% of each run, Pallas kernels for 7% -> 9%
where the time goes in v5:
time: 89.5 us; the launch traced here: 89 us
  waiting for transfers between devices  38.2 us (43%)
  starting transfers between devices  28.9 us (32%)
  Pallas kernels  16.5 us (18%)
  local copies, waits for them, and re-layouts  2.57 us (3%)
  other arithmetic  1.99 us (2%)
    all_to_all x1, waiting for transfers between devices, body(): lax.all_to_all(sending, 'gy', split_axis=0, concat_axis=0, tiled=True)  14 us
    all_to_all x1, waiting for transfers between devices, body(): lax.all_to_all(back.reshape(groups, 2 * BACK_ROWS, LANES), 'gy', split_ax...  12.7 us
    all_to_all x1, starting transfers between devices, body(): lax.all_to_all(sending, 'gy', split_axis=0, concat_axis=0, tiled=True)  11.5 us
    ppermute x1, waiting for transfers between devices, body(): before = lax.ppermute(coarse_state[:, :, CELLS - 8:], 'gx', up)  10.6 us
    all_to_all x1, starting transfers between devices, body(): lax.all_to_all(back.reshape(groups, 2 * BACK_ROWS, LANES), 'gy', split_ax...  5.85 us
    pallas_call x1, Pallas kernels, body(): pl.pallas_call(coarse_kernel, out_shape=(shaped(slots * FIELDS * FINE, LA...  4.99 us
    ppermute x1, starting transfers between devices, body(): before = lax.ppermute(coarse_state[:, :, CELLS - 8:], 'gx', up)  4.83 us
    pallas_call x1, Pallas kernels, body(): pl.pallas_call(fine_kernel, out_shape=(shaped(slots * FIELDS * FINE, LANE...  4.5 us
  transfers between devices with their start and end apart: 5, of which 4 were waited for; matrix products, arithmetic and copies ran while one was open for 3% of the time, Pallas kernels for 9%

profile of v5, /device:TPU:1, one launch (start us, length us, event | category | flops | bytes accessed | tf_op | source)
XLA Modules:
  0.0 89.0 jit_solution(12781962616555585753)
XLA Ops:
  0.6 1.0 %fusion.4 = (f32[6,5,8,128]{3,2,1,0:T(8,128)S(1)}, f32[6,5,8,128]{3,2,1,0:T(8,128)S(1)}) fusion(f32[6,5,32,128]{3,2,1,0:T(8,128)} %param.6), kind=kLoop, calls=%fused_computation.15 | loop fusion | bytes 491520 | tf_op jit(solution)/shard_map/slice | solution.py:547
  1.7 4.8 %collective-permute-start = (f32[6,5,8,128]{3,2,1,0:T(8,128)S(1)}, f32[6,5,8,128]{3,2,1,0:T(8,128)S(1)}, u32[]{:S(2)}, u32[]{:S(2)}) collective-permute-start(f32[6,5,8,128]{3,2,1,0:T(8,128)S(1)} %get-tuple-element.21), channel_id=1, source_target_pairs={{0,64},{64,128},{128,192},{192,256},{256,320},{320,384},{384,448},... | collective-permute-start | bytes 368648 | tf_op jit(solution)/shard_map/ppermute | solution.py:546
  6.6 0.7 add_reduce_fusion
  7.5 0.2 fusion
  7.8 0.1 reshape.64.codes
  8.0 1.3 %inner.1 = (f32[960,128]{1,0:T(8,128)S(1)}, f32[5,5,6,128]{3,2,1,0:T(8,128)S(1)}) custom-call(f32[960,128]{1,0:T(8,128)S(1)} %bitcast.16), custom_call_target="tpu_custom_call" | custom-call | flops 4000000 | bytes 3000000 | tf_op jit(solution)/shard_map/inner/pallas_call | solution.py:567
  9.3 10.6 %collective-permute-done = f32[6,5,8,128]{3,2,1,0:T(8,128)S(1)} collective-permute-done((f32[6,5,8,128]{3,2,1,0:T(8,128)S(1)}, f32[6,5,8,128]{3,2,1,0:T(8,128)S(1)}, u32[]{:S(2)}, u32[]{:S(2)}) %collective-permute-start) | collective-permute-done | bytes 122912 | tf_op jit(solution)/shard_map/ppermute | solution.py:546
  19.9 2.6 %edge.1 = (f32[960,128]{1,0:T(8,128)}, f32[64,5,4,128]{3,2,1,0:T(4,128)}) custom-call(s32[128]{0:T(128)S(1)} %reshape.64.codes, f32[960,128]{1,0:T(8,128)S(1)} %bitcast.17, f32[240,128]{1,0:T(8,128)S(1)} %bitcast.23, f32[5,5,6,128]{3,2,1,0:T(8,128)S(1)} %get-tuple-element.11.kept, f32[960,128]{1,0:T(8,128)S(1)} %get-tuple-element.12.table_in), custom_call_target="tpu_custom_call" | custom-call | tf_op jit(solution)/shard_map/edge/pallas_call | solution.py:576
  22.5 11.5 %all-to-all-start = ((f32[64,5,4,128]{3,2,1,0:T(4,128)}), f32[64,5,4,128]{3,2,1,0:T(4,128)S(1)}, u32[]{:S(2)}, u32[]{:S(2)}) async-start(f32[64,5,4,128]{3,2,1,0:T(4,128)} %get-tuple-element.13), calls=%async_computation | async-start | bytes 1310720 | tf_op jit(solution)/shard_map/all_to_all | solution.py:588
  34.0 3.4 %collective-permute-start.1 = (f32[6,5,8,128]{3,2,1,0:T(8,128)S(1)}, f32[6,5,8,128]{3,2,1,0:T(8,128)S(1)}, u32[]{:S(2)}, u32[]{:S(2)}) collective-permute-start(f32[6,5,8,128]{3,2,1,0:T(8,128)S(1)} %get-tuple-element.20), channel_id=1, source_target_pairs={{64,0},{128,64},{192,128},{256,192},{320,256},{384,320},{448,384},... | collective-permute-start | bytes 368648 | tf_op jit(solution)/shard_map/ppermute | solution.py:547
  37.4 0.2 fusion.3
  37.6 0.6 copy-done.2
  38.2 0.6 constant_dynamic-slice_fusion
  38.8 0.7 pad_add_fusion.1.lookups
  39.5 0.8 collective-permute-done.1
  40.4 14.0 %all-to-all-done.arrived = f32[64,5,4,128]{3,2,1,0:T(4,128)S(1)} async-done(((f32[64,5,4,128]{3,2,1,0:T(4,128)}), f32[64,5,4,128]{3,2,1,0:T(4,128)S(1)}, u32[]{:S(2)}, u32[]{:S(2)}) %all-to-all-start) | async-done | bytes 655392 | tf_op jit(solution)/shard_map/all_to_all | solution.py:588
  54.4 4.5 %fine.1 = (f32[1280,128]{1,0:T(8,128)S(1)}, f32[1024,128]{1,0:T(8,128)}) custom-call(s32[33]{0:T(128)S(1)} %pad_add_fusion.1.lookups, f32[64,5,4,128]{3,2,1,0:T(4,128)S(1)} %all-to-all-done.arrived, f32[1280,128]{1,0:T(8,128)S(1)} %bitcast.22, f32[240,128]{1,0:T(8,128)S(1)} %bitcast.25), custom_call_target="tpu_custom_call" | custom-call | tf_op jit(solution)/shard_map/fine/pallas_call | solution.py:590
  58.9 5.8 %all-to-all-start.1 = ((f32[64,16,128]{2,1,0:T(8,128)}), f32[64,16,128]{2,1,0:T(8,128)S(1)}, u32[]{:S(2)}, u32[]{:S(2)}) async-start(f32[64,16,128]{2,1,0:T(8,128)} %bitcast.9), calls=%async_computation.1 | async-start | bytes 1048576 | tf_op jit(solution)/shard_map/all_to_all | solution.py:627
  64.7 5.0 %coarse.1 = (f32[1280,128]{1,0:T(8,128)}, f32[960,128]{1,0:T(8,128)S(1)}, f32[6,5,6,128]{3,2,1,0:T(8,128)S(1)}, s32[512]{0:T(512)S(1)}) custom-call(s32[128]{0:T(128)S(1)} %reshape.64.codes, s32[64]{0:T(128)S(1)} %bitcast.27, s32[1]{0:T(128)} %bitcast.3.live, f32[960,128]{1,0:T(8,128)S(1)} %bitcast.18, f32[240,128]{1,0:T(8,128)S(1)} %bitcast.24, ...), custom_call_target="tpu_custom_call" | custom-call | flops 10000000 | bytes 12000000 | tf_op jit(solution)/shard_map/coarse/pallas_call | solution.py:607
  69.7 12.7 %all-to-all-done.1 = f32[64,16,128]{2,1,0:T(8,128)S(1)} async-done(((f32[64,16,128]{2,1,0:T(8,128)}), f32[64,16,128]{2,1,0:T(8,128)S(1)}, u32[]{:S(2)}, u32[]{:S(2)}) %all-to-all-start.1) | async-done | bytes 524320 | tf_op jit(solution)/shard_map/all_to_all | solution.py:627
  82.5 0.8 left.1.left_in
  83.2 3.4 %collective-permute-start.2 = (f32[5,6,128]{2,1,0:T(8,128)S(1)}, f32[5,6,128]{2,1,0:T(8,128)S(1)}, u32[]{:S(2)}, u32[]{:S(2)}) collective-permute-start(f32[5,6,128]{2,1,0:T(8,128)S(1)} %left.1.left_in), channel_id=1, source_target_pairs={{64,0},{128,64},{192,128},{256,192},{320,256},{384,320},{448,384},... | collective-permute-start | bytes 46088 | tf_op jit(solution)/shard_map/ppermute | solution.py:640
  86.6 1.5 %merge.1 = f32[960,128]{1,0:T(8,128)S(1)} custom-call(s32[512]{0:T(512)S(1)} %get-tuple-element.15.lists, f32[1024,128]{1,0:T(8,128)S(1)} %bitcast.20, f32[960,128]{1,0:T(8,128)S(1)} %get-tuple-element.18.swept, f32[6,5,6,128]{3,2,1,0:T(8,128)S(1)} %get-tuple-element.17.face_in, f32[5,6,128]{2,1,0:T(8,128)S(1)} %left.1.left_in), custom_call_target="tpu_custom_call" | custom-call | flops 2000000 | bytes 8000000 | tf_op jit(solution)/shard_map/merge/pallas_call | solution.py:641
  88.1 0.8 last.1
  (15 shorter events, 0.3 us)
Async XLA Ops:
  0.6 7.3 %copy-start = (f32[6,5,32,128]{3,2,1,0:T(8,128)S(1)}, f32[6,5,32,128]{3,2,1,0:T(8,128)}, u32[]{:S(2)}) copy-start(f32[6,5,32,128]{3,2,1,0:T(8,128)} %param.6) | copy-start | bytes 1474564
  1.7 4.9 %copy-start.3 = (s32[1,2048]{1,0:T(1,128)S(1)}, s32[1,2048]{1,0:T(1,128)}, u32[]{:S(2)}) copy-start(s32[1,2048]{1,0:T(1,128)} %param.11) | copy-start | bytes 24580
  1.7 18.2 %collective-permute-start = (f32[6,5,8,128]{3,2,1,0:T(8,128)S(1)}, f32[6,5,8,128]{3,2,1,0:T(8,128)S(1)}, u32[]{:S(2)}, u32[]{:S(2)}) collective-permute-start(f32[6,5,8,128]{3,2,1,0:T(8,128)S(1)} %get-tuple-element.21), channel_id=1, source_target_pairs={{0,64},{64,128},{128,192},{192,256},{256,320},{320,384},{384,448},... | collective-permute-start | bytes 368648 | tf_op jit(solution)/shard_map/ppermute | solution.py:546
  22.5 31.9 %copy-start.1 = (f32[1,32,5,8,128]{4,3,2,1,0:T(8,128)S(1)}, f32[1,32,5,8,128]{4,3,2,1,0:T(8,128)}, u32[]{:S(2)}) copy-start(f32[1,32,5,8,128]{4,3,2,1,0:T(8,128)} %param.7) | copy-start | bytes 1966084
  22.5 31.9 %all-to-all-start = ((f32[64,5,4,128]{3,2,1,0:T(4,128)}), f32[64,5,4,128]{3,2,1,0:T(4,128)S(1)}, u32[]{:S(2)}, u32[]{:S(2)}) async-start(f32[64,5,4,128]{3,2,1,0:T(4,128)} %get-tuple-element.13), calls=%async_computation | async-start | bytes 1310720 | tf_op jit(solution)/shard_map/all_to_all | solution.py:588
  34.0 6.3 %collective-permute-start.1 = (f32[6,5,8,128]{3,2,1,0:T(8,128)S(1)}, f32[6,5,8,128]{3,2,1,0:T(8,128)S(1)}, u32[]{:S(2)}, u32[]{:S(2)}) collective-permute-start(f32[6,5,8,128]{3,2,1,0:T(8,128)S(1)} %get-tuple-element.20), channel_id=1, source_target_pairs={{64,0},{128,64},{192,128},{256,192},{320,256},{384,320},{448,384},... | collective-permute-start | bytes 368648 | tf_op jit(solution)/shard_map/ppermute | solution.py:547
  37.6 0.7 copy-start.2
  58.9 23.6 %all-to-all-start.1 = ((f32[64,16,128]{2,1,0:T(8,128)}), f32[64,16,128]{2,1,0:T(8,128)S(1)}, u32[]{:S(2)}, u32[]{:S(2)}) async-start(f32[64,16,128]{2,1,0:T(8,128)} %bitcast.9), calls=%async_computation.1 | async-start | bytes 1048576 | tf_op jit(solution)/shard_map/all_to_all | solution.py:627
  83.2 4.9 %collective-permute-start.2 = (f32[5,6,128]{2,1,0:T(8,128)S(1)}, f32[5,6,128]{2,1,0:T(8,128)S(1)}, u32[]{:S(2)}, u32[]{:S(2)}) collective-permute-start(f32[5,6,128]{2,1,0:T(8,128)S(1)} %left.1.left_in), channel_id=1, source_target_pairs={{64,0},{128,64},{192,128},{256,192},{320,256},{384,320},{448,384},... | collective-permute-start | bytes 46088 | tf_op jit(solution)/shard_map/ppermute | solution.py:640

commit v6 on v5

--- a/solution.py
+++ b/solution.py
@@ -38,11 +38,11 @@
     up = right_edge - center
     twice_down = down + down
     twice_up = up + up
-    new_down = jnp.maximum(jnp.minimum(down, twice_up), 0.0) + jnp.minimum(
-        jnp.maximum(down, twice_up), 0.0
-    )
-    new_up = jnp.maximum(jnp.minimum(up, twice_down), 0.0) + jnp.minimum(
-        jnp.maximum(up, twice_down), 0.0
+    new_down = jnp.minimum(
+        jnp.maximum(down, jnp.minimum(twice_up, 0.0)), jnp.maximum(twice_up, 0.0)
+    )
+    new_up = jnp.minimum(
+        jnp.maximum(up, jnp.minimum(twice_down, 0.0)), jnp.maximum(twice_down, 0.0)
     )
     return (center - new_down, center + new_up)
 
@@ -51,11 +51,12 @@
     density, mom_x, mom_y, mom_z, energy = state
     inverse = 1.0 / density
     velocity = mom_x * inverse
-    kinetic = 0.5 * (mom_x * mom_x + mom_y * mom_y + mom_z * mom_z) * inverse
+    carried = mom_x * velocity
+    kinetic = 0.5 * (carried + (mom_y * mom_y + mom_z * mom_z) * inverse)
     pressure = (GAMMA - 1.0) * (energy - kinetic)
     fluxes = (
         mom_x,
-        mom_x * velocity + pressure,
+        carried + pressure,
         mom_y * velocity,
         mom_z * velocity,
         (energy + pressure) * velocity,
@@ -143,7 +144,10 @@
         new.update(swept_cells(cell, first, last))
     for i, x in enumerate(KEPT):
         for f in range(FIELDS):
-            kept[i, f] = new[x][f]
+            kept[6 + i, f] = new[x][f]
+    for x in range(6):
+        for f, value in enumerate(cell(x)):
+            kept[x, f] = value
     for e, h, start in STARTS[1:]:
         where = [start + o for o in (-2, -1, 4, 5)]
         ages = {0: [cell(x) for x in where]}
@@ -152,19 +156,17 @@
         write_boxes(table, e, h, ages)
 
 
-def edge_kernel(codes, own, before, kept, table_in, table, sending, staged, sems):
-    inner = own_cell(own)
-
+def edge_kernel(codes, before, kept, table_in, table, sending, staged, sems):
     def cell(x):
         if x >= 0:
-            return inner(x)
+            return [kept[x, f] for f in range(FIELDS)]
         return [before[pl.ds(f * 8 + 8 + x, TILES, stride=FIELDS * 8), :] for f in range(FIELDS)]
 
     table[...] = table_in[...]
     new = swept_cells(cell, -2, -1)
     new.update(swept_cells(cell, 2, 2))
     for i, x in enumerate(KEPT):
-        new[x] = [kept[i, f] for f in range(FIELDS)]
+        new[x] = [kept[6 + i, f] for f in range(FIELDS)]
     for e, h, start in STARTS[:2]:
         where = [start + o for o in (-2, -1, 4, 5)]
         ages = {1: [new[x] for x in where]}
@@ -566,7 +568,7 @@
     table_shape = shaped(TILES * 16 * GHOST_ROWS, LANES)
     table, kept = pl.pallas_call(
         inner_kernel,
-        out_shape=(table_shape, shaped(len(KEPT), FIELDS, TILES, LANES)),
+        out_shape=(table_shape, shaped(6 + len(KEPT), FIELDS, TILES, LANES)),
         in_specs=[in_vmem()],
         out_specs=(in_vmem(), in_vmem()),
         cost_estimate=pl.CostEstimate(flops=4_000_000, bytes_accessed=3_000_000, transcendentals=0),
@@ -576,7 +578,7 @@
     table, sending = pl.pallas_call(
         edge_kernel,
         out_shape=(table_shape, shaped(groups, 5, 4, LANES)),
-        in_specs=[in_smem(), in_vmem(), in_vmem(), in_vmem(), in_vmem()],
+        in_specs=[in_smem(), in_vmem(), in_vmem(), in_vmem()],
         out_specs=(in_vmem(), anywhere()),
         scratch_shapes=[
             pltpu.VMEM((groups, 5, 4, LANES), jnp.float32),
@@ -584,7 +586,7 @@
         ],
         compiler_params=params,
         name="edge",
-    )(codes, whole, before, kept, table)
+    )(codes, before, kept, table)
     arrived = lax.all_to_all(sending, "gy", split_axis=0, concat_axis=0, tiled=True)
 
     final, back = pl.pallas_call(

time: 89.5 us -> 89.6 us (level)
  no operation moved by 1% of the time
where the time goes in v6:
time: 89.6 us; the launch traced here: 89 us
  waiting for transfers between devices  38.2 us (43%)
  starting transfers between devices  29 us (32%)
  Pallas kernels  16.4 us (18%)
  local copies, waits for them, and re-layouts  2.57 us (3%)
  other arithmetic  1.99 us (2%)
    all_to_all x1, waiting for transfers between devices, body(): lax.all_to_all(sending, 'gy', split_axis=0, concat_axis=0, tiled=True)  14 us
    all_to_all x1, waiting for transfers between devices, body(): lax.all_to_all(back.reshape(groups, 2 * BACK_ROWS, LANES), 'gy', split_ax...  12.7 us
    all_to_all x1, starting transfers between devices, body(): lax.all_to_all(sending, 'gy', split_axis=0, concat_axis=0, tiled=True)  11.5 us
    ppermute x1, waiting for transfers between devices, body(): before = lax.ppermute(coarse_state[:, :, CELLS - 8:], 'gx', up)  10.6 us
    all_to_all x1, starting transfers between devices, body(): lax.all_to_all(back.reshape(groups, 2 * BACK_ROWS, LANES), 'gy', split_ax...  5.88 us
    pallas_call x1, Pallas kernels, body(): pl.pallas_call(coarse_kernel, out_shape=(shaped(slots * FIELDS * FINE, LA...  4.99 us
    ppermute x1, starting transfers between devices, body(): before = lax.ppermute(coarse_state[:, :, CELLS - 8:], 'gx', up)  4.83 us
    pallas_call x1, Pallas kernels, body(): pl.pallas_call(fine_kernel, out_shape=(shaped(slots * FIELDS * FINE, LANE...  4.41 us
  transfers between devices with their start and end apart: 5, of which 4 were waited for; matrix products, arithmetic and copies ran while one was open for 3% of the time, Pallas kernels for 9%

profile of v6, /device:TPU:1, one launch (start us, length us, event | category | flops | bytes accessed | tf_op | source)
XLA Modules:
  0.0 89.0 jit_solution(6482585773023792434)
XLA Ops:
  0.6 1.0 %fusion.4 = (f32[6,5,8,128]{3,2,1,0:T(8,128)S(1)}, f32[6,5,8,128]{3,2,1,0:T(8,128)S(1)}) fusion(f32[6,5,32,128]{3,2,1,0:T(8,128)} %param.6), kind=kLoop, calls=%fused_computation.15 | loop fusion | bytes 491520 | tf_op jit(solution)/shard_map/slice | solution.py:549
  1.7 4.8 %collective-permute-start = (f32[6,5,8,128]{3,2,1,0:T(8,128)S(1)}, f32[6,5,8,128]{3,2,1,0:T(8,128)S(1)}, u32[]{:S(2)}, u32[]{:S(2)}) collective-permute-start(f32[6,5,8,128]{3,2,1,0:T(8,128)S(1)} %get-tuple-element.21), channel_id=1, source_target_pairs={{0,64},{64,128},{128,192},{192,256},{256,320},{320,384},{384,448},... | collective-permute-start | bytes 368648 | tf_op jit(solution)/shard_map/ppermute | solution.py:548
  6.6 0.7 add_reduce_fusion
  7.5 0.2 fusion
  7.8 0.1 reshape.64.codes
  8.0 1.3 %inner.1 = (f32[960,128]{1,0:T(8,128)S(1)}, f32[11,5,6,128]{3,2,1,0:T(8,128)S(1)}) custom-call(f32[960,128]{1,0:T(8,128)S(1)} %bitcast.18), custom_call_target="tpu_custom_call" | custom-call | flops 4000000 | bytes 3000000 | tf_op jit(solution)/shard_map/inner/pallas_call | solution.py:569
  9.2 10.6 %collective-permute-done = f32[6,5,8,128]{3,2,1,0:T(8,128)S(1)} collective-permute-done((f32[6,5,8,128]{3,2,1,0:T(8,128)S(1)}, f32[6,5,8,128]{3,2,1,0:T(8,128)S(1)}, u32[]{:S(2)}, u32[]{:S(2)}) %collective-permute-start) | collective-permute-done | bytes 122912 | tf_op jit(solution)/shard_map/ppermute | solution.py:548
  19.9 2.6 %edge.1 = (f32[960,128]{1,0:T(8,128)}, f32[64,5,4,128]{3,2,1,0:T(4,128)}) custom-call(s32[128]{0:T(128)S(1)} %reshape.64.codes, f32[240,128]{1,0:T(8,128)S(1)} %bitcast.22, f32[11,5,6,128]{3,2,1,0:T(8,128)S(1)} %get-tuple-element.11.kept, f32[960,128]{1,0:T(8,128)S(1)} %get-tuple-element.12.table_in), custom_call_target="tpu_custom_call" | custom-call | tf_op jit(solution)/shard_map/edge/pallas_call | solution.py:578
  22.5 11.5 %all-to-all-start = ((f32[64,5,4,128]{3,2,1,0:T(4,128)}), f32[64,5,4,128]{3,2,1,0:T(4,128)S(1)}, u32[]{:S(2)}, u32[]{:S(2)}) async-start(f32[64,5,4,128]{3,2,1,0:T(4,128)} %get-tuple-element.13), calls=%async_computation | async-start | bytes 1310720 | tf_op jit(solution)/shard_map/all_to_all | solution.py:590
  34.0 3.4 %collective-permute-start.1 = (f32[6,5,8,128]{3,2,1,0:T(8,128)S(1)}, f32[6,5,8,128]{3,2,1,0:T(8,128)S(1)}, u32[]{:S(2)}, u32[]{:S(2)}) collective-permute-start(f32[6,5,8,128]{3,2,1,0:T(8,128)S(1)} %get-tuple-element.20), channel_id=1, source_target_pairs={{64,0},{128,64},{192,128},{256,192},{320,256},{384,320},{448,384},... | collective-permute-start | bytes 368648 | tf_op jit(solution)/shard_map/ppermute | solution.py:549
  37.4 0.2 fusion.3
  37.6 0.6 copy-done.2
  38.2 0.6 constant_dynamic-slice_fusion
  38.8 0.7 pad_add_fusion.1.lookups
  39.5 0.8 collective-permute-done.1
  40.3 14.0 %all-to-all-done.arrived = f32[64,5,4,128]{3,2,1,0:T(4,128)S(1)} async-done(((f32[64,5,4,128]{3,2,1,0:T(4,128)}), f32[64,5,4,128]{3,2,1,0:T(4,128)S(1)}, u32[]{:S(2)}, u32[]{:S(2)}) %all-to-all-start) | async-done | bytes 655392 | tf_op jit(solution)/shard_map/all_to_all | solution.py:590
  54.4 4.4 %fine.1 = (f32[1280,128]{1,0:T(8,128)S(1)}, f32[1024,128]{1,0:T(8,128)}) custom-call(s32[33]{0:T(128)S(1)} %pad_add_fusion.1.lookups, f32[64,5,4,128]{3,2,1,0:T(4,128)S(1)} %all-to-all-done.arrived, f32[1280,128]{1,0:T(8,128)S(1)} %bitcast.21, f32[240,128]{1,0:T(8,128)S(1)} %bitcast.24), custom_call_target="tpu_custom_call" | custom-call | tf_op jit(solution)/shard_map/fine/pallas_call | solution.py:592
  58.8 5.9 %all-to-all-start.1 = ((f32[64,16,128]{2,1,0:T(8,128)}), f32[64,16,128]{2,1,0:T(8,128)S(1)}, u32[]{:S(2)}, u32[]{:S(2)}) async-start(f32[64,16,128]{2,1,0:T(8,128)} %bitcast.9), calls=%async_computation.1 | async-start | bytes 1048576 | tf_op jit(solution)/shard_map/all_to_all | solution.py:629
  64.7 5.0 %coarse.1 = (f32[1280,128]{1,0:T(8,128)}, f32[960,128]{1,0:T(8,128)S(1)}, f32[6,5,6,128]{3,2,1,0:T(8,128)S(1)}, s32[512]{0:T(512)S(1)}) custom-call(s32[128]{0:T(128)S(1)} %reshape.64.codes, s32[64]{0:T(128)S(1)} %bitcast.26, s32[1]{0:T(128)} %bitcast.3.live, f32[960,128]{1,0:T(8,128)S(1)} %bitcast.19, f32[240,128]{1,0:T(8,128)S(1)} %bitcast.23, ...), custom_call_target="tpu_custom_call" | custom-call | flops 10000000 | bytes 12000000 | tf_op jit(solution)/shard_map/coarse/pallas_call | solution.py:609
  69.7 12.7 %all-to-all-done.1 = f32[64,16,128]{2,1,0:T(8,128)S(1)} async-done(((f32[64,16,128]{2,1,0:T(8,128)}), f32[64,16,128]{2,1,0:T(8,128)S(1)}, u32[]{:S(2)}, u32[]{:S(2)}) %all-to-all-start.1) | async-done | bytes 524320 | tf_op jit(solution)/shard_map/all_to_all | solution.py:629
  82.4 0.8 left.1.left_in
  83.2 3.5 %collective-permute-start.2 = (f32[5,6,128]{2,1,0:T(8,128)S(1)}, f32[5,6,128]{2,1,0:T(8,128)S(1)}, u32[]{:S(2)}, u32[]{:S(2)}) collective-permute-start(f32[5,6,128]{2,1,0:T(8,128)S(1)} %left.1.left_in), channel_id=1, source_target_pairs={{64,0},{128,64},{192,128},{256,192},{320,256},{384,320},{448,384},... | collective-permute-start | bytes 46088 | tf_op jit(solution)/shard_map/ppermute | solution.py:642
  86.6 1.6 %merge.1 = f32[960,128]{1,0:T(8,128)S(1)} custom-call(s32[512]{0:T(512)S(1)} %get-tuple-element.15.lists, f32[1024,128]{1,0:T(8,128)S(1)} %bitcast.17, f32[960,128]{1,0:T(8,128)S(1)} %get-tuple-element.18.swept, f32[6,5,6,128]{3,2,1,0:T(8,128)S(1)} %get-tuple-element.17.face_in, f32[5,6,128]{2,1,0:T(8,128)S(1)} %left.1.left_in), custom_call_target="tpu_custom_call" | custom-call | flops 2000000 | bytes 8000000 | tf_op jit(solution)/shard_map/merge/pallas_call | solution.py:643
  88.2 0.8 last.1
  (15 shorter events, 0.3 us)
Async XLA Ops:
  0.6 7.3 %copy-start = (f32[6,5,32,128]{3,2,1,0:T(8,128)S(1)}, f32[6,5,32,128]{3,2,1,0:T(8,128)}, u32[]{:S(2)}) copy-start(f32[6,5,32,128]{3,2,1,0:T(8,128)} %param.6) | copy-start | bytes 1474564
  1.7 4.9 %copy-start.3 = (s32[1,2048]{1,0:T(1,128)S(1)}, s32[1,2048]{1,0:T(1,128)}, u32[]{:S(2)}) copy-start(s32[1,2048]{1,0:T(1,128)} %param.11) | copy-start | bytes 24580
  1.7 18.2 %collective-permute-start = (f32[6,5,8,128]{3,2,1,0:T(8,128)S(1)}, f32[6,5,8,128]{3,2,1,0:T(8,128)S(1)}, u32[]{:S(2)}, u32[]{:S(2)}) collective-permute-start(f32[6,5,8,128]{3,2,1,0:T(8,128)S(1)} %get-tuple-element.21), channel_id=1, source_target_pairs={{0,64},{64,128},{128,192},{192,256},{256,320},{320,384},{384,448},... | collective-permute-start | bytes 368648 | tf_op jit(solution)/shard_map/ppermute | solution.py:548
  22.5 31.9 %copy-start.1 = (f32[1,32,5,8,128]{4,3,2,1,0:T(8,128)S(1)}, f32[1,32,5,8,128]{4,3,2,1,0:T(8,128)}, u32[]{:S(2)}) copy-start(f32[1,32,5,8,128]{4,3,2,1,0:T(8,128)} %param.7) | copy-start | bytes 1966084
  22.5 31.9 %all-to-all-start = ((f32[64,5,4,128]{3,2,1,0:T(4,128)}), f32[64,5,4,128]{3,2,1,0:T(4,128)S(1)}, u32[]{:S(2)}, u32[]{:S(2)}) async-start(f32[64,5,4,128]{3,2,1,0:T(4,128)} %get-tuple-element.13), calls=%async_computation | async-start | bytes 1310720 | tf_op jit(solution)/shard_map/all_to_all | solution.py:590
  34.0 6.3 %collective-permute-start.1 = (f32[6,5,8,128]{3,2,1,0:T(8,128)S(1)}, f32[6,5,8,128]{3,2,1,0:T(8,128)S(1)}, u32[]{:S(2)}, u32[]{:S(2)}) collective-permute-start(f32[6,5,8,128]{3,2,1,0:T(8,128)S(1)} %get-tuple-element.20), channel_id=1, source_target_pairs={{64,0},{128,64},{192,128},{256,192},{320,256},{384,320},{448,384},... | collective-permute-start | bytes 368648 | tf_op jit(solution)/shard_map/ppermute | solution.py:549
  37.6 0.7 copy-start.2
  58.8 23.6 %all-to-all-start.1 = ((f32[64,16,128]{2,1,0:T(8,128)}), f32[64,16,128]{2,1,0:T(8,128)S(1)}, u32[]{:S(2)}, u32[]{:S(2)}) async-start(f32[64,16,128]{2,1,0:T(8,128)} %bitcast.9), calls=%async_computation.1 | async-start | bytes 1048576 | tf_op jit(solution)/shard_map/all_to_all | solution.py:629
  83.2 5.0 %collective-permute-start.2 = (f32[5,6,128]{2,1,0:T(8,128)S(1)}, f32[5,6,128]{2,1,0:T(8,128)S(1)}, u32[]{:S(2)}, u32[]{:S(2)}) collective-permute-start(f32[5,6,128]{2,1,0:T(8,128)S(1)} %left.1.left_in), channel_id=1, source_target_pairs={{64,0},{128,64},{192,128},{256,192},{320,256},{384,320},{448,384},... | collective-permute-start | bytes 46088 | tf_op jit(solution)/shard_map/ppermute | solution.py:642

commit v7 on v6

--- a/solution.py
+++ b/solution.py
@@ -156,7 +156,7 @@
         write_boxes(table, e, h, ages)
 
 
-def edge_kernel(codes, before, kept, table_in, table, sending, staged, sems):
+def edge_kernel(codes, before, kept, table_in, sending, table, staged, sems):
     def cell(x):
         if x >= 0:
             return [kept[x, f] for f in range(FIELDS)]
@@ -575,12 +575,13 @@
         compiler_params=params,
         name="inner",
     )(whole)
-    table, sending = pl.pallas_call(
+    sending = pl.pallas_call(
         edge_kernel,
-        out_shape=(table_shape, shaped(groups, 5, 4, LANES)),
+        out_shape=shaped(groups, 5, 4, LANES),
         in_specs=[in_smem(), in_vmem(), in_vmem(), in_vmem()],
-        out_specs=(in_vmem(), anywhere()),
+        out_specs=anywhere(),
         scratch_shapes=[
+            pltpu.VMEM(table_shape.shape, jnp.float32),
             pltpu.VMEM((groups, 5, 4, LANES), jnp.float32),
             pltpu.SemaphoreType.DMA((4,)),
         ],

time: 89.6 us -> 88.6 us (0.989)
  no operation moved by 1% of the time
where the time goes in v7:
time: 88.6 us; the launch traced here: 88.1 us
  waiting for transfers between devices  38.2 us (43%)
  starting transfers between devices  28.8 us (33%)
  Pallas kernels  15.7 us (18%)
  local copies, waits for them, and re-layouts  2.57 us (3%)
  other arithmetic  1.99 us (2%)
    all_to_all x1, waiting for transfers between devices, body(): lax.all_to_all(sending, 'gy', split_axis=0, concat_axis=0, tiled=True)  14 us
    all_to_all x1, waiting for transfers between devices, body(): lax.all_to_all(back.reshape(groups, 2 * BACK_ROWS, LANES), 'gy', split_ax...  12.7 us
    all_to_all x1, starting transfers between devices, body(): lax.all_to_all(sending, 'gy', split_axis=0, concat_axis=0, tiled=True)  11.5 us
    ppermute x1, waiting for transfers between devices, body(): before = lax.ppermute(coarse_state[:, :, CELLS - 8:], 'gx', up)  10.6 us
    all_to_all x1, starting transfers between devices, body(): lax.all_to_all(back.reshape(groups, 2 * BACK_ROWS, LANES), 'gy', split_ax...  5.84 us
    pallas_call x1, Pallas kernels, body(): pl.pallas_call(coarse_kernel, out_shape=(shaped(slots * FIELDS * FINE, LA...  4.99 us
    ppermute x1, starting transfers between devices, body(): before = lax.ppermute(coarse_state[:, :, CELLS - 8:], 'gx', up)  4.83 us
    pallas_call x1, Pallas kernels, body(): pl.pallas_call(fine_kernel, out_shape=(shaped(slots * FIELDS * FINE, LANE...  4.43 us
  transfers between devices with their start and end apart: 5, of which 4 were waited for; matrix products, arithmetic and copies ran while one was open for 3% of the time, Pallas kernels for 9%

profile of v7, /device:TPU:1, one launch (start us, length us, event | category | flops | bytes accessed | tf_op | source)
XLA Modules:
  0.0 88.1 jit_solution(469949918021234107)
XLA Ops:
  0.6 1.0 %fusion.4 = (f32[6,5,8,128]{3,2,1,0:T(8,128)S(1)}, f32[6,5,8,128]{3,2,1,0:T(8,128)S(1)}) fusion(f32[6,5,32,128]{3,2,1,0:T(8,128)} %param.6), kind=kLoop, calls=%fused_computation.15 | loop fusion | bytes 491520 | tf_op jit(solution)/shard_map/slice | solution.py:549
  1.7 4.8 %collective-permute-start = (f32[6,5,8,128]{3,2,1,0:T(8,128)S(1)}, f32[6,5,8,128]{3,2,1,0:T(8,128)S(1)}, u32[]{:S(2)}, u32[]{:S(2)}) collective-permute-start(f32[6,5,8,128]{3,2,1,0:T(8,128)S(1)} %get-tuple-element.19), channel_id=1, source_target_pairs={{0,64},{64,128},{128,192},{192,256},{256,320},{320,384},{384,448},... | collective-permute-start | bytes 368648 | tf_op jit(solution)/shard_map/ppermute | solution.py:548
  6.6 0.7 add_reduce_fusion
  7.5 0.2 fusion
  7.8 0.1 reshape.64.codes
  8.0 1.3 %inner.1 = (f32[960,128]{1,0:T(8,128)S(1)}, f32[11,5,6,128]{3,2,1,0:T(8,128)S(1)}) custom-call(f32[960,128]{1,0:T(8,128)S(1)} %bitcast.18), custom_call_target="tpu_custom_call" | custom-call | flops 4000000 | bytes 3000000 | tf_op jit(solution)/shard_map/inner/pallas_call | solution.py:569
  9.2 10.6 %collective-permute-done = f32[6,5,8,128]{3,2,1,0:T(8,128)S(1)} collective-permute-done((f32[6,5,8,128]{3,2,1,0:T(8,128)S(1)}, f32[6,5,8,128]{3,2,1,0:T(8,128)S(1)}, u32[]{:S(2)}, u32[]{:S(2)}) %collective-permute-start) | collective-permute-done | bytes 122912 | tf_op jit(solution)/shard_map/ppermute | solution.py:548
  19.9 1.8 %edge.1 = f32[64,5,4,128]{3,2,1,0:T(4,128)} custom-call(s32[128]{0:T(128)S(1)} %reshape.64.codes, f32[240,128]{1,0:T(8,128)S(1)} %bitcast.22, f32[11,5,6,128]{3,2,1,0:T(8,128)S(1)} %get-tuple-element.10.kept, f32[960,128]{1,0:T(8,128)S(1)} %get-tuple-element.11.table_in), custom_call_target="tpu_custom_call" | custom-call | tf_op jit(solution)/shard_map/edge/pallas_call | solution.py:578
  21.7 11.5 %all-to-all-start = ((f32[64,5,4,128]{3,2,1,0:T(4,128)}), f32[64,5,4,128]{3,2,1,0:T(4,128)S(1)}, u32[]{:S(2)}, u32[]{:S(2)}) async-start(f32[64,5,4,128]{3,2,1,0:T(4,128)} %edge.1), calls=%async_computation | async-start | bytes 1310720 | tf_op jit(solution)/shard_map/all_to_all | solution.py:591
  33.2 3.4 %collective-permute-start.1 = (f32[6,5,8,128]{3,2,1,0:T(8,128)S(1)}, f32[6,5,8,128]{3,2,1,0:T(8,128)S(1)}, u32[]{:S(2)}, u32[]{:S(2)}) collective-permute-start(f32[6,5,8,128]{3,2,1,0:T(8,128)S(1)} %get-tuple-element.18), channel_id=1, source_target_pairs={{64,0},{128,64},{192,128},{256,192},{320,256},{384,320},{448,384},... | collective-permute-start | bytes 368648 | tf_op jit(solution)/shard_map/ppermute | solution.py:549
  36.6 0.2 fusion.3
  36.8 0.6 copy-done.2
  37.5 0.6 constant_dynamic-slice_fusion
  38.0 0.7 pad_add_fusion.1.lookups
  38.8 0.8 collective-permute-done.1
  39.6 14.0 %all-to-all-done.arrived = f32[64,5,4,128]{3,2,1,0:T(4,128)S(1)} async-done(((f32[64,5,4,128]{3,2,1,0:T(4,128)}), f32[64,5,4,128]{3,2,1,0:T(4,128)S(1)}, u32[]{:S(2)}, u32[]{:S(2)}) %all-to-all-start) | async-done | bytes 655392 | tf_op jit(solution)/shard_map/all_to_all | solution.py:591
  53.6 4.4 %fine.1 = (f32[1280,128]{1,0:T(8,128)S(1)}, f32[1024,128]{1,0:T(8,128)}) custom-call(s32[33]{0:T(128)S(1)} %pad_add_fusion.1.lookups, f32[64,5,4,128]{3,2,1,0:T(4,128)S(1)} %all-to-all-done.arrived, f32[1280,128]{1,0:T(8,128)S(1)} %bitcast.21, f32[240,128]{1,0:T(8,128)S(1)} %bitcast.24), custom_call_target="tpu_custom_call" | custom-call | tf_op jit(solution)/shard_map/fine/pallas_call | solution.py:593
  58.0 5.8 %all-to-all-start.1 = ((f32[64,16,128]{2,1,0:T(8,128)}), f32[64,16,128]{2,1,0:T(8,128)S(1)}, u32[]{:S(2)}, u32[]{:S(2)}) async-start(f32[64,16,128]{2,1,0:T(8,128)} %bitcast.9), calls=%async_computation.1 | async-start | bytes 1048576 | tf_op jit(solution)/shard_map/all_to_all | solution.py:630
  63.9 5.0 %coarse.1 = (f32[1280,128]{1,0:T(8,128)}, f32[960,128]{1,0:T(8,128)S(1)}, f32[6,5,6,128]{3,2,1,0:T(8,128)S(1)}, s32[512]{0:T(512)S(1)}) custom-call(s32[128]{0:T(128)S(1)} %reshape.64.codes, s32[64]{0:T(128)S(1)} %bitcast.26, s32[1]{0:T(128)} %bitcast.3.live, f32[960,128]{1,0:T(8,128)S(1)} %bitcast.19, f32[240,128]{1,0:T(8,128)S(1)} %bitcast.23, ...), custom_call_target="tpu_custom_call" | custom-call | flops 10000000 | bytes 12000000 | tf_op jit(solution)/shard_map/coarse/pallas_call | solution.py:610
  68.9 12.7 %all-to-all-done.1 = f32[64,16,128]{2,1,0:T(8,128)S(1)} async-done(((f32[64,16,128]{2,1,0:T(8,128)}), f32[64,16,128]{2,1,0:T(8,128)S(1)}, u32[]{:S(2)}, u32[]{:S(2)}) %all-to-all-start.1) | async-done | bytes 524320 | tf_op jit(solution)/shard_map/all_to_all | solution.py:630
  81.6 0.8 left.1.left_in
  82.4 3.3 %collective-permute-start.2 = (f32[5,6,128]{2,1,0:T(8,128)S(1)}, f32[5,6,128]{2,1,0:T(8,128)S(1)}, u32[]{:S(2)}, u32[]{:S(2)}) collective-permute-start(f32[5,6,128]{2,1,0:T(8,128)S(1)} %left.1.left_in), channel_id=1, source_target_pairs={{64,0},{128,64},{192,128},{256,192},{320,256},{384,320},{448,384},... | collective-permute-start | bytes 46088 | tf_op jit(solution)/shard_map/ppermute | solution.py:643
  85.7 1.6 %merge.1 = f32[960,128]{1,0:T(8,128)S(1)} custom-call(s32[512]{0:T(512)S(1)} %get-tuple-element.13.lists, f32[1024,128]{1,0:T(8,128)S(1)} %bitcast.17, f32[960,128]{1,0:T(8,128)S(1)} %get-tuple-element.16.swept, f32[6,5,6,128]{3,2,1,0:T(8,128)S(1)} %get-tuple-element.15.face_in, f32[5,6,128]{2,1,0:T(8,128)S(1)} %left.1.left_in), custom_call_target="tpu_custom_call" | custom-call | flops 2000000 | bytes 8000000 | tf_op jit(solution)/shard_map/merge/pallas_call | solution.py:644
  87.2 0.8 last.1
  (15 shorter events, 0.3 us)
Async XLA Ops:
  0.6 7.3 %copy-start = (f32[6,5,32,128]{3,2,1,0:T(8,128)S(1)}, f32[6,5,32,128]{3,2,1,0:T(8,128)}, u32[]{:S(2)}) copy-start(f32[6,5,32,128]{3,2,1,0:T(8,128)} %param.6) | copy-start | bytes 1474564
  1.7 4.9 %copy-start.3 = (s32[1,2048]{1,0:T(1,128)S(1)}, s32[1,2048]{1,0:T(1,128)}, u32[]{:S(2)}) copy-start(s32[1,2048]{1,0:T(1,128)} %param.11) | copy-start | bytes 24580
  1.7 18.2 %collective-permute-start = (f32[6,5,8,128]{3,2,1,0:T(8,128)S(1)}, f32[6,5,8,128]{3,2,1,0:T(8,128)S(1)}, u32[]{:S(2)}, u32[]{:S(2)}) collective-permute-start(f32[6,5,8,128]{3,2,1,0:T(8,128)S(1)} %get-tuple-element.19), channel_id=1, source_target_pairs={{0,64},{64,128},{128,192},{192,256},{256,320},{320,384},{384,448},... | collective-permute-start | bytes 368648 | tf_op jit(solution)/shard_map/ppermute | solution.py:548
  21.7 31.9 %copy-start.1 = (f32[1,32,5,8,128]{4,3,2,1,0:T(8,128)S(1)}, f32[1,32,5,8,128]{4,3,2,1,0:T(8,128)}, u32[]{:S(2)}) copy-start(f32[1,32,5,8,128]{4,3,2,1,0:T(8,128)} %param.7) | copy-start | bytes 1966084
  21.7 31.9 %all-to-all-start = ((f32[64,5,4,128]{3,2,1,0:T(4,128)}), f32[64,5,4,128]{3,2,1,0:T(4,128)S(1)}, u32[]{:S(2)}, u32[]{:S(2)}) async-start(f32[64,5,4,128]{3,2,1,0:T(4,128)} %edge.1), calls=%async_computation | async-start | bytes 1310720 | tf_op jit(solution)/shard_map/all_to_all | solution.py:591
  33.2 6.3 %collective-permute-start.1 = (f32[6,5,8,128]{3,2,1,0:T(8,128)S(1)}, f32[6,5,8,128]{3,2,1,0:T(8,128)S(1)}, u32[]{:S(2)}, u32[]{:S(2)}) collective-permute-start(f32[6,5,8,128]{3,2,1,0:T(8,128)S(1)} %get-tuple-element.18), channel_id=1, source_target_pairs={{64,0},{128,64},{192,128},{256,192},{320,256},{384,320},{448,384},... | collective-permute-start | bytes 368648 | tf_op jit(solution)/shard_map/ppermute | solution.py:549
  36.8 0.7 copy-start.2
  58.0 23.6 %all-to-all-start.1 = ((f32[64,16,128]{2,1,0:T(8,128)}), f32[64,16,128]{2,1,0:T(8,128)S(1)}, u32[]{:S(2)}, u32[]{:S(2)}) async-start(f32[64,16,128]{2,1,0:T(8,128)} %bitcast.9), calls=%async_computation.1 | async-start | bytes 1048576 | tf_op jit(solution)/shard_map/all_to_all | solution.py:630
  82.4 4.9 %collective-permute-start.2 = (f32[5,6,128]{2,1,0:T(8,128)S(1)}, f32[5,6,128]{2,1,0:T(8,128)S(1)}, u32[]{:S(2)}, u32[]{:S(2)}) collective-permute-start(f32[5,6,128]{2,1,0:T(8,128)S(1)} %left.1.left_in), channel_id=1, source_target_pairs={{64,0},{128,64},{192,128},{256,192},{320,256},{384,320},{448,384},... | collective-permute-start | bytes 46088 | tf_op jit(solution)/shard_map/ppermute | solution.py:643
